TPU v7x, 32 devices: a whole 2x2x4 slice. The times are simulated.
32 devices in a mesh: group: 16 (over z, x, core), head: 2 (over y).
Axes of the slice: x: 2, y: 2, z: 4, core: 2. Of those that a mesh axis runs over, the one named last changes fastest.
Arguments:
- tokens: bfloat16 [1024, 3072], P(('group', 'head')), may hold values from -10 to 10
- attn_gain: float32 [3072], replicated, may hold values from 0.25 to 1.75
- w_query: bfloat16 [3072, 1536], P('group', 'head'), may hold values from -1 to 1
- w_key: bfloat16 [3072, 1536], P('group', 'head'), may hold values from -1 to 1
- w_value: bfloat16 [3072, 1536], P('group', 'head'), may hold values from -0.109375 to 0.109375
- w_out: bfloat16 [1536, 3072], P('head', 'group'), may hold values from -0.15625 to 0.15625
- mlp_gain: float32 [3072], replicated, may hold values from 0.25 to 1.75
- w_gate: bfloat16 [3072, 4096], P('group', 'head'), may hold values from -0.109375 to 0.109375
- w_up: bfloat16 [3072, 4096], P('group', 'head'), may hold values from -0.109375 to 0.109375
- w_down: bfloat16 [4096, 3072], P('head', 'group'), may hold values from -0.09375 to 0.09375
- segment_ids: int32 [16, 64], P('group'), may hold values from 0 to 3, never falling along the last dimension, each value on 1 to 32 neighbouring positions
- cache_slot: int32 [16, 64], P('group'), may hold values from 0 to 63, each once within a row
Outputs:
- layer_out: bfloat16 [1024, 3072], P(('group', 'head'))
- cache_keys: bfloat16 [1024, 1536], P('group', 'head')
- cache_values: bfloat16 [1024, 1536], P('group', 'head')
Inputs may be any that keep to these rules, and one draw needn't show every extreme that they name: `segment_ids`: within each group, segment ids never fall; each of the 4 prompts has 1 to 32 tokens and one has exactly 32. `cache_slot`: each group's row of cache slots holds every slot once.
All inputs are finite; a program needn't handle non-finite values.
Results may differ from a plain program's by a relative error of at most 0.018.
Values may be sent and summed in bfloat16 or wider, within the bound.
No kernel may reach another device: no remote copies, remote signals or barrier semaphores. Data moves between devices by JAX's collectives and lax.ppermute only.
A program may use at most 128 MiB of HBM per device.

v0:
```python
import jax
import jax.numpy as jnp
from jax import lax
from jax.sharding import PartitionSpec as P

HEAD_DIM = 96


def norm_rows(rows, gain):
    values = rows.astype(jnp.float32)
    scale = lax.rsqrt(jnp.mean(values * values, axis=-1, keepdims=True) + 1e-05)
    return (values * scale * gain).astype(jnp.bfloat16)


def positions(segment):
    count = segment.shape[0]
    index = jnp.arange(count, dtype=jnp.int32)
    before = jnp.concatenate([jnp.full((1,), -1, jnp.int32), segment[:-1]])
    starts = jnp.where(segment != before, index, jnp.zeros_like(index))
    return index - lax.cummax(starts, axis=0)


def rotate(heads, place):
    half = heads.shape[-1] // 2
    freq = 10000.0 ** (-2.0 * jnp.arange(half, dtype=jnp.float32) / heads.shape[-1])
    angle = place.astype(jnp.float32)[:, None] * freq[None, :]
    cosine = jnp.cos(angle)[:, None, :]
    sine = jnp.sin(angle)[:, None, :]
    first = heads[..., :half]
    second = heads[..., half:]
    return jnp.concatenate(
        [first * cosine - second * sine, second * cosine + first * sine], axis=-1
    )


def accumulate(source, pieces):
    return tuple((jnp.dot(source, piece, preferred_element_type=jnp.float32) for piece in pieces))


def per_device(
    tokens,
    attn_gain,
    w_query,
    w_key,
    w_value,
    w_out,
    mlp_gain,
    w_gate,
    w_up,
    w_down,
    segment_ids,
    cache_slot,
):
    width = w_query.shape[1]
    heads_here = width // HEAD_DIM
    normed = norm_rows(tokens, attn_gain)
    whole = lax.all_gather(normed, "head", axis=0, tiled=True)
    count = whole.shape[0]
    query, key, value = accumulate(
        whole,
        (
            lax.all_gather(w_query, "group", axis=0, tiled=True),
            lax.all_gather(w_key, "group", axis=0, tiled=True),
            lax.all_gather(w_value, "group", axis=0, tiled=True),
        ),
    )
    segment = segment_ids[0]
    place = positions(segment)
    q_rot = rotate(query.reshape(count, heads_here, HEAD_DIM), place).astype(jnp.bfloat16)
    k_rot = rotate(key.reshape(count, heads_here, HEAD_DIM), place).astype(jnp.bfloat16)
    v_b = value.astype(jnp.bfloat16)
    slots = cache_slot[0]
    k_flat = k_rot.reshape(count, width)
    cache_keys = jnp.zeros_like(k_flat).at[slots].set(k_flat)
    cache_values = jnp.zeros_like(v_b).at[slots].set(v_b)
    index = jnp.arange(count, dtype=jnp.int32)
    allowed = (segment[:, None] == segment[None, :]) & (index[None, :] <= index[:, None])
    scores = jnp.einsum("qhd,khd->hqk", q_rot, k_rot, preferred_element_type=jnp.float32)
    scores = scores * (1.0 / HEAD_DIM**0.5)
    scores = jnp.where(allowed[None, :, :], scores, -1e30)
    top = jnp.max(scores, axis=-1, keepdims=True)
    expo = jnp.exp(scores - top)
    probs = (expo / jnp.sum(expo, axis=-1, keepdims=True)).astype(jnp.bfloat16)
    v_heads = v_b.reshape(count, heads_here, HEAD_DIM)
    attended = jnp.einsum("hqk,khd->qhd", probs, v_heads, preferred_element_type=jnp.float32)
    attended = attended.astype(jnp.bfloat16).reshape(count, width)
    out_terms = jnp.dot(
        attended,
        lax.all_gather(w_out, "group", axis=1, tiled=True),
        preferred_element_type=jnp.float32,
    )
    attn_rows = lax.psum_scatter(
        out_terms.astype(jnp.bfloat16), "head", scatter_dimension=0, tiled=True
    ).astype(jnp.float32)
    middle = (tokens.astype(jnp.float32) + attn_rows).astype(jnp.bfloat16)
    normed2 = norm_rows(middle, mlp_gain)
    mlp_in = lax.all_gather(normed2, "head", axis=0, tiled=True)
    gate, up = accumulate(
        mlp_in,
        (
            lax.all_gather(w_gate, "group", axis=0, tiled=True),
            lax.all_gather(w_up, "group", axis=0, tiled=True),
        ),
    )
    hidden = (jax.nn.silu(gate) * up).astype(jnp.bfloat16)
    down_terms = jnp.dot(
        hidden,
        lax.all_gather(w_down, "group", axis=1, tiled=True),
        preferred_element_type=jnp.float32,
    )
    mlp_rows = lax.psum_scatter(
        down_terms.astype(jnp.bfloat16), "head", scatter_dimension=0, tiled=True
    ).astype(jnp.float32)
    layer_out = (middle.astype(jnp.float32) + mlp_rows).astype(jnp.bfloat16)
    return (layer_out, cache_keys, cache_values)


def solution(mesh):
    in_specs = (
        P(("group", "head"), None),
        P(),
        P("group", "head"),
        P("group", "head"),
        P("group", "head"),
        P("head", "group"),
        P(),
        P("group", "head"),
        P("group", "head"),
        P("head", "group"),
        P("group", None),
        P("group", None),
    )
    out_specs = (P(("group", "head"), None), P("group", "head"), P("group", "head"))
    return jax.shard_map(
        per_device, mesh=mesh, in_specs=in_specs, out_specs=out_specs, check_vma=False
    )
```

profile of v0, /device:TPU:0, one launch (start us, length us, event | category | flops | bytes accessed | tf_op | source)
XLA Modules:
  0.0 585.9 jit_solution(3633983477332343174)
XLA Ops:
  7.2 0.0 all-gather.12.cloned.1.call-start
  7.2 0.7 all-gather.12.cloned.1.call-update
  7.9 0.0 all-gather.10.cloned.1.call-start
  7.9 0.7 all-gather.10.cloned.1.call-update
  8.6 0.0 all-gather.8.cloned.1.call-start
  8.7 0.7 all-gather.8.cloned.1.call-update
  9.4 0.0 all-gather.14.cloned.1.call-start
  9.4 0.5 all-gather.14.cloned.1.call-update
  10.0 0.0 reduce-scatter.3.cloned.1.call-start
  10.0 0.7 slice_bitcast_fusion
  10.7 0.7 compare_select_fusion.1
  11.4 0.1 copy.23
  11.5 0.1 reduce-window.8
  11.6 0.1 reduce
  11.7 1.1 fusion.11
  12.8 1.1 fusion.13
  13.8 8.5 %all_gather.27 = bf16[64,3072]{1,0:T(8,128)(2,1)S(1)} all-gather(bf16[32,3072]{1,0:T(8,128)(2,1)S(1)} %fusion.13), channel_id=1, replica_groups=mesh['group'=16,'head'=2] {'head'}, dimensions={0}, use_global_device_ids=true | all-gather | bytes 589824 | tf_op jit(solution)/shard_map/all_gather | solution.py:57
  22.4 0.8 fusion.29
  23.2 0.2 multiply_cosine_fusion
  23.4 42.8 %all-gather.12.cloned.1.call-done = bf16[3072,768]{1,0:T(8,128)(2,1)} async-done(((bf16[192,768]{1,0:T(8,128)(2,1)}), bf16[3072,768]{1,0:T(8,128)(2,1)}) %all-gather.12.cloned.1.call-update) | async-done | bytes 4718608 | tf_op jit(solution)/shard_map/all_gather | solution.py:63
  66.2 3.2 fusion.46
  69.5 0.1 reshape.232
  69.6 50.7 %all-gather.10.cloned.1.call-done = bf16[3072,768]{1,0:T(8,128)(2,1)} async-done(((bf16[192,768]{1,0:T(8,128)(2,1)}), bf16[3072,768]{1,0:T(8,128)(2,1)}) %all-gather.10.cloned.1.call-update) | async-done | bytes 4718608 | tf_op jit(solution)/shard_map/all_gather | solution.py:62
  120.3 3.2 fusion.45
  123.6 0.1 reshape.230
  123.7 50.7 %all-gather.8.cloned.1.call-done = bf16[3072,768]{1,0:T(8,128)(2,1)} async-done(((bf16[192,768]{1,0:T(8,128)(2,1)}), bf16[3072,768]{1,0:T(8,128)(2,1)}) %all-gather.8.cloned.1.call-update) | async-done | bytes 4718608 | tf_op jit(solution)/shard_map/all_gather | solution.py:64
  174.5 3.2 convolution_convert_fusion.3
  177.7 0.2 reshape.229
  177.9 0.1 fusion.41
  178.0 0.1 multiply_subtract_fusion
  178.1 0.1 maximum_convert_fusion
  178.2 0.1 fusion.40
  178.4 0.1 subtract_convert_fusion
  178.5 0.3 fusion.42
  178.8 0.3 fusion.3
  179.1 0.3 fusion.5
  179.4 0.1 copy.29
  179.5 0.1 reshape.233
  179.6 48.8 %all-gather.14.cloned.1.call-done = bf16[768,3072]{0,1:T(8,128)(2,1)} async-done(((bf16[768,192]{0,1:T(8,128)(2,1)}), bf16[768,3072]{0,1:T(8,128)(2,1)}) %all-gather.14.cloned.1.call-update) | async-done | bytes 4718608 | tf_op jit(solution)/shard_map/all_gather | solution.py:89
  228.4 4.6 convolution_convert_fusion
  233.0 0.0 reduce-scatter.3.cloned.1.call-update
  233.1 0.0 all-gather.16.cloned.1.call-start
  233.1 0.5 all-gather.16.cloned.1.call-update
  233.7 0.0 all-gather.18.cloned.1.call-start
  233.7 0.7 all-gather.18.cloned.1.call-update
  234.4 0.0 all-gather.20.cloned.1.call-start
  234.4 0.7 all-gather.20.cloned.1.call-update
  235.2 0.0 reduce-scatter.5.cloned.1.call-start
  235.2 9.7 %reduce-scatter.3.cloned.1.call-done = bf16[32,3072]{1,0:T(8,128)(2,1)} async-done(((bf16[64,3072]{1,0:T(8,128)(2,1)}), bf16[32,3072]{1,0:T(8,128)(2,1)}) %reduce-scatter.3.cloned.1.call-update) | async-done | bytes 196624 | tf_op jit(solution)/shard_map/reduce_scatter | solution.py:92
  244.9 1.1 fusion.15
  246.0 1.0 fusion.17
  247.1 7.5 %all_gather.32 = bf16[64,3072]{1,0:T(8,128)(2,1)S(1)} all-gather(bf16[32,3072]{1,0:T(8,128)(2,1)S(1)} %fusion.17), channel_id=1, replica_groups=mesh['group'=16,'head'=2] {'head'}, dimensions={0}, use_global_device_ids=true | all-gather | bytes 589824 | tf_op jit(solution)/shard_map/all_gather | solution.py:97
  254.6 93.5 %all-gather.16.cloned.1.call-done = bf16[3072,2048]{1,0:T(8,128)(2,1)} async-done(((bf16[192,2048]{1,0:T(8,128)(2,1)}), bf16[3072,2048]{1,0:T(8,128)(2,1)}) %all-gather.16.cloned.1.call-update) | async-done | bytes 12582928 | tf_op jit(solution)/shard_map/all_gather | solution.py:101
  348.1 6.9 %fusion.47 = f32[64,2048]{1,0:T(8,128)S(1)} fusion(bf16[64,3072]{1,0:T(8,128)(2,1)S(1)} %all_gather.32, bf16[3072,2048]{1,0:T(8,128)(2,1)} %all-gather.16.cloned.1.call-done), kind=kOutput, calls=%fused_computation.72 | convolution fusion | flops 805306368 | bytes 13500416 | tf_op jit(solution)/shard_map/dot_general | solution.py:37
  355.0 94.7 %all-gather.18.cloned.1.call-done = bf16[3072,2048]{1,0:T(8,128)(2,1)} async-done(((bf16[192,2048]{1,0:T(8,128)(2,1)}), bf16[3072,2048]{1,0:T(8,128)(2,1)}) %all-gather.18.cloned.1.call-update) | async-done | bytes 12582928 | tf_op jit(solution)/shard_map/all_gather | solution.py:102
  449.6 101.5 %all-gather.20.cloned.1.call-done = bf16[2048,3072]{0,1:T(8,128)(2,1)} async-done(((bf16[2048,192]{0,1:T(8,128)(2,1)}), bf16[2048,3072]{0,1:T(8,128)(2,1)}) %all-gather.20.cloned.1.call-update) | async-done | bytes 12582928 | tf_op jit(solution)/shard_map/all_gather | solution.py:108
  551.2 15.1 %convolution_convert_fusion.1 = bf16[64,3072]{1,0:T(8,128)(2,1)} fusion(bf16[2048,3072]{0,1:T(8,128)(2,1)} %all-gather.20.cloned.1.call-done, bf16[64,3072]{1,0:T(8,128)(2,1)S(1)} %all_gather.32, bf16[3072,2048]{1,0:T(8,128)(2,1)} %all-gather.18.cloned.1.call-done, f32[64,2048]{1,0:T(8,128)S(1)} %fusion.47), kind=kOutput, calls=%fused_computation.4 | convolution fusion | flops 1611595776 | bytes 26476544 | tf_op jit(solution)/shard_map/dot_general | solution.py:106
  566.2 0.0 reduce-scatter.5.cloned.1.call-update
  566.3 0.1 copy.30
  566.4 0.1 reshape.238
  566.5 1.5 scatter_custom_fusion.1
  568.0 1.5 scatter_custom_fusion
  569.4 8.3 %reduce-scatter.5.cloned.1.call-done = bf16[32,3072]{1,0:T(8,128)(2,1)} async-done(((bf16[64,3072]{1,0:T(8,128)(2,1)}), bf16[32,3072]{1,0:T(8,128)(2,1)}) %reduce-scatter.5.cloned.1.call-update) | async-done | bytes 196624 | tf_op jit(solution)/shard_map/reduce_scatter | solution.py:111
  577.7 1.7 fusion.18
  (13 shorter events, 0.1 us)
Async XLA Ops:
  7.2 59.1 %all-gather.12.cloned.1.call-start = ((), (), s32[]{:S(2)}) async-start(), calls=%async_computation.4 | async-start | bytes 5013504 | tf_op jit(solution)/shard_map/all_gather | solution.py:63
  7.9 112.5 %all-gather.10.cloned.1.call-start = ((), (), s32[]{:S(2)}) async-start(), calls=%async_computation.3 | async-start | bytes 5013504 | tf_op jit(solution)/shard_map/all_gather | solution.py:62
  8.6 165.8 %all-gather.8.cloned.1.call-start = ((), (), s32[]{:S(2)}) async-start(), calls=%async_computation.2 | async-start | bytes 5013504 | tf_op jit(solution)/shard_map/all_gather | solution.py:64
  9.4 219.0 %all-gather.14.cloned.1.call-start = ((), (), s32[]{:S(2)}) async-start(), calls=%async_computation.5 | async-start | bytes 5013504 | tf_op jit(solution)/shard_map/all_gather | solution.py:89
  10.0 234.9 %reduce-scatter.3.cloned.1.call-start = ((), (), s32[]{:S(2)}) async-start(), calls=%async_computation.6 | async-start | bytes 589824 | tf_op jit(solution)/shard_map/reduce_scatter | solution.py:92
  179.1 65.8 %copy-start = (bf16[32,3072]{1,0:T(8,128)(2,1)S(1)}, bf16[32,3072]{1,0:T(8,128)(2,1)}, u32[]{:S(2)}) copy-start(bf16[32,3072]{1,0:T(8,128)(2,1)} %param.12) | copy-start | bytes 589828
  179.4 66.6 %copy-start.2 = (f32[3072]{0:T(1024)S(1)}, f32[3072]{0:T(1024)}, u32[]{:S(2)}) copy-start(f32[3072]{0:T(1024)} %param.18) | copy-start | bytes 36868
  233.1 115.0 %all-gather.16.cloned.1.call-start = ((), (), s32[]{:S(2)}) async-start(), calls=%async_computation.7 | async-start | bytes 13369344 | tf_op jit(solution)/shard_map/all_gather | solution.py:101
  233.7 216.0 %all-gather.18.cloned.1.call-start = ((), (), s32[]{:S(2)}) async-start(), calls=%async_computation.8 | async-start | bytes 13369344 | tf_op jit(solution)/shard_map/all_gather | solution.py:102
  234.4 316.8 %all-gather.20.cloned.1.call-start = ((), (), s32[]{:S(2)}) async-start(), calls=%async_computation.9 | async-start | bytes 13369344 | tf_op jit(solution)/shard_map/all_gather | solution.py:108
  235.2 342.5 %reduce-scatter.5.cloned.1.call-start = ((), (), s32[]{:S(2)}) async-start(), calls=%async_computation.10 | async-start | bytes 589824 | tf_op jit(solution)/shard_map/reduce_scatter | solution.py:111
  354.9 211.3 %copy-start.3 = (s32[1,64]{1,0:T(1,128)S(1)}, s32[1,64]{1,0:T(1,128)}, u32[]{:S(2)}) copy-start(s32[1,64]{1,0:T(1,128)} %param.23) | copy-start | bytes 772
  355.0 222.7 %copy-start.1 = (bf16[32,3072]{1,0:T(8,128)(2,1)S(1)}, bf16[32,3072]{1,0:T(8,128)(2,1)}, u32[]{:S(2)}) copy-start(bf16[32,3072]{1,0:T(8,128)(2,1)} %reduce-scatter.3.cloned.1.call-done) | copy-start | bytes 589828
Sparse Core Ops, SparseCore 0:
  10.3 55.9 all-gather.11
  68.5 51.7 all-gather.9
  122.6 51.7 all-gather.7
  176.6 51.7 all-gather.13
  233.2 11.6 reduce-scatter.2
  247.3 100.7 all-gather.15
  350.6 98.9 all-gather.17
  452.2 98.9 all-gather.19
  566.4 11.2 reduce-scatter.4
where the time goes:
time: 586 us
  waiting for transfers between devices  505 us (86%)
  matrix products  37.2 us (6%)
  blocking collectives  16 us (3%)
  between operations  14 us (2%)
  other arithmetic  8.25 us (1%)
    all_gather x1, waiting for transfers between devices, per_device(): lax.all_gather(w_down, 'group', axis=1, tiled=True)  102 us
    all_gather x1, waiting for transfers between devices, per_device(): lax.all_gather(w_up, 'group', axis=0, tiled=True)  94.7 us
    all_gather x1, waiting for transfers between devices, per_device(): lax.all_gather(w_gate, 'group', axis=0, tiled=True)  93.5 us
    all_gather x1, waiting for transfers between devices, per_device(): lax.all_gather(w_value, 'group', axis=0, tiled=True)  50.7 us
    all_gather x1, waiting for transfers between devices, per_device(): lax.all_gather(w_query, 'group', axis=0, tiled=True)  50.7 us
    all_gather x1, waiting for transfers between devices, per_device(): lax.all_gather(w_out, 'group', axis=1, tiled=True)  48.8 us
    all_gather x1, waiting for transfers between devices, per_device(): lax.all_gather(w_key, 'group', axis=0, tiled=True)  42.8 us
    dot_general x4, matrix products, accumulate(): jnp.dot(source, piece, preferred_element_type=jnp.float32)  16.6 us
  transfers between devices with their start and end apart: 9, of which 9 were waited for; matrix products, arithmetic and copies ran while one was open for 5% of the time, Pallas kernels for 0%

commit v1 on v0

v1 whole, which is shorter than its diff:
```python
import jax
import jax.numpy as jnp
from jax import lax
from jax.sharding import PartitionSpec as P

HEAD_DIM = 96
EPS = 1e-05
OCT = 8
BF = jnp.bfloat16
F32 = jnp.float32


def norm_rows(rows, gain):
    values = rows.astype(F32)
    scale = lax.rsqrt(jnp.mean(values * values, axis=-1, keepdims=True) + EPS)
    return (values * scale * gain).astype(BF)


def positions(segment):
    count = segment.shape[0]
    index = jnp.arange(count, dtype=jnp.int32)
    before = jnp.concatenate([jnp.full((1,), -1, jnp.int32), segment[:-1]])
    starts = jnp.where(segment != before, index, jnp.zeros_like(index))
    return index - lax.cummax(starts, axis=0)


def rotate(heads, place):
    half = heads.shape[-1] // 2
    freq = 10000.0 ** (-2.0 * jnp.arange(half, dtype=F32) / heads.shape[-1])
    angle = place.astype(F32)[:, None] * freq[None, :]
    cosine = jnp.cos(angle)[:, None, :]
    sine = jnp.sin(angle)[:, None, :]
    first = heads[..., :half]
    second = heads[..., half:]
    return jnp.concatenate(
        [first * cosine - second * sine, second * cosine + first * sine], axis=-1
    )


def dot(a, b):
    return jnp.dot(a, b, preferred_element_type=F32)


def attention(query, key, v_b, segment, slots):
    count, width = v_b.shape
    heads_here = width // HEAD_DIM
    index = jnp.arange(count, dtype=jnp.int32)
    place = positions(segment)
    q_rot = rotate(query.reshape(count, heads_here, HEAD_DIM), place).astype(BF)
    k_rot = rotate(key.reshape(count, heads_here, HEAD_DIM), place).astype(BF)
    k_flat = k_rot.reshape(count, width)
    cache_keys = jnp.zeros_like(k_flat).at[slots].set(k_flat)
    cache_values = jnp.zeros_like(v_b).at[slots].set(v_b)
    allowed = (segment[:, None] == segment[None, :]) & (index[None, :] <= index[:, None])
    scores = jnp.einsum("qhd,khd->hqk", q_rot, k_rot, preferred_element_type=F32)
    scores = scores * (1.0 / HEAD_DIM**0.5)
    scores = jnp.where(allowed[None, :, :], scores, -1e30)
    top = jnp.max(scores, axis=-1, keepdims=True)
    expo = jnp.exp(scores - top)
    probs = (expo / jnp.sum(expo, axis=-1, keepdims=True)).astype(BF)
    v_heads = v_b.reshape(count, heads_here, HEAD_DIM)
    attended = jnp.einsum("hqk,khd->qhd", probs, v_heads, preferred_element_type=F32)
    return attended.astype(BF).reshape(count, width), cache_keys, cache_values


def gathered_plan(
    tokens, attn_gain, w_query, w_key, w_value, w_out, mlp_gain, w_gate, w_up, w_down, segment_ids, cache_slot,
):
    whole = lax.all_gather(norm_rows(tokens, attn_gain), "head", axis=0, tiled=True)
    query, key, value = (
        dot(whole, lax.all_gather(w, "group", axis=0, tiled=True)) for w in (w_query, w_key, w_value)
    )
    attended, cache_keys, cache_values = attention(
        query, key, value.astype(BF), segment_ids[0], cache_slot[0]
    )
    out_terms = dot(attended, lax.all_gather(w_out, "group", axis=1, tiled=True))
    attn_rows = lax.psum_scatter(out_terms.astype(BF), "head", scatter_dimension=0, tiled=True)
    middle = (tokens.astype(F32) + attn_rows.astype(F32)).astype(BF)
    mlp_in = lax.all_gather(norm_rows(middle, mlp_gain), "head", axis=0, tiled=True)
    gate, up = (dot(mlp_in, lax.all_gather(w, "group", axis=0, tiled=True)) for w in (w_gate, w_up))
    hidden = (jax.nn.silu(gate) * up).astype(BF)
    down_terms = dot(hidden, lax.all_gather(w_down, "group", axis=1, tiled=True))
    mlp_rows = lax.psum_scatter(down_terms.astype(BF), "head", scatter_dimension=0, tiled=True)
    layer_out = (middle.astype(F32) + mlp_rows.astype(F32)).astype(BF)
    return (layer_out, cache_keys, cache_values)


def octet_plan(n_group):
    octets = [[OCT * i + j for j in range(OCT)] for i in range(n_group // OCT)]
    swap = [(g, g ^ OCT) for g in range(n_group)]

    def across(x):
        return lax.ppermute(x, "group", swap)

    def other_head(x):
        return lax.ppermute(x, "head", [(0, 1), (1, 0)])

    def gather(w, axis):
        return lax.all_gather(w, "group", axis=axis, tiled=True, axis_index_groups=octets)

    def split_sum(x):
        high = x.astype(BF)
        low = (x - high.astype(F32)).astype(BF)
        return jnp.concatenate([high, low, jnp.zeros((x.shape[0], 126), BF)], axis=1)

    def exchange(partial, squares):
        rows = partial.shape[0] // 2
        sent = jnp.concatenate([partial[rows:].astype(BF), split_sum(squares[rows:])], axis=1)
        got = across(sent).astype(F32)
        width = partial.shape[1]
        total = partial[:rows] + got[:, :width]
        return total, squares[:rows] + got[:, width : width + 1] + got[:, width + 1 : width + 2]

    def per_device(
        tokens, attn_gain, w_query, w_key, w_value, w_out, mlp_gain, w_gate, w_up, w_down, segment_ids, cache_slot,
    ):
        side = lax.axis_index("group") // OCT
        row = lax.axis_index("head")
        mine, model = tokens.shape
        half = model // 2
        width = w_query.shape[1]
        units = w_gate.shape[1]

        w_qkv = gather(jnp.concatenate([w_query, w_key, w_value], axis=1), 0)
        w_o = gather(w_out, 1)
        w_gu = gather(jnp.concatenate([w_gate, w_up], axis=1), 0)
        w_d = gather(w_down, 1)

        kept = lax.dynamic_slice(tokens, (0, side * half), (mine, half))
        given = lax.dynamic_slice(tokens, (0, (1 - side) * half), (mine, half))
        both = jnp.stack([kept, across(given)])
        others = other_head(both)
        rows = jnp.stack([jnp.where(row == 0, both, others), jnp.where(row == 0, others, both)], axis=1)
        rows = rows.reshape(4 * mine, half)

        def scaled(x, gain):
            values = x.astype(F32)
            own = lax.dynamic_slice(gain, (side * half,), (half,))
            return (values * own).astype(BF), jnp.sum(values * values, axis=-1, keepdims=True)

        lhs, squares = scaled(rows, attn_gain)
        qkv, squares = exchange(dot(lhs, w_qkv), squares)
        qkv = qkv * lax.rsqrt(squares / model + EPS)
        attended, cache_keys, cache_values = attention(
            qkv[:, :width], qkv[:, width : 2 * width], qkv[:, 2 * width :].astype(BF),
            segment_ids[0], cache_slot[0],
        )
        attended = jnp.concatenate([attended, across(attended)], axis=0)
        terms = dot(attended, w_o).astype(BF)
        middle = (rows.astype(F32) + (terms.astype(F32) + other_head(terms).astype(F32))).astype(BF)
        lhs, squares = scaled(middle, mlp_gain)
        gu, squares = exchange(dot(lhs, w_gu), squares)
        gu = gu * lax.rsqrt(squares / model + EPS)
        hidden = (jax.nn.silu(gu[:, :units]) * gu[:, units:]).astype(BF)
        hidden = jnp.concatenate([hidden, across(hidden)], axis=0)
        terms = dot(hidden, w_d).astype(BF).reshape(2, 2, mine, half)
        given = other_head(lax.dynamic_index_in_dim(terms, 1 - row, 1, keepdims=False))
        mlp = lax.dynamic_index_in_dim(terms, row, 1, keepdims=False).astype(F32) + given.astype(F32)
        kept = lax.dynamic_index_in_dim(middle.reshape(2, 2, mine, half), row, 1, keepdims=False)
        out = (kept.astype(F32) + mlp).astype(BF)
        got = across(out[1])
        layer_out = jnp.where(
            side == 0, jnp.concatenate([out[0], got], axis=1), jnp.concatenate([got, out[0]], axis=1)
        )
        return (layer_out, cache_keys, cache_values)

    return per_device


def solution(mesh):
    n_group = mesh.shape["group"]
    in_specs = (
        P(("group", "head"), None),
        P(),
        P("group", "head"),
        P("group", "head"),
        P("group", "head"),
        P("head", "group"),
        P(),
        P("group", "head"),
        P("group", "head"),
        P("head", "group"),
        P("group", None),
        P("group", None),
    )
    out_specs = (P(("group", "head"), None), P("group", "head"), P("group", "head"))
    body = octet_plan(n_group) if n_group == 2 * OCT else gathered_plan
    return jax.shard_map(body, mesh=mesh, in_specs=in_specs, out_specs=out_specs, check_vma=False)
```

time: 586 us -> 237 us (0.40)
  waiting for transfers between devices: 505 us -> 168 us
  matrix products: 37.2 us -> 19.2 us
  starting transfers between devices: 0.35 us -> 16.7 us
  blocking collectives: 16 us -> 0 us
    all_gather x7 -> x4, waiting for transfers between devices: 483 us -> 100 us  [gather(): lax.all_gather(w, 'group', axis=axis, tiled=True, axis_index_groups=octets)]
    ppermute x0 -> x9, waiting for transfers between devices: none -> 67.6 us  [the longest x6 49.6 us: across(): return lax.ppermute(x, 'group', swap)]
    reduce_scatter x2 -> x0, waiting for transfers between devices: 18 us -> none  [the longest x1 9.7 us: per_device(): lax.psum_scatter(out_terms.astype(jnp.bfloat16), 'head', scatter_dimensio...]
    dot_general x8 -> x6, matrix products: 36.8 us -> 18.9 us  [the longest x4 18.4 us: dot(): return jnp.dot(a, b, preferred_element_type=F32)]
    ppermute x0 -> x9, starting transfers between devices: none -> 16.5 us  [the longest x6 11.7 us: across(): return lax.ppermute(x, 'group', swap)]
    all_gather x2 -> x0, blocking collectives: 16 us -> none  [the longest x1 8.53 us: per_device(): whole = lax.all_gather(normed, 'head', axis=0, tiled=True)]
  transfers between devices with their start and end apart: 9 -> 13, of which waited for: 9 -> 13; matrix products, arithmetic and copies ran while one was open for 5% -> 12% of each run, Pallas kernels for 0% -> 0%
where the time goes in v1:
time: 237 us
  waiting for transfers between devices  168 us (71%)
  matrix products  19.2 us (8%)
  starting transfers between devices  16.7 us (7%)
  between operations  14.3 us (6%)
  local copies, waits for them, and re-layouts  9.88 us (4%)
  other arithmetic  8.21 us (3%)
    all_gather x4, waiting for transfers between devices, gather(): lax.all_gather(w, 'group', axis=axis, tiled=True, axis_index_groups=octets)  100 us
    ppermute x6, waiting for transfers between devices, across(): return lax.ppermute(x, 'group', swap)  49.6 us
    dot_general x4, matrix products, dot(): return jnp.dot(a, b, preferred_element_type=F32)  18.4 us
    ppermute x3, waiting for transfers between devices, other_head(): return lax.ppermute(x, 'head', [(0, 1), (1, 0)])  18 us
    ppermute x6, starting transfers between devices, across(): return lax.ppermute(x, 'group', swap)  11.7 us
    ppermute x3, starting transfers between devices, other_head(): return lax.ppermute(x, 'head', [(0, 1), (1, 0)])  4.78 us
  transfers between devices with their start and end apart: 13, of which 13 were waited for; matrix products, arithmetic and copies ran while one was open for 12% of the time, Pallas kernels for 0%

profile of v1, /device:TPU:0, one launch (start us, length us, event | category | flops | bytes accessed | tf_op | source)
XLA Modules:
  0.0 236.8 jit_solution(16005103751208114983)
XLA Ops:
  7.2 2.2 pad_maximum_fusion.1
  9.5 0.7 all-gather.7.cloned.1.call-update
  10.3 1.3 pad_maximum_fusion
  11.8 4.1 %collective-permute-start = (bf16[32,1536]{1,0:T(8,128)(2,1)S(1)}, bf16[32,1536]{1,0:T(8,128)(2,1)S(1)}, u32[]{:S(2)}, u32[]{:S(2)}) collective-permute-start(bf16[32,1536]{1,0:T(8,128)(2,1)S(1)} %get-tuple-element.22), channel_id=1, source_target_pairs={{0,16},{2,18},{4,20},{6,22},{8,24},{10,26},{12,28},{14,30},{16,0},... | collective-permute-start | bytes 294920 | tf_op jit(solution)/shard_map/ppermute | solution.py:93
  15.9 0.7 fusion.31
  16.9 0.1 reduce.3
  17.1 3.7 %collective-permute-done = bf16[32,1536]{1,0:T(8,128)(2,1)S(1)} collective-permute-done((bf16[32,1536]{1,0:T(8,128)(2,1)S(1)}, bf16[32,1536]{1,0:T(8,128)(2,1)S(1)}, u32[]{:S(2)}, u32[]{:S(2)}) %collective-permute-start) | collective-permute-done | bytes 98336 | tf_op jit(solution)/shard_map/ppermute | solution.py:93
  20.8 1.6 collective-permute-start.1
  22.4 4.5 %collective-permute-done.1 = bf16[2,32,1536]{2,1,0:T(8,128)(2,1)S(1)} collective-permute-done((bf16[2,32,1536]{2,1,0:T(8,128)(2,1)S(1)}, bf16[2,32,1536]{2,1,0:T(8,128)(2,1)S(1)}, u32[]{:S(2)}, u32[]{:S(2)}) %collective-permute-start.1) | collective-permute-done | bytes 196640 | tf_op jit(solution)/shard_map/ppermute | solution.py:96
  27.1 0.2 multiply_reduce_fusion
  27.4 0.1 copy.86
  27.5 0.1 copy.87
  27.7 26.1 %all-gather.5.cloned.1.call-done = bf16[1536,2304]{1,0:T(8,128)(2,1)} async-done(((bf16[192,2304]{1,0:T(8,128)(2,1)}), bf16[1536,2304]{1,0:T(8,128)(2,1)}) %all-gather.5.cloned.1.call-update) | async-done | bytes 7077904 | tf_op jit(solution)/shard_map/all_gather | solution.py:99
  53.8 4.1 %fusion.52 = f32[128,2304]{1,0:T(8,128)S(1)} fusion(bf16[128,1536]{1,0:T(8,128)(2,1)S(1)} %fusion.10, bf16[1536,2304]{1,0:T(8,128)(2,1)} %all-gather.5.cloned.1.call-done), kind=kOutput, calls=%fused_computation.100 | convolution fusion | flops 905969664 | bytes 8650752 | tf_op jit(solution)/shard_map/dot_general | solution.py:41
  58.0 0.1 concatenate.44
  58.1 2.5 %collective-permute-start.2 = (bf16[64,2432]{1,0:T(8,128)(2,1)S(1)}, bf16[64,2432]{1,0:T(8,128)(2,1)S(1)}, u32[]{:S(2)}, u32[]{:S(2)}) collective-permute-start(bf16[64,2432]{1,0:T(8,128)(2,1)S(1)} %concatenate.44), channel_id=1, source_target_pairs={{0,16},{2,18},{4,20},{6,22},{8,24},{10,26},{12,28},{14,30},{16,0},... | collective-permute-start | bytes 933896 | tf_op jit(solution)/shard_map/ppermute | solution.py:93
  60.5 0.2 multiply_cosine_fusion
  60.9 0.4 copy.107
  61.3 14.0 %collective-permute-done.2 = bf16[64,2432]{1,0:T(8,128)(2,1)S(1)} collective-permute-done((bf16[64,2432]{1,0:T(8,128)(2,1)S(1)}, bf16[64,2432]{1,0:T(8,128)(2,1)S(1)}, u32[]{:S(2)}, u32[]{:S(2)}) %collective-permute-start.2) | collective-permute-done | bytes 311328 | tf_op jit(solution)/shard_map/ppermute | solution.py:93
  75.3 0.3 copy.88
  75.7 0.2 fusion.3
  76.0 0.1 copy.108
  76.1 0.1 copy.109
  76.3 0.1 copy.110
  76.4 0.1 copy.111
  76.7 0.1 maximum_convert_fusion.1
  76.8 0.8 subtract_convert_fusion
  77.6 0.3 fusion.49
  78.0 0.3 fusion.4
  78.3 0.3 fusion.6
  78.6 0.1 copy.96
  78.7 0.1 reshape.266
  78.8 0.3 collective-permute-start.3
  79.1 5.2 %all-gather.7.cloned.1.call-done = bf16[768,1536]{0,1:T(8,128)(2,1)} async-done(((bf16[768,192]{0,1:T(8,128)(2,1)}), bf16[768,1536]{0,1:T(8,128)(2,1)}) %all-gather.7.cloned.1.call-update) | async-done | bytes 2359312 | tf_op jit(solution)/shard_map/all_gather | solution.py:99
  84.3 1.7 collective-permute-done.3
  86.0 2.6 %convolution_convert_fusion = bf16[128,1536]{1,0:T(8,128)(2,1)S(1)} fusion(bf16[768,1536]{0,1:T(8,128)(2,1)} %all-gather.7.cloned.1.call-done, bf16[64,768]{1,0:T(8,128)(2,1)S(1)} %collective-permute-done.3, bf16[64,768]{1,0:T(8,128)(2,1)S(1)} %reshape.266), kind=kOutput, calls=%fused_computation.3 | convolution fusion | flops 302579712 | bytes 2949120 | tf_op jit(solution)/shard_map/dot_general | solution.py:41
  88.6 1.5 collective-permute-start.4
  90.2 8.9 %collective-permute-done.4 = bf16[128,1536]{1,0:T(8,128)(2,1)S(1)} collective-permute-done((bf16[128,1536]{1,0:T(8,128)(2,1)S(1)}, bf16[128,1536]{1,0:T(8,128)(2,1)S(1)}, u32[]{:S(2)}, u32[]{:S(2)}) %collective-permute-start.4) | collective-permute-done | bytes 393248 | tf_op jit(solution)/shard_map/ppermute | solution.py:96
  99.1 0.2 fusion.9
  99.4 0.1 copy.100
  99.5 0.3 copy-done.10
  99.9 0.1 copy.99
  100.0 49.7 %all-gather.9.cloned.1.call-done = bf16[1536,4096]{1,0:T(8,128)(2,1)} async-done(((bf16[192,4096]{1,0:T(8,128)(2,1)}), bf16[1536,4096]{1,0:T(8,128)(2,1)}) %all-gather.9.cloned.1.call-update) | async-done | bytes 12582928 | tf_op jit(solution)/shard_map/all_gather | solution.py:99
  149.7 6.4 %fusion.15 = f32[128,4096]{1,0:T(8,128)S(1)} fusion(bf16[1536,4096]{1,0:T(8,128)(2,1)} %all-gather.9.cloned.1.call-done, bf16[128,1536]{1,0:T(8,128)(2,1)S(1)} %get-tuple-element.6, f32[1536]{0:T(1024)S(1)} %dynamic_slice.26), kind=kOutput, calls=%fused_computation.33 | convolution fusion | flops 1611202560 | bytes 15079424 | tf_op jit(solution)/shard_map/dot_general | solution.py:41
  156.1 0.9 concatenate.51
  157.1 2.4 %collective-permute-start.5 = (bf16[64,4224]{1,0:T(8,128)(2,1)}, bf16[64,4224]{1,0:T(8,128)(2,1)}, u32[]{:S(2)}, u32[]{:S(2)}) collective-permute-start(bf16[64,4224]{1,0:T(8,128)(2,1)} %concatenate.51), channel_id=1, source_target_pairs={{0,16},{2,18},{4,20},{6,22},{8,24},{10,26},{12,28},{14,30},{16,0},... | collective-permute-start | bytes 1622024 | tf_op jit(solution)/shard_map/ppermute | solution.py:93
  159.6 0.6 copy.113
  160.2 24.2 %collective-permute-done.5 = bf16[64,4224]{1,0:T(8,128)(2,1)} collective-permute-done((bf16[64,4224]{1,0:T(8,128)(2,1)}, bf16[64,4224]{1,0:T(8,128)(2,1)}, u32[]{:S(2)}, u32[]{:S(2)}) %collective-permute-start.5) | collective-permute-done | bytes 540704 | tf_op jit(solution)/shard_map/ppermute | solution.py:93
  184.4 1.8 copy.101
  186.2 0.1 convert_element_type.161
  186.3 0.3 fusion.1
  186.7 0.3 fusion.7
  186.9 2.4 %collective-permute-start.6 = (bf16[64,2048]{0,1:T(8,128)(2,1)S(1)}, bf16[64,2048]{0,1:T(8,128)(2,1)S(1)}, u32[]{:S(2)}, u32[]{:S(2)}) collective-permute-start(bf16[64,2048]{0,1:T(8,128)(2,1)S(1)} %fusion.7), channel_id=1, source_target_pairs={{0,16},{2,18},{4,20},{6,22},{8,24},{10,26},{12,28},{14,30},{16,0},... | collective-permute-start | bytes 786440 | tf_op jit(solution)/shard_map/ppermute | solution.py:93
  189.4 19.1 %all-gather.11.cloned.1.call-done = bf16[2048,1536]{0,1:T(8,128)(2,1)} async-done(((bf16[2048,192]{0,1:T(8,128)(2,1)}), bf16[2048,1536]{0,1:T(8,128)(2,1)}) %all-gather.11.cloned.1.call-update) | async-done | bytes 6291472 | tf_op jit(solution)/shard_map/all_gather | solution.py:99
  208.5 3.7 %collective-permute-done.6 = bf16[64,2048]{0,1:T(8,128)(2,1)S(1)} collective-permute-done((bf16[64,2048]{0,1:T(8,128)(2,1)S(1)}, bf16[64,2048]{0,1:T(8,128)(2,1)S(1)}, u32[]{:S(2)}, u32[]{:S(2)}) %collective-permute-start.6) | collective-permute-done | bytes 262176 | tf_op jit(solution)/shard_map/ppermute | solution.py:93
  212.2 5.3 %convolution_convert_fusion.1 = bf16[128,1536]{1,0:T(8,128)(2,1)S(1)} fusion(bf16[2048,1536]{0,1:T(8,128)(2,1)} %all-gather.11.cloned.1.call-done, bf16[64,2048]{0,1:T(8,128)(2,1)S(1)} %collective-permute-done.6, bf16[64,2048]{0,1:T(8,128)(2,1)S(1)} %fusion.7), kind=kOutput, calls=%fused_computation.4 | convolution fusion | flops 806551552 | bytes 7208960 | tf_op jit(solution)/shard_map/dot_general | solution.py:41
  217.6 1.6 collective-permute-start.7
  219.2 4.7 %collective-permute-done.7 = bf16[2,32,1536]{2,1,0:T(8,128)(2,1)S(1)} collective-permute-done((bf16[2,32,1536]{2,1,0:T(8,128)(2,1)S(1)}, bf16[2,32,1536]{2,1,0:T(8,128)(2,1)S(1)}, u32[]{:S(2)}, u32[]{:S(2)}) %collective-permute-start.7) | collective-permute-done | bytes 196640 | tf_op jit(solution)/shard_map/ppermute | solution.py:96
  224.2 0.1 copy.104
  224.3 0.1 reshape.276
  224.4 1.5 scatter_custom_fusion
  225.9 1.5 scatter_custom_fusion.1
  227.3 2.2 collective-permute-done.8
  229.5 0.7 maximum_select_fusion
  (71 shorter events, 2.1 us)
Async XLA Ops:
  7.2 3.1 %copy-start.3 = (bf16[192,2048]{1,0:T(8,128)(2,1)S(1)}, bf16[192,2048]{1,0:T(8,128)(2,1)}, u32[]{:S(2)}) copy-start(bf16[192,2048]{1,0:T(8,128)(2,1)} %param.19) | copy-start | bytes 2359300
  7.2 3.1 %copy-start.2 = (bf16[192,2048]{1,0:T(8,128)(2,1)S(1)}, bf16[192,2048]{1,0:T(8,128)(2,1)}, u32[]{:S(2)}) copy-start(bf16[192,2048]{1,0:T(8,128)(2,1)} %param.20) | copy-start | bytes 2359300
  7.2 46.6 %all-gather.5.cloned.1.call-start = ((), (), s32[]{:S(2)}) async-start(), calls=%async_computation | async-start | bytes 7962624 | tf_op jit(solution)/shard_map/all_gather | solution.py:99
  9.5 74.8 %all-gather.7.cloned.1.call-start = ((), (), s32[]{:S(2)}) async-start(), calls=%async_computation.1 | async-start | bytes 2654208 | tf_op jit(solution)/shard_map/all_gather | solution.py:99
  10.2 1.5 copy-start.5
  10.2 139.5 %all-gather.9.cloned.1.call-start = ((), (), s32[]{:S(2)}) async-start(), calls=%async_computation.2 | async-start | bytes 14155776 | tf_op jit(solution)/shard_map/all_gather | solution.py:99
  11.6 4.3 %copy-start.9 = (s32[1,64]{1,0:T(1,128)S(1)}, s32[1,64]{1,0:T(1,128)}, u32[]{:S(2)}) copy-start(s32[1,64]{1,0:T(1,128)} %param.22) | copy-start | bytes 772
  11.6 5.0 %copy-start.7 = (f32[3072]{0:T(1024)S(1)}, f32[3072]{0:T(1024)}, u32[]{:S(2)}) copy-start(f32[3072]{0:T(1024)} %param.13) | copy-start | bytes 36868
  11.7 196.8 %all-gather.11.cloned.1.call-start = ((), (), s32[]{:S(2)}) async-start(), calls=%async_computation.3 | async-start | bytes 7077888 | tf_op jit(solution)/shard_map/all_gather | solution.py:99
  11.8 9.0 %collective-permute-start = (bf16[32,1536]{1,0:T(8,128)(2,1)S(1)}, bf16[32,1536]{1,0:T(8,128)(2,1)S(1)}, u32[]{:S(2)}, u32[]{:S(2)}) collective-permute-start(bf16[32,1536]{1,0:T(8,128)(2,1)S(1)} %get-tuple-element.22), channel_id=1, source_target_pairs={{0,16},{2,18},{4,20},{6,22},{8,24},{10,26},{12,28},{14,30},{16,0},... | collective-permute-start | bytes 294920 | tf_op jit(solution)/shard_map/ppermute | solution.py:93
  20.8 6.2 %collective-permute-start.1 = (bf16[2,32,1536]{2,1,0:T(8,128)(2,1)S(1)}, bf16[2,32,1536]{2,1,0:T(8,128)(2,1)S(1)}, u32[]{:S(2)}, u32[]{:S(2)}) collective-permute-start(bf16[2,32,1536]{2,1,0:T(8,128)(2,1)S(1)} %pad_maximum_fusion.2), channel_id=1, source_target_pairs={{0,1},{1,0},{2,3},{3,2},{4,5},{5,4},{6,7},{7,6},{8,9},{9,8},{10,11... | collective-permute-start | bytes 589832 | tf_op jit(solution)/shard_map/ppermute | solution.py:96
  58.1 17.2 %collective-permute-start.2 = (bf16[64,2432]{1,0:T(8,128)(2,1)S(1)}, bf16[64,2432]{1,0:T(8,128)(2,1)S(1)}, u32[]{:S(2)}, u32[]{:S(2)}) collective-permute-start(bf16[64,2432]{1,0:T(8,128)(2,1)S(1)} %concatenate.44), channel_id=1, source_target_pairs={{0,16},{2,18},{4,20},{6,22},{8,24},{10,26},{12,28},{14,30},{16,0},... | collective-permute-start | bytes 933896 | tf_op jit(solution)/shard_map/ppermute | solution.py:93
  60.7 15.8 %copy-start.4 = (f32[64,48]{1,0:T(8,128)}, f32[64,48]{1,0:T(8,128)S(1)}, u32[]{:S(2)}) copy-start(f32[64,48]{1,0:T(8,128)S(1)} %get-tuple-element.24) | copy-start | bytes 36868
  76.1 1.5 copy-start.6
  78.3 11.9 %copy-start.8 = (f32[3072]{0:T(1024)S(1)}, f32[3072]{0:T(1024)}, u32[]{:S(2)}) copy-start(f32[3072]{0:T(1024)} %param.18) | copy-start | bytes 36868
  78.8 7.2 %collective-permute-start.3 = (bf16[64,768]{1,0:T(8,128)(2,1)S(1)}, bf16[64,768]{1,0:T(8,128)(2,1)S(1)}, u32[]{:S(2)}, u32[]{:S(2)}) collective-permute-start(bf16[64,768]{1,0:T(8,128)(2,1)S(1)} %reshape.266), channel_id=1, source_target_pairs={{0,16},{2,18},{4,20},{6,22},{8,24},{10,26},{12,28},{14,30},{16,0},... | collective-permute-start | bytes 294920 | tf_op jit(solution)/shard_map/ppermute | solution.py:93
  88.6 10.5 %collective-permute-start.4 = (bf16[128,1536]{1,0:T(8,128)(2,1)S(1)}, bf16[128,1536]{1,0:T(8,128)(2,1)S(1)}, u32[]{:S(2)}, u32[]{:S(2)}) collective-permute-start(bf16[128,1536]{1,0:T(8,128)(2,1)S(1)} %convolution_convert_fusion), channel_id=1, source_target_pairs={{0,1},{1,0},{2,3},{3,2},{4,5},{5,4},{6,7},{7,6},{8,9},{9,8},{10,11... | collective-permute-start | bytes 1179656 | tf_op jit(solution)/shard_map/ppermute | solution.py:96
  99.3 0.5 copy-start.10
  99.3 56.8 %copy-start = (bf16[128,1536]{1,0:T(8,128)(2,1)}, bf16[128,1536]{1,0:T(8,128)(2,1)S(1)}, u32[]{:S(2)}) copy-start(bf16[128,1536]{1,0:T(8,128)(2,1)S(1)} %get-tuple-element.6) | copy-start | bytes 1179652
  157.1 27.3 %collective-permute-start.5 = (bf16[64,4224]{1,0:T(8,128)(2,1)}, bf16[64,4224]{1,0:T(8,128)(2,1)}, u32[]{:S(2)}, u32[]{:S(2)}) collective-permute-start(bf16[64,4224]{1,0:T(8,128)(2,1)} %concatenate.51), channel_id=1, source_target_pairs={{0,16},{2,18},{4,20},{6,22},{8,24},{10,26},{12,28},{14,30},{16,0},... | collective-permute-start | bytes 1622024 | tf_op jit(solution)/shard_map/ppermute | solution.py:93
  160.2 26.1 %copy-start.11 = (f32[128]{0:T(128)S(1)}, f32[128]{0:T(128)}, u32[]{:S(2)}) copy-start(f32[128]{0:T(128)} %copy-done.10) | copy-start | bytes 1540
  186.9 25.3 %collective-permute-start.6 = (bf16[64,2048]{0,1:T(8,128)(2,1)S(1)}, bf16[64,2048]{0,1:T(8,128)(2,1)S(1)}, u32[]{:S(2)}, u32[]{:S(2)}) collective-permute-start(bf16[64,2048]{0,1:T(8,128)(2,1)S(1)} %fusion.7), channel_id=1, source_target_pairs={{0,16},{2,18},{4,20},{6,22},{8,24},{10,26},{12,28},{14,30},{16,0},... | collective-permute-start | bytes 786440 | tf_op jit(solution)/shard_map/ppermute | solution.py:93
  189.4 34.5 %copy-start.1 = (bf16[128,1536]{1,0:T(8,128)(2,1)S(1)}, bf16[128,1536]{1,0:T(8,128)(2,1)}, u32[]{:S(2)}) copy-start(bf16[128,1536]{1,0:T(8,128)(2,1)} %copy-done) | copy-start | bytes 1179652
  189.4 34.7 %copy-start.12 = (s32[1,64]{1,0:T(1,128)S(1)}, s32[1,64]{1,0:T(1,128)}, u32[]{:S(2)}) copy-start(s32[1,64]{1,0:T(1,128)} %param.23) | copy-start | bytes 772
  217.6 6.3 %collective-permute-start.7 = (bf16[2,32,1536]{2,1,0:T(8,128)(2,1)S(1)}, bf16[2,32,1536]{2,1,0:T(8,128)(2,1)S(1)}, u32[]{:S(2)}, u32[]{:S(2)}) collective-permute-start(bf16[2,32,1536]{2,1,0:T(8,128)(2,1)S(1)} %dynamic-slice_bitcast_fusion), channel_id=1, source_target_pairs={{0,1},{1,0},{2,3},{3,2},{4,5},{5,4},{6,7},{7,6},{8,9},{9,8},{10,11... | collective-permute-start | bytes 589832 | tf_op jit(solution)/shard_map/ppermute | solution.py:96
  224.0 5.6 %collective-permute-start.8 = (bf16[32,1536]{1,0:T(8,128)(2,1)S(1)}, bf16[32,1536]{1,0:T(8,128)(2,1)S(1)}, u32[]{:S(2)}, u32[]{:S(2)}) collective-permute-start(bf16[32,1536]{1,0:T(8,128)(2,1)S(1)} %get-tuple-element.20), channel_id=1, source_target_pairs={{0,16},{2,18},{4,20},{6,22},{8,24},{10,26},{12,28},{14,30},{16,0},... | collective-permute-start | bytes 294920 | tf_op jit(solution)/shard_map/ppermute | solution.py:93
Sparse Core Ops, SparseCore 0:
  9.7 44.0 all-gather.4
  55.4 28.7 all-gather.6
  85.9 63.7 all-gather.8
  151.2 57.2 all-gather.10

commit v2 on v1

--- a/solution.py
+++ b/solution.py
@@ -1,6 +1,10 @@
+import functools
+
 import jax
 import jax.numpy as jnp
 from jax import lax
+from jax.experimental import pallas as pl
+from jax.experimental.pallas import tpu as pltpu
 from jax.sharding import PartitionSpec as P
 
 HEAD_DIM = 96
@@ -8,6 +12,8 @@
 OCT = 8
 BF = jnp.bfloat16
 F32 = jnp.float32
+VMEM = 32 * 1024 * 1024
+VMEM_ALL = 60 * 1024 * 1024
 
 
 def norm_rows(rows, gain):
@@ -85,75 +91,315 @@
     return (layer_out, cache_keys, cache_values)
 
 
+def prepared(x, gain_ref, lhs_ref, coded_ref, squares_ref):
+    rows, depth = x.shape
+    keep, wide = rows // 2, depth // OCT
+    squares = jnp.broadcast_to(jnp.sum(x * x, axis=1, keepdims=True), (rows, 128))
+    scaled = (x * gain_ref[...]).astype(BF)
+    if len(lhs_ref.shape) == 2:
+        lhs_ref[...] = scaled
+    else:
+        for i in range(OCT):
+            lhs_ref[i] = scaled[:, i * wide : (i + 1) * wide]
+    high = squares.astype(BF).astype(F32)
+    lane = lax.broadcasted_iota(jnp.int32, (rows, 128), 1)
+    coded_ref[...] = jnp.where(lane < 64, high, squares - high)[keep:].astype(BF)
+    squares_ref[...] = squares[:keep]
+
+
+def first_kernel(row, kept_ref, partner_ref, others_ref, gain_ref, rows_ref, lhs_ref, coded_ref, squares_ref):
+    mine = kept_ref.shape[0]
+    own = (kept_ref, partner_ref)
+    for g in range(2):
+        at = pl.multiple_of(2 * mine * g + row[0] * mine, mine)
+        rows_ref[pl.ds(at, mine)] = own[g][...]
+        at = pl.multiple_of(2 * mine * g + (1 - row[0]) * mine, mine)
+        rows_ref[pl.ds(at, mine)] = others_ref[g]
+    prepared(rows_ref[...].astype(F32), gain_ref, lhs_ref, coded_ref, squares_ref)
+
+
+def middle_kernel(row, rows_ref, terms_ref, others_ref, gain_ref, middle_ref, lhs_ref, coded_ref, squares_ref):
+    total = terms_ref[...].astype(F32) + others_ref[...].astype(F32)
+    middle_ref[...] = (rows_ref[...].astype(F32) + total).astype(BF)
+    prepared(middle_ref[...].astype(F32), gain_ref, lhs_ref, coded_ref, squares_ref)
+
+
+def prepare(kernel, row, operands, rows, depth, cut):
+    keep = rows // 2
+    shapes = [
+        jax.ShapeDtypeStruct((rows, depth), BF),
+        jax.ShapeDtypeStruct((OCT, rows, depth // OCT) if cut else (rows, depth), BF),
+        jax.ShapeDtypeStruct((keep, 128), BF),
+        jax.ShapeDtypeStruct((keep, 128), F32),
+    ]
+    def spec(x):
+        return pl.BlockSpec(x.shape, lambda j, p: (0,) * len(x.shape))
+    return pl.pallas_call(
+        kernel,
+        grid_spec=pltpu.PrefetchScalarGridSpec(
+            num_scalar_prefetch=1,
+            grid=(1,),
+            in_specs=[spec(x) for x in operands],
+            out_specs=[spec(x) for x in shapes],
+        ),
+        out_shape=shapes,
+        compiler_params=pltpu.CompilerParams(vmem_limit_bytes=VMEM),
+    )(row, *operands)
+
+
+def rows_kernel(place, lhs, coded_ref, *refs):
+    weights, (sent_ref, own_ref) = refs[: 2 * OCT], refs[2 * OCT :]
+    step = pl.program_id(0)
+    block = weights[0].shape[-1]
+    keep, width = own_ref.shape
+
+    @pl.when(step == 0)
+    def _():
+        sent_ref[:, width:] = coded_ref[...]
+
+    for i in range(2):
+        total = None
+        for k in range(OCT):
+            term = dot(lhs[place[0] ^ k], weights[OCT * i + k][...])
+            total = term if total is None else total + term
+        columns = pl.ds(pl.multiple_of(i * (width // 2) + step * block, 128), block)
+        own_ref[:, columns] = total[:keep]
+        sent_ref[:, columns] = total[keep:].astype(BF)
+
+
+def rows_product(place, lhs, coded, pieces, block):
+    _, rows, wide = lhs.shape
+    keep = rows // 2
+    each = pieces[0].shape[1]
+    width = 2 * each
+    whole = lambda j, p: (0, 0)
+    return pl.pallas_call(
+        rows_kernel,
+        grid_spec=pltpu.PrefetchScalarGridSpec(
+            num_scalar_prefetch=1,
+            grid=(each // block,),
+            in_specs=[pl.BlockSpec(lhs.shape, lambda j, p: (0, 0, 0)), pl.BlockSpec(coded.shape, whole)]
+            + [pl.BlockSpec((wide, block), lambda j, p: (0, j))] * len(pieces),
+            out_specs=[pl.BlockSpec((keep, width + 128), whole), pl.BlockSpec((keep, width), whole)],
+        ),
+        out_shape=[jax.ShapeDtypeStruct((keep, width + 128), BF), jax.ShapeDtypeStruct((keep, width), F32)],
+        compiler_params=pltpu.CompilerParams(vmem_limit_bytes=VMEM_ALL),
+    )(place, lhs, coded, *pieces)
+
+
+def flat_kernel(x_ref, coded_ref, w_ref, sent_ref, own_ref):
+    step = pl.program_id(0)
+    block = w_ref.shape[1]
+    keep, width = own_ref.shape
+    if sent_ref.shape[1] > width:
+
+        @pl.when(step == 0)
+        def _():
+            sent_ref[:, width:] = coded_ref[...]
+
+    total = dot(x_ref[...], w_ref[...])
+    columns = pl.ds(pl.multiple_of(step * block, 128), block)
+    own_ref[:, columns] = total[:keep]
+    sent_ref[:, columns] = total[keep:].astype(BF)
+
+
+def flat_product(x, coded, w, block, with_squares):
+    rows, depth = x.shape
+    keep = rows // 2
+    width = w.shape[1]
+    sent = width + (128 if with_squares else 0)
+    whole = lambda j: (0, 0)
+    return pl.pallas_call(
+        flat_kernel,
+        grid=(width // block,),
+        in_specs=[
+            pl.BlockSpec(x.shape, whole),
+            pl.BlockSpec(coded.shape, whole),
+            pl.BlockSpec((depth, block), lambda j: (0, j)),
+        ],
+        out_specs=[pl.BlockSpec((keep, sent), whole), pl.BlockSpec((keep, width), whole)],
+        out_shape=[jax.ShapeDtypeStruct((keep, sent), BF), jax.ShapeDtypeStruct((keep, width), F32)],
+        compiler_params=pltpu.CompilerParams(vmem_limit_bytes=VMEM),
+    )(x, coded, w)
+
+
+def columns_kernel(natural, place, own_ref, got_ref, *refs):
+    weights, (out_ref, parts, a_ref) = refs[:OCT], refs[OCT:]
+    keep, depth = own_ref.shape
+    wide = weights[0].shape[-1] // 2
+    a_ref[:keep] = own_ref[...]
+    a_ref[keep:] = got_ref[...]
+    for k in range(OCT):
+        lower = dot(a_ref[:, : depth // 2], weights[k][...])
+        upper = dot(a_ref[:, depth // 2 :], weights[k][...])
+        parts[k if natural else place[0] ^ k] = (lower[:, :wide] + upper[:, wide:]).astype(BF)
+    for i in range(OCT):
+        out_ref[:, i * wide : (i + 1) * wide] = parts[i]
+
+
+def columns_product(place, own, got, pieces):
+    keep, depth = own.shape
+    rows = 2 * keep
+    natural = len(pieces) == 1
+    deep, double = depth // 2, pieces[0].shape[1]
+    wide = double // 2
+    whole = lambda j, p: (0, 0)
+    if natural:
+        pieces = pieces * OCT
+        specs = [pl.BlockSpec((deep, double), lambda j, p, k=k: (k, 0)) for k in range(OCT)]
+    else:
+        specs = [pl.BlockSpec((deep, double), whole)] * OCT
+    return pl.pallas_call(
+        functools.partial(columns_kernel, natural),
+        grid_spec=pltpu.PrefetchScalarGridSpec(
+            num_scalar_prefetch=1,
+            grid=(1,),
+            in_specs=[pl.BlockSpec((keep, depth), whole)] * 2 + specs,
+            out_specs=pl.BlockSpec((rows, OCT * wide), whole),
+            scratch_shapes=[pltpu.VMEM((OCT, rows, wide), BF), pltpu.VMEM((rows, depth), BF)],
+        ),
+        out_shape=jax.ShapeDtypeStruct((rows, OCT * wide), BF),
+        compiler_params=pltpu.CompilerParams(vmem_limit_bytes=VMEM),
+    )(place, own, got, *pieces)
+
+
+def attention_kernel(model, *refs):
+    own, got, squares, cosine, left, right, seg_row, seg_col, slot, out_ref, keys_ref, values_ref = refs
+    count, width = out_ref.shape
+    heads_here = width // HEAD_DIM
+    last = got[:, 3 * width :].astype(F32)
+    scale = lax.rsqrt((squares[:, :1] + last[:, :1] + last[:, 64:65]) / model + EPS)
+    query, key, value = (
+        (own[:, i * width : (i + 1) * width] + got[:, i * width : (i + 1) * width].astype(F32)) * scale for i in range(3)
+    )
+
+    def rotated(x):
+        ahead = pltpu.roll(x, width - HEAD_DIM // 2, 1)
+        behind = pltpu.roll(x, HEAD_DIM // 2, 1)
+        return (x * cosine[...] + ahead * left[...] + behind * right[...]).astype(BF)
+
+    q_rot, k_rot, v_b = rotated(query), rotated(key), value.astype(BF)
+    spot = lax.broadcasted_iota(jnp.int32, (count, count), 0)
+    hot = jnp.where(spot == slot[...], 1.0, 0.0).astype(BF)
+    keys_ref[...] = dot(hot, k_rot).astype(BF)
+    values_ref[...] = dot(hot, v_b).astype(BF)
+    lane = lax.broadcasted_iota(jnp.int32, (count, width), 1)
+    within = [(lane >= h * HEAD_DIM) & (lane < (h + 1) * HEAD_DIM) for h in range(heads_here)]
+    zero = jnp.zeros((count, width), BF)
+    spread_q = jnp.concatenate([jnp.where(w, q_rot, zero) for w in within], axis=0)
+    scores = lax.dot_general(spread_q, k_rot, (((1,), (1,)), ((), ())), preferred_element_type=F32)
+    scores = (scores * (1.0 / HEAD_DIM**0.5)).reshape(heads_here, count, count)
+    other = lax.broadcasted_iota(jnp.int32, (count, count), 1)
+    allowed = (seg_col[...] == seg_row[...]) & (other <= spot)
+    scores = jnp.where(allowed[None], scores, -1e30)
+    expo = jnp.exp(scores - jnp.max(scores, axis=-1, keepdims=True))
+    probs = (expo / jnp.sum(expo, axis=-1, keepdims=True)).astype(BF)
+    mixed = dot(probs.reshape(heads_here * count, count), v_b)
+    total = jnp.zeros((count, width), F32)
+    for h in range(heads_here):
+        total = total + jnp.where(within[h], mixed[h * count : (h + 1) * count], 0.0)
+    out_ref[...] = total.astype(BF)
+
+
+def attend(model, own, got, squares, tables, segment, slots):
+    count, width = own.shape[0], own.shape[1] // 3
+    out = jax.ShapeDtypeStruct((count, width), BF)
+    return pl.pallas_call(
+        functools.partial(attention_kernel, model),
+        out_shape=[out, out, out],
+        compiler_params=pltpu.CompilerParams(vmem_limit_bytes=VMEM),
+    )(own, got, squares, *tables, segment.reshape(1, count), segment.reshape(count, 1), slots.reshape(1, count))
+
+
+def rotation_tables(segment, width):
+    half = HEAD_DIM // 2
+    lane = jnp.arange(width, dtype=jnp.int32)
+    freq = 10000.0 ** (-2.0 * (lane % half).astype(F32) / HEAD_DIM)
+    angle = positions(segment).astype(F32)[:, None] * freq[None, :]
+    first = ((lane % HEAD_DIM) < half)[None, :]
+    sine = jnp.sin(angle)
+    return jnp.cos(angle), jnp.where(first, -sine, 0.0), jnp.where(first, 0.0, sine)
+
+
+def after(x, *others):
+    return lax.optimization_barrier((x,) + others)[0]
+
+
 def octet_plan(n_group):
+    def swap(bit):
+        pairs = [(g, g ^ bit) for g in range(n_group)]
+        return lambda x: lax.ppermute(x, "group", pairs)
+
     octets = [[OCT * i + j for j in range(OCT)] for i in range(n_group // OCT)]
-    swap = [(g, g ^ OCT) for g in range(n_group)]
-
-    def across(x):
-        return lax.ppermute(x, "group", swap)
+    core, near, next_to, across = swap(1), swap(2), swap(4), swap(OCT)
 
     def other_head(x):
         return lax.ppermute(x, "head", [(0, 1), (1, 0)])
 
-    def gather(w, axis):
-        return lax.all_gather(w, "group", axis=axis, tiled=True, axis_index_groups=octets)
-
-    def split_sum(x):
-        high = x.astype(BF)
-        low = (x - high.astype(F32)).astype(BF)
-        return jnp.concatenate([high, low, jnp.zeros((x.shape[0], 126), BF)], axis=1)
-
-    def exchange(partial, squares):
-        rows = partial.shape[0] // 2
-        sent = jnp.concatenate([partial[rows:].astype(BF), split_sum(squares[rows:])], axis=1)
-        got = across(sent).astype(F32)
-        width = partial.shape[1]
-        total = partial[:rows] + got[:, :width]
-        return total, squares[:rows] + got[:, width : width + 1] + got[:, width + 1 : width + 2]
+    def beside(w):
+        depth = w.shape[0]
+        return jnp.concatenate([w[: depth // 2], w[depth // 2 :]], axis=1)
+
+    def all_pieces(own, x, z, diagonal):
+        return [p for part in (own, x, z, diagonal) for p in (part, core(part))]
+
+    def gathered(w):
+        return lax.all_gather(w, "group", axis=0, tiled=True, axis_index_groups=octets)
 
     def per_device(
         tokens, attn_gain, w_query, w_key, w_value, w_out, mlp_gain, w_gate, w_up, w_down, segment_ids, cache_slot,
     ):
-        side = lax.axis_index("group") // OCT
+        group = lax.axis_index("group")
+        side = group // OCT
+        place = (group % OCT).astype(jnp.int32).reshape(1)
         row = lax.axis_index("head")
+        at_row = row.astype(jnp.int32).reshape(1)
         mine, model = tokens.shape
         half = model // 2
         width = w_query.shape[1]
         units = w_gate.shape[1]
 
-        w_qkv = gather(jnp.concatenate([w_query, w_key, w_value], axis=1), 0)
-        w_o = gather(w_out, 1)
-        w_gu = gather(jnp.concatenate([w_gate, w_up], axis=1), 0)
-        w_d = gather(w_down, 1)
+        def own_gain(gain):
+            return lax.dynamic_slice(gain, (side * half,), (half,)).reshape(1, half)
 
         kept = lax.dynamic_slice(tokens, (0, side * half), (mine, half))
         given = lax.dynamic_slice(tokens, (0, (1 - side) * half), (mine, half))
-        both = jnp.stack([kept, across(given)])
-        others = other_head(both)
-        rows = jnp.stack([jnp.where(row == 0, both, others), jnp.where(row == 0, others, both)], axis=1)
-        rows = rows.reshape(4 * mine, half)
-
-        def scaled(x, gain):
-            values = x.astype(F32)
-            own = lax.dynamic_slice(gain, (side * half,), (half,))
-            return (values * own).astype(BF), jnp.sum(values * values, axis=-1, keepdims=True)
-
-        lhs, squares = scaled(rows, attn_gain)
-        qkv, squares = exchange(dot(lhs, w_qkv), squares)
-        qkv = qkv * lax.rsqrt(squares / model + EPS)
-        attended, cache_keys, cache_values = attention(
-            qkv[:, :width], qkv[:, width : 2 * width], qkv[:, 2 * width :].astype(BF),
-            segment_ids[0], cache_slot[0],
+        gain1, gain2 = own_gain(attn_gain), own_gain(mlp_gain)
+        o_own, d_own = lax.optimization_barrier((beside(w_out), beside(w_down)))
+        tables = rotation_tables(segment_ids[0], width)
+        w_g, w_u, w_d = gathered(w_gate), gathered(w_up), gathered(d_own)
+        partner = across(given)
+        cut = width // 2
+        first = jnp.concatenate([w_query, w_key[:, :cut]], axis=1)
+        second = jnp.concatenate([w_key[:, cut:], w_value], axis=1)
+        x_1, x_2 = near(first), near(second)
+        z_2, z_1 = next_to(second), next_to(first)
+        others = other_head(jnp.stack([kept, partner]))
+        d_1, d_2 = next_to(after(x_1, others)), near(z_2)
+        x_o, z_o = near(after(o_own, d_1)), next_to(after(o_own, d_1))
+        d_o = near(z_o)
+        others = after(others, gain1, gain2, *tables)
+        rows, lhs, coded, squares = prepare(
+            first_kernel, at_row, (kept, partner, others, gain1), 4 * mine, half, True
         )
-        attended = jnp.concatenate([attended, across(attended)], axis=0)
-        terms = dot(attended, w_o).astype(BF)
-        middle = (rows.astype(F32) + (terms.astype(F32) + other_head(terms).astype(F32))).astype(BF)
-        lhs, squares = scaled(middle, mlp_gain)
-        gu, squares = exchange(dot(lhs, w_gu), squares)
-        gu = gu * lax.rsqrt(squares / model + EPS)
-        hidden = (jax.nn.silu(gu[:, :units]) * gu[:, units:]).astype(BF)
-        hidden = jnp.concatenate([hidden, across(hidden)], axis=0)
-        terms = dot(hidden, w_d).astype(BF).reshape(2, 2, mine, half)
+        pieces = all_pieces(first, x_1, z_1, d_1) + all_pieces(second, x_2, z_2, d_2)
+        sent, own = rows_product(place, lhs, coded, pieces, 384)
+        got = after(across(sent), x_o, z_o)
+        attended, cache_keys, cache_values = attend(model, own, got, squares, tables, segment_ids[0], cache_slot[0])
+        terms = columns_product(place, attended, across(attended), all_pieces(o_own, x_o, z_o, d_o))
+        middle, lhs, coded, squares = prepare(
+            middle_kernel, at_row, (rows, terms, other_head(terms), gain2), 4 * mine, half, False
+        )
+        sent_g, own_g = flat_product(lhs, coded, w_g, 512, True)
+        got_g = across(sent_g)
+        sent_u, own_u = flat_product(after(lhs, sent_g), coded, w_u, 512, False)
+        got_u = across(sent_u)
+        last = got_g[:, units:].astype(F32)
+        scale = lax.rsqrt((squares[:, :1] + last[:, :1] + last[:, 64:65]) / model + EPS)
+        gate = (own_g + got_g[:, :units].astype(F32)) * scale
+        up = (own_u + got_u.astype(F32)) * scale
+        hidden = (jax.nn.silu(gate) * up).astype(BF)
+        terms = columns_product(place, hidden, across(hidden), [w_d]).reshape(2, 2, mine, half)
         given = other_head(lax.dynamic_index_in_dim(terms, 1 - row, 1, keepdims=False))
         mlp = lax.dynamic_index_in_dim(terms, row, 1, keepdims=False).astype(F32) + given.astype(F32)
         kept = lax.dynamic_index_in_dim(middle.reshape(2, 2, mine, half), row, 1, keepdims=False)

time: 237 us -> 208 us (0.88)
  waiting for transfers between devices: 168 us -> 120 us
  starting transfers between devices: 16.7 us -> 37.3 us
  matrix products: 19.2 us -> 0 us
  Pallas kernels: 0 us -> 16.5 us
  local copies, waits for them, and re-layouts: 9.88 us -> 14.7 us
  other arithmetic: 8.21 us -> 4.73 us
    all_gather x4 -> x3, waiting for transfers between devices: 100 us -> 13.7 us  [gathered(): lax.all_gather(w, 'group', axis=0, tiled=True, axis_index_groups=octets)]
    ppermute x6 -> x28, waiting for transfers between devices: 49.6 us -> 90.2 us  [swap(): return lambda x: lax.ppermute(x, 'group', pairs)]
    ppermute x6 -> x28, starting transfers between devices: 11.7 us -> 32.2 us  [swap(): return lambda x: lax.ppermute(x, 'group', pairs)]
    dot_general x6 -> x0, matrix products: 18.9 us -> none  [the longest x4 18.4 us: dot(): return jnp.dot(a, b, preferred_element_type=F32)]
    pallas_call x0 -> x8, Pallas kernels: none -> 16.5 us  [the longest x1 6.01 us: rows_product(): pl.pallas_call(rows_kernel, grid_spec=pltpu.PrefetchScalarGridSpec(num_sc...]
    unnamed x32 -> x42, local copies, waits for them, and re-layouts: 1.82 us -> 12.1 us
    ppermute x3, waiting for transfers between devices: 18 us -> 14.8 us  [other_head(): return lax.ppermute(x, 'head', [(0, 1), (1, 0)])]
    scatter x2 -> x0, local copies, waits for them, and re-layouts: 2.91 us -> none  [the longest x1 1.46 us: attention(): cache_keys = jnp.zeros_like(k_flat).at[slots].set(k_flat)]
  transfers between devices with their start and end apart: 13 -> 34, of which waited for: 13 -> 17; matrix products, arithmetic and copies ran while one was open for 12% -> 3% of each run, Pallas kernels for 0% -> 7%
where the time goes in v2:
time: 208 us; the launch traced here: 207 us
  waiting for transfers between devices  120 us (58%)
  starting transfers between devices  37.3 us (18%)
  Pallas kernels  16.5 us (8%)
  local copies, waits for them, and re-layouts  14.7 us (7%)
  between operations  14.1 us (7%)
  other arithmetic  4.73 us (2%)
    ppermute x28, waiting for transfers between devices, swap(): return lambda x: lax.ppermute(x, 'group', pairs)  90.2 us
    ppermute x28, starting transfers between devices, swap(): return lambda x: lax.ppermute(x, 'group', pairs)  32.2 us
    ppermute x3, waiting for transfers between devices, other_head(): return lax.ppermute(x, 'head', [(0, 1), (1, 0)])  14.8 us
    all_gather x3, waiting for transfers between devices, gathered(): lax.all_gather(w, 'group', axis=0, tiled=True, axis_index_groups=octets)  13.7 us
    unnamed x42, local copies, waits for them, and re-layouts  12.1 us
    pallas_call x1, Pallas kernels, rows_product(): pl.pallas_call(rows_kernel, grid_spec=pltpu.PrefetchScalarGridSpec(num_sc...  6.01 us
    ppermute x3, starting transfers between devices, other_head(): return lax.ppermute(x, 'head', [(0, 1), (1, 0)])  4.97 us
    pallas_call x2, Pallas kernels, columns_product(): pl.pallas_call(functools.partial(columns_kernel, natural), grid_spec=pltp...  4.26 us
  transfers between devices with their start and end apart: 34, of which 17 were waited for; matrix products, arithmetic and copies ran while one was open for 3% of the time, Pallas kernels for 7%

profile of v2, /device:TPU:0, one launch (start us, length us, event | category | flops | bytes accessed | tf_op | source)
XLA Modules:
  0.0 207.5 jit_solution(11012364711735780342)
XLA Ops:
  7.3 0.7 all-gather.4.cloned.1.call-update
  8.0 0.7 all-gather.6.cloned.1.call-update
  8.8 1.2 fusion.19
  9.9 0.2 copy.33
  10.3 1.0 fusion.20
  11.8 1.2 pad_maximum_fusion
  13.1 4.1 %collective-permute-start = (bf16[32,1536]{1,0:T(8,128)(2,1)S(1)}, bf16[32,1536]{1,0:T(8,128)(2,1)S(1)}, u32[]{:S(2)}, u32[]{:S(2)}) collective-permute-start(bf16[32,1536]{1,0:T(8,128)(2,1)S(1)} %get-tuple-element.59), channel_id=1, source_target_pairs={{0,16},{2,18},{4,20},{6,22},{8,24},{10,26},{12,28},{14,30},{16,0},... | collective-permute-start | bytes 294920 | tf_op jit(solution)/shard_map/ppermute | solution.py:331
  17.3 1.6 collective-permute-start.3
  18.8 1.0 pad_maximum_fusion.2.refs_8_
  19.9 1.6 collective-permute-start.12
  21.5 0.6 collective-permute-done.partner_ref
  22.1 1.6 collective-permute-start.1
  23.8 1.6 collective-permute-start.10
  25.3 0.6 collective-permute-start.5
  25.9 2.3 %collective-permute-done.1.others_ref = bf16[2,32,1536]{2,1,0:T(8,128)(2,1)S(1)} collective-permute-done((bf16[2,32,1536]{2,1,0:T(8,128)(2,1)S(1)}, bf16[2,32,1536]{2,1,0:T(8,128)(2,1)S(1)}, u32[]{:S(2)}, u32[]{:S(2)}) %collective-permute-start.1) | collective-permute-done | bytes 196640 | tf_op jit(solution)/shard_map/ppermute | solution.py:337
  28.3 9.7 %collective-permute-done.3.refs_2_ = bf16[192,1152]{1,0:T(8,128)(2,1)S(1)} collective-permute-done((bf16[192,1152]{1,0:T(8,128)(2,1)S(1)}, bf16[192,1152]{1,0:T(8,128)(2,1)S(1)}, u32[]{:S(2)}, u32[]{:S(2)}) %collective-permute-start.3) | collective-permute-done | bytes 442400 | tf_op jit(solution)/shard_map/ppermute | solution.py:331
  37.9 4.2 %collective-permute-done.12.refs_12_ = bf16[192,1152]{1,0:T(8,128)(2,1)S(1)} collective-permute-done((bf16[192,1152]{1,0:T(8,128)(2,1)S(1)}, bf16[192,1152]{1,0:T(8,128)(2,1)S(1)}, u32[]{:S(2)}, u32[]{:S(2)}) %collective-permute-start.12) | collective-permute-done | bytes 442400 | tf_op jit(solution)/shard_map/ppermute | solution.py:331
  42.1 1.5 collective-permute-start.7
  43.9 12.1 %collective-permute-done.10.refs_10_ = bf16[192,1152]{1,0:T(8,128)(2,1)S(1)} collective-permute-done((bf16[192,1152]{1,0:T(8,128)(2,1)S(1)}, bf16[192,1152]{1,0:T(8,128)(2,1)S(1)}, u32[]{:S(2)}, u32[]{:S(2)}) %collective-permute-start.10) | collective-permute-done | bytes 442400 | tf_op jit(solution)/shard_map/ppermute | solution.py:331
  56.0 2.5 %collective-permute-start.14 = (bf16[192,1152]{1,0:T(8,128)(2,1)S(1)}, bf16[192,1152]{1,0:T(8,128)(2,1)}, u32[]{:S(2)}, u32[]{:S(2)}) collective-permute-start(bf16[192,1152]{1,0:T(8,128)(2,1)S(1)} %collective-permute-done.12.refs_12_), channel_id=1, source_target_pairs={{0,4},{2,6},{4,0},{6,2},{8,12},{10,14},{12,8},{14,10},{16,20},{18,... | collective-permute-start | bytes 1327112 | tf_op jit(solution)/shard_map/ppermute | solution.py:331
  58.4 2.8 %collective-permute-done.5.refs_4_ = bf16[192,1152]{1,0:T(8,128)(2,1)} collective-permute-done((bf16[192,1152]{1,0:T(8,128)(2,1)S(1)}, bf16[192,1152]{1,0:T(8,128)(2,1)}, u32[]{:S(2)}, u32[]{:S(2)}) %collective-permute-start.5) | collective-permute-done | bytes 442400 | tf_op jit(solution)/shard_map/ppermute | solution.py:331
  61.2 0.5 collective-permute-start.4
  62.1 13.8 %collective-permute-done.7.refs_6_ = bf16[192,1152]{1,0:T(8,128)(2,1)} collective-permute-done((bf16[192,1152]{1,0:T(8,128)(2,1)S(1)}, bf16[192,1152]{1,0:T(8,128)(2,1)}, u32[]{:S(2)}, u32[]{:S(2)}) %collective-permute-start.7) | collective-permute-done | bytes 442400 | tf_op jit(solution)/shard_map/ppermute | solution.py:331
  75.9 1.3 collective-permute-start.18
  77.3 0.3 collective-permute-start.6
  77.6 0.3 collective-permute-start.8
  77.9 0.2 collective-permute-start.15
  78.1 0.7 collective-permute-start.17
  78.8 6.6 %collective-permute-done.18.refs_4_ = bf16[384,384]{1,0:T(8,128)(2,1)S(1)} collective-permute-done((bf16[384,384]{1,0:T(8,128)(2,1)S(1)}, bf16[384,384]{1,0:T(8,128)(2,1)S(1)}, u32[]{:S(2)}, u32[]{:S(2)}) %collective-permute-start.18) | collective-permute-done | bytes 294944 | tf_op jit(solution)/shard_map/ppermute | solution.py:331
  85.4 1.1 collective-permute-start.23
  86.5 0.8 fusion.2
  87.3 0.3 shard_map.139
  87.6 0.8 copy-done.4
  88.4 0.6 copy-done.5
  89.0 6.0 %shard_map.140 = (bf16[64,2432]{1,0:T(8,128)(2,1)}, f32[64,2304]{1,0:T(8,128)}) custom-call(s32[1]{0:T(128)} %bitcast.5.place, bf16[8,128,192]{2,1,0:T(8,128)(2,1)} %copy-done.4, bf16[64,128]{1,0:T(8,128)(2,1)} %copy-done.5, bf16[192,1152]{1,0:T(8,128)(2,1)} %copy-done.8, bf16[192,1152]{1,0:T(8,128)(2,1)} %collective-permute-done.2.refs_1_, ...), custom_call_target="tpu_custom_call" | custom-call | tf_op jit(solution)/shard_map/pallas_call | solution.py:176
  95.0 1.5 collective-permute-start.16
  96.5 0.5 collective-permute-start.21
  97.0 3.4 %collective-permute-done.23.refs_6_ = bf16[384,384]{1,0:T(8,128)(2,1)S(1)} collective-permute-done((bf16[384,384]{1,0:T(8,128)(2,1)S(1)}, bf16[384,384]{1,0:T(8,128)(2,1)S(1)}, u32[]{:S(2)}, u32[]{:S(2)}) %collective-permute-start.23) | collective-permute-done | bytes 294944 | tf_op jit(solution)/shard_map/ppermute | solution.py:331
  100.5 10.4 %collective-permute-done.16.refs_1_ = bf16[64,2432]{1,0:T(8,128)(2,1)S(1)} collective-permute-done((bf16[64,2432]{1,0:T(8,128)(2,1)}, bf16[64,2432]{1,0:T(8,128)(2,1)S(1)}, u32[]{:S(2)}, u32[]{:S(2)}) %collective-permute-start.16) | collective-permute-done | bytes 311328 | tf_op jit(solution)/shard_map/ppermute | solution.py:331
  111.0 1.1 copy-done.3
  112.0 1.6 shard_map.141
  113.6 2.7 %collective-permute-start.19 = (bf16[64,768]{1,0:T(8,128)(2,1)S(1)}, bf16[64,768]{1,0:T(8,128)(2,1)S(1)}, u32[]{:S(2)}, u32[]{:S(2)}) collective-permute-start(bf16[64,768]{1,0:T(8,128)(2,1)S(1)} %get-tuple-element.38.own_ref), channel_id=1, source_target_pairs={{0,16},{2,18},{4,20},{6,22},{8,24},{10,26},{12,28},{14,30},{16,0},... | collective-permute-start | bytes 294920 | tf_op jit(solution)/shard_map/ppermute | solution.py:331
  116.3 4.2 %collective-permute-done.19.got_ref = bf16[64,768]{1,0:T(8,128)(2,1)S(1)} collective-permute-done((bf16[64,768]{1,0:T(8,128)(2,1)S(1)}, bf16[64,768]{1,0:T(8,128)(2,1)S(1)}, u32[]{:S(2)}, u32[]{:S(2)}) %collective-permute-start.19) | collective-permute-done | bytes 98336 | tf_op jit(solution)/shard_map/ppermute | solution.py:331
  120.5 2.2 %shard_map.142.terms_ref = bf16[128,1536]{1,0:T(8,128)(2,1)S(1)} custom-call(s32[1]{0:T(128)} %bitcast.5.place, bf16[64,768]{1,0:T(8,128)(2,1)S(1)} %get-tuple-element.38.own_ref, bf16[64,768]{1,0:T(8,128)(2,1)S(1)} %collective-permute-done.19.got_ref, bf16[384,384]{1,0:T(8,128)(2,1)S(1)} %pad_maximum_fusion.3.refs_0_, ...), custom_call_target="tpu_custom_call" | custom-call | tf_op jit(solution)/shard_map/pallas_call | solution.py:252
  122.6 1.8 collective-permute-start.25
  124.4 6.9 %collective-permute-done.25.others_ref = bf16[128,1536]{1,0:T(8,128)(2,1)S(1)} collective-permute-done((bf16[128,1536]{1,0:T(8,128)(2,1)S(1)}, bf16[128,1536]{1,0:T(8,128)(2,1)S(1)}, u32[]{:S(2)}, u32[]{:S(2)}) %collective-permute-start.25) | collective-permute-done | bytes 393248 | tf_op jit(solution)/shard_map/ppermute | solution.py:337
  131.3 0.3 shard_map.143
  131.7 3.3 %copy-done.2 = bf16[1536,2048]{1,0:T(8,128)(2,1)S(1)} copy-done((bf16[1536,2048]{1,0:T(8,128)(2,1)S(1)}, bf16[1536,2048]{1,0:T(8,128)(2,1)}, u32[]{:S(2)}) %copy-start.2) | copy-done | bytes 6291480
  134.9 2.0 shard_map.144
  137.0 3.6 %collective-permute-start.26 = (bf16[64,2176]{1,0:T(8,128)(2,1)S(1)}, bf16[64,2176]{1,0:T(8,128)(2,1)S(1)}, u32[]{:S(2)}, u32[]{:S(2)}) collective-permute-start(bf16[64,2176]{1,0:T(8,128)(2,1)S(1)} %get-tuple-element.43), channel_id=1, source_target_pairs={{0,16},{2,18},{4,20},{6,22},{8,24},{10,26},{12,28},{14,30},{16,0},... | collective-permute-start | bytes 835592 | tf_op jit(solution)/shard_map/ppermute | solution.py:331
  140.6 2.8 %copy-done.1 = bf16[1536,2048]{1,0:T(8,128)(2,1)S(1)} copy-done((bf16[1536,2048]{1,0:T(8,128)(2,1)S(1)}, bf16[1536,2048]{1,0:T(8,128)(2,1)}, u32[]{:S(2)}) %copy-start.1) | copy-done | bytes 6291480
  143.4 2.1 shard_map.145
  145.6 7.9 %collective-permute-done.26 = bf16[64,2176]{1,0:T(8,128)(2,1)S(1)} collective-permute-done((bf16[64,2176]{1,0:T(8,128)(2,1)S(1)}, bf16[64,2176]{1,0:T(8,128)(2,1)S(1)}, u32[]{:S(2)}, u32[]{:S(2)}) %collective-permute-start.26) | collective-permute-done | bytes 278560 | tf_op jit(solution)/shard_map/ppermute | solution.py:331
  153.8 9.7 %collective-permute-done.27 = bf16[64,2048]{1,0:T(8,128)(2,1)S(1)} collective-permute-done((bf16[64,2048]{1,0:T(8,128)(2,1)S(1)}, bf16[64,2048]{1,0:T(8,128)(2,1)S(1)}, u32[]{:S(2)}, u32[]{:S(2)}) %collective-permute-start.27) | collective-permute-done | bytes 262176 | tf_op jit(solution)/shard_map/ppermute | solution.py:331
  163.5 0.3 multiply_convert_fusion.own_ref
  163.8 3.4 %collective-permute-start.28 = (bf16[64,2048]{1,0:T(8,128)(2,1)S(1)}, bf16[64,2048]{1,0:T(8,128)(2,1)S(1)}, u32[]{:S(2)}, u32[]{:S(2)}) collective-permute-start(bf16[64,2048]{1,0:T(8,128)(2,1)S(1)} %multiply_convert_fusion.own_ref), channel_id=1, source_target_pairs={{0,16},{2,18},{4,20},{6,22},{8,24},{10,26},{12,28},{14,30},{16,0},... | collective-permute-start | bytes 786440 | tf_op jit(solution)/shard_map/ppermute | solution.py:331
  167.2 13.6 %all-gather.8.cloned.1.call-done.refs_0_.refs_1_.refs_2_.refs_3_.refs_4_.refs_5_.refs_6_.refs_7_ = bf16[8192,384]{1,0:T(8,128)(2,1)} async-done(((bf16[1024,384]{1,0:T(8,128)(2,1)}), bf16[8192,384]{1,0:T(8,128)(2,1)}) %all-gather.8.cloned.1.call-update) | async-done | bytes 6291472 | tf_op jit(solution)/shard_map/all_gather | solution.py:347
  180.9 2.8 %copy-done = bf16[8192,384]{1,0:T(8,128)(2,1)S(1)} copy-done((bf16[8192,384]{1,0:T(8,128)(2,1)S(1)}, bf16[8192,384]{1,0:T(8,128)(2,1)}, u32[]{:S(2)}) %copy-start) | copy-done | bytes 6291480
  183.7 2.1 %shard_map.146 = bf16[128,1536]{1,0:T(8,128)(2,1)S(1)} custom-call(s32[1]{0:T(128)} %bitcast.5.place, bf16[64,2048]{1,0:T(8,128)(2,1)S(1)} %multiply_convert_fusion.own_ref, bf16[64,2048]{1,0:T(8,128)(2,1)S(1)} %collective-permute-done.28.got_ref, bf16[8192,384]{1,0:T(8,128)(2,1)S(1)} %copy-done, bf16[8192,384]{1,0:T(8,128)(2,1)S(1)} %copy-done, ...), custom_call_target="tpu_custom_call" | custom-call | tf_op jit(solution)/shard_map/pallas_call | solution.py:252
  185.8 1.5 collective-permute-start.29
  187.3 5.6 %collective-permute-done.29 = bf16[2,32,1536]{2,1,0:T(8,128)(2,1)S(1)} collective-permute-done((bf16[2,32,1536]{2,1,0:T(8,128)(2,1)S(1)}, bf16[2,32,1536]{2,1,0:T(8,128)(2,1)S(1)}, u32[]{:S(2)}, u32[]{:S(2)}) %collective-permute-start.29) | collective-permute-done | bytes 196640 | tf_op jit(solution)/shard_map/ppermute | solution.py:337
  193.0 2.5 %collective-permute-start.30 = (bf16[32,1536]{1,0:T(8,128)(2,1)S(1)}, bf16[32,1536]{1,0:T(8,128)(2,1)S(1)}, u32[]{:S(2)}, u32[]{:S(2)}) collective-permute-start(bf16[32,1536]{1,0:T(8,128)(2,1)S(1)} %get-tuple-element.58), channel_id=1, source_target_pairs={{0,16},{2,18},{4,20},{6,22},{8,24},{10,26},{12,28},{14,30},{16,0},... | collective-permute-start | bytes 294920 | tf_op jit(solution)/shard_map/ppermute | solution.py:331
  195.5 4.8 %collective-permute-done.30 = bf16[32,1536]{1,0:T(8,128)(2,1)S(1)} collective-permute-done((bf16[32,1536]{1,0:T(8,128)(2,1)S(1)}, bf16[32,1536]{1,0:T(8,128)(2,1)S(1)}, u32[]{:S(2)}, u32[]{:S(2)}) %collective-permute-start.30) | collective-permute-done | bytes 98336 | tf_op jit(solution)/shard_map/ppermute | solution.py:331
  200.2 0.7 maximum_select_fusion
  (87 shorter events, 2.1 us)
Async XLA Ops:
  7.2 5.9 %copy-start.16 = (bf16[32,3072]{1,0:T(8,128)(2,1)S(1)}, bf16[32,3072]{1,0:T(8,128)(2,1)}, u32[]{:S(2)}) copy-start(bf16[32,3072]{1,0:T(8,128)(2,1)} %param.12) | copy-start | bytes 589828
  7.2 10.0 %copy-start.15 = (bf16[192,768]{1,0:T(8,128)(2,1)S(1)}, bf16[192,768]{1,0:T(8,128)(2,1)}, u32[]{:S(2)}) copy-start(bf16[192,768]{1,0:T(8,128)(2,1)} %param.15) | copy-start | bytes 884740
  7.2 10.0 %copy-start.14 = (bf16[192,768]{1,0:T(8,128)(2,1)S(1)}, bf16[192,768]{1,0:T(8,128)(2,1)}, u32[]{:S(2)}) copy-start(bf16[192,768]{1,0:T(8,128)(2,1)} %param.14) | copy-start | bytes 884740
  7.2 36.5 %copy-start.6 = (s32[1,64]{1,0:T(1,128)S(1)}, s32[1,64]{1,0:T(1,128)}, u32[]{:S(2)}) copy-start(s32[1,64]{1,0:T(1,128)} %refs_6_.1) | copy-start | bytes 772
  7.2 36.5 %copy-start.17 = (f32[3072]{0:T(1024)S(1)}, f32[3072]{0:T(1024)}, u32[]{:S(2)}) copy-start(f32[3072]{0:T(1024)} %param.13) | copy-start | bytes 36868
  7.2 36.6 %copy-start.18 = (f32[3072]{0:T(1024)S(1)}, f32[3072]{0:T(1024)}, u32[]{:S(2)}) copy-start(f32[3072]{0:T(1024)} %param.18) | copy-start | bytes 36868
  7.2 124.4 %all-gather.4.cloned.1.call-start = ((), (), s32[]{:S(2)}) async-start(), calls=%async_computation | async-start | bytes 7077888 | tf_op jit(solution)/shard_map/all_gather | solution.py:347
  8.0 132.6 %all-gather.6.cloned.1.call-start = ((), (), s32[]{:S(2)}) async-start(), calls=%async_computation.1 | async-start | bytes 7077888 | tf_op jit(solution)/shard_map/all_gather | solution.py:347
  8.7 172.2 %all-gather.8.cloned.1.call-start = ((), (), s32[]{:S(2)}) async-start(), calls=%async_computation.2 | async-start | bytes 7077888 | tf_op jit(solution)/shard_map/all_gather | solution.py:347
  13.0 98.0 %copy-start.7 = (s32[1,64]{1,0:T(1,128)S(1)}, s32[1,64]{1,0:T(1,128)}, u32[]{:S(2)}) copy-start(s32[1,64]{1,0:T(1,128)} %refs_8_.1) | copy-start | bytes 772
  13.1 9.0 %collective-permute-start = (bf16[32,1536]{1,0:T(8,128)(2,1)S(1)}, bf16[32,1536]{1,0:T(8,128)(2,1)S(1)}, u32[]{:S(2)}, u32[]{:S(2)}) collective-permute-start(bf16[32,1536]{1,0:T(8,128)(2,1)S(1)} %get-tuple-element.59), channel_id=1, source_target_pairs={{0,16},{2,18},{4,20},{6,22},{8,24},{10,26},{12,28},{14,30},{16,0},... | collective-permute-start | bytes 294920 | tf_op jit(solution)/shard_map/ppermute | solution.py:331
  17.3 71.7 %copy-start.8 = (bf16[192,1152]{1,0:T(8,128)(2,1)}, bf16[192,1152]{1,0:T(8,128)(2,1)S(1)}, u32[]{:S(2)}) copy-start(bf16[192,1152]{1,0:T(8,128)(2,1)S(1)} %pad_maximum_fusion.1.refs_0_) | copy-start | bytes 1327108
  17.3 20.6 %collective-permute-start.3 = (bf16[192,1152]{1,0:T(8,128)(2,1)S(1)}, bf16[192,1152]{1,0:T(8,128)(2,1)S(1)}, u32[]{:S(2)}, u32[]{:S(2)}) collective-permute-start(bf16[192,1152]{1,0:T(8,128)(2,1)S(1)} %pad_maximum_fusion.1.refs_0_), channel_id=1, source_target_pairs={{0,4},{2,6},{4,0},{6,2},{8,12},{10,14},{12,8},{14,10},{16,20},{18,... | collective-permute-start | bytes 1327112 | tf_op jit(solution)/shard_map/ppermute | solution.py:331
  19.9 69.1 %copy-start.9 = (bf16[192,1152]{1,0:T(8,128)(2,1)}, bf16[192,1152]{1,0:T(8,128)(2,1)S(1)}, u32[]{:S(2)}) copy-start(bf16[192,1152]{1,0:T(8,128)(2,1)S(1)} %pad_maximum_fusion.2.refs_8_) | copy-start | bytes 1327108
  19.9 22.3 %collective-permute-start.12 = (bf16[192,1152]{1,0:T(8,128)(2,1)S(1)}, bf16[192,1152]{1,0:T(8,128)(2,1)S(1)}, u32[]{:S(2)}, u32[]{:S(2)}) collective-permute-start(bf16[192,1152]{1,0:T(8,128)(2,1)S(1)} %pad_maximum_fusion.2.refs_8_), channel_id=1, source_target_pairs={{0,8},{2,10},{4,12},{6,14},{8,0},{10,2},{12,4},{14,6},{16,24},{18,... | collective-permute-start | bytes 1327112 | tf_op jit(solution)/shard_map/ppermute | solution.py:331
  22.1 6.1 %collective-permute-start.1 = (bf16[2,32,1536]{2,1,0:T(8,128)(2,1)S(1)}, bf16[2,32,1536]{2,1,0:T(8,128)(2,1)S(1)}, u32[]{:S(2)}, u32[]{:S(2)}) collective-permute-start(bf16[2,32,1536]{2,1,0:T(8,128)(2,1)S(1)} %pad_maximum_fusion.4), channel_id=1, source_target_pairs={{0,1},{1,0},{2,3},{3,2},{4,5},{5,4},{6,7},{7,6},{8,9},{9,8},{10,11... | collective-permute-start | bytes 589832 | tf_op jit(solution)/shard_map/ppermute | solution.py:337
  23.8 32.2 %collective-permute-start.10 = (bf16[192,1152]{1,0:T(8,128)(2,1)S(1)}, bf16[192,1152]{1,0:T(8,128)(2,1)S(1)}, u32[]{:S(2)}, u32[]{:S(2)}) collective-permute-start(bf16[192,1152]{1,0:T(8,128)(2,1)S(1)} %pad_maximum_fusion.2.refs_8_), channel_id=1, source_target_pairs={{0,4},{2,6},{4,0},{6,2},{8,12},{10,14},{12,8},{14,10},{16,20},{18,... | collective-permute-start | bytes 1327112 | tf_op jit(solution)/shard_map/ppermute | solution.py:331
  25.3 35.9 %collective-permute-start.5 = (bf16[192,1152]{1,0:T(8,128)(2,1)S(1)}, bf16[192,1152]{1,0:T(8,128)(2,1)}, u32[]{:S(2)}, u32[]{:S(2)}) collective-permute-start(bf16[192,1152]{1,0:T(8,128)(2,1)S(1)} %pad_maximum_fusion.1.refs_0_), channel_id=1, source_target_pairs={{0,8},{2,10},{4,12},{6,14},{8,0},{10,2},{12,4},{14,6},{16,24},{18,... | collective-permute-start | bytes 1327112 | tf_op jit(solution)/shard_map/ppermute | solution.py:331
  28.3 33.0 %collective-permute-start.2 = (bf16[192,1152]{1,0:T(8,128)(2,1)S(1)}, bf16[192,1152]{1,0:T(8,128)(2,1)}, u32[]{:S(2)}, u32[]{:S(2)}) collective-permute-start(bf16[192,1152]{1,0:T(8,128)(2,1)S(1)} %pad_maximum_fusion.1.refs_0_), channel_id=1, source_target_pairs={{0,2},{2,0},{4,6},{6,4},{8,10},{10,8},{12,14},{14,12},{16,18},{18,... | collective-permute-start | bytes 1327112 | tf_op jit(solution)/shard_map/ppermute | solution.py:331
  37.9 40.2 %copy-start.10 = (bf16[192,1152]{1,0:T(8,128)(2,1)}, bf16[192,1152]{1,0:T(8,128)(2,1)S(1)}, u32[]{:S(2)}) copy-start(bf16[192,1152]{1,0:T(8,128)(2,1)S(1)} %collective-permute-done.3.refs_2_) | copy-start | bytes 1327108
  37.9 38.0 %collective-permute-start.9 = (bf16[192,1152]{1,0:T(8,128)(2,1)S(1)}, bf16[192,1152]{1,0:T(8,128)(2,1)}, u32[]{:S(2)}, u32[]{:S(2)}) collective-permute-start(bf16[192,1152]{1,0:T(8,128)(2,1)S(1)} %pad_maximum_fusion.2.refs_8_), channel_id=1, source_target_pairs={{0,2},{2,0},{4,6},{6,4},{8,10},{10,8},{12,14},{14,12},{16,18},{18,... | collective-permute-start | bytes 1327112 | tf_op jit(solution)/shard_map/ppermute | solution.py:331
  42.1 43.3 %copy-start.11 = (bf16[192,1152]{1,0:T(8,128)(2,1)}, bf16[192,1152]{1,0:T(8,128)(2,1)S(1)}, u32[]{:S(2)}) copy-start(bf16[192,1152]{1,0:T(8,128)(2,1)S(1)} %collective-permute-done.12.refs_12_) | copy-start | bytes 1327108
  42.1 33.8 %collective-permute-start.7 = (bf16[192,1152]{1,0:T(8,128)(2,1)S(1)}, bf16[192,1152]{1,0:T(8,128)(2,1)}, u32[]{:S(2)}, u32[]{:S(2)}) collective-permute-start(bf16[192,1152]{1,0:T(8,128)(2,1)S(1)} %collective-permute-done.3.refs_2_), channel_id=1, source_target_pairs={{0,8},{2,10},{4,12},{6,14},{8,0},{10,2},{12,4},{14,6},{16,24},{18,... | collective-permute-start | bytes 1327112 | tf_op jit(solution)/shard_map/ppermute | solution.py:331
  56.0 29.5 %copy-start.12 = (bf16[192,1152]{1,0:T(8,128)(2,1)}, bf16[192,1152]{1,0:T(8,128)(2,1)S(1)}, u32[]{:S(2)}) copy-start(bf16[192,1152]{1,0:T(8,128)(2,1)S(1)} %collective-permute-done.10.refs_10_) | copy-start | bytes 1327108
  56.0 21.3 %collective-permute-start.14 = (bf16[192,1152]{1,0:T(8,128)(2,1)S(1)}, bf16[192,1152]{1,0:T(8,128)(2,1)}, u32[]{:S(2)}, u32[]{:S(2)}) collective-permute-start(bf16[192,1152]{1,0:T(8,128)(2,1)S(1)} %collective-permute-done.12.refs_12_), channel_id=1, source_target_pairs={{0,4},{2,6},{4,0},{6,2},{8,12},{10,14},{12,8},{14,10},{16,20},{18,... | collective-permute-start | bytes 1327112 | tf_op jit(solution)/shard_map/ppermute | solution.py:331
  61.2 16.4 %collective-permute-start.13 = (bf16[192,1152]{1,0:T(8,128)(2,1)S(1)}, bf16[192,1152]{1,0:T(8,128)(2,1)}, u32[]{:S(2)}, u32[]{:S(2)}) collective-permute-start(bf16[192,1152]{1,0:T(8,128)(2,1)S(1)} %collective-permute-done.12.refs_12_), channel_id=1, source_target_pairs={{0,2},{2,0},{4,6},{6,4},{8,10},{10,8},{12,14},{14,12},{16,18},{18,... | collective-permute-start | bytes 1327112 | tf_op jit(solution)/shard_map/ppermute | solution.py:331
  61.2 16.7 %collective-permute-start.4 = (bf16[192,1152]{1,0:T(8,128)(2,1)S(1)}, bf16[192,1152]{1,0:T(8,128)(2,1)}, u32[]{:S(2)}, u32[]{:S(2)}) collective-permute-start(bf16[192,1152]{1,0:T(8,128)(2,1)S(1)} %collective-permute-done.3.refs_2_), channel_id=1, source_target_pairs={{0,2},{2,0},{4,6},{6,4},{8,10},{10,8},{12,14},{14,12},{16,18},{18,... | collective-permute-start | bytes 1327112 | tf_op jit(solution)/shard_map/ppermute | solution.py:331
  75.9 2.2 %collective-permute-start.11 = (bf16[192,1152]{1,0:T(8,128)(2,1)S(1)}, bf16[192,1152]{1,0:T(8,128)(2,1)S(1)}, u32[]{:S(2)}, u32[]{:S(2)}) collective-permute-start(bf16[192,1152]{1,0:T(8,128)(2,1)S(1)} %collective-permute-done.10.refs_10_), channel_id=1, source_target_pairs={{0,2},{2,0},{4,6},{6,4},{8,10},{10,8},{12,14},{14,12},{16,18},{18,... | collective-permute-start | bytes 1327112 | tf_op jit(solution)/shard_map/ppermute | solution.py:331
  75.9 9.5 %collective-permute-start.18 = (bf16[384,384]{1,0:T(8,128)(2,1)S(1)}, bf16[384,384]{1,0:T(8,128)(2,1)S(1)}, u32[]{:S(2)}, u32[]{:S(2)}) collective-permute-start(bf16[384,384]{1,0:T(8,128)(2,1)S(1)} %pad_maximum_fusion.3.refs_0_), channel_id=1, source_target_pairs={{0,8},{2,10},{4,12},{6,14},{8,0},{10,2},{12,4},{14,6},{16,24},{18,... | collective-permute-start | bytes 884744 | tf_op jit(solution)/shard_map/ppermute | solution.py:331
  77.3 11.7 %collective-permute-start.6 = (bf16[192,1152]{1,0:T(8,128)(2,1)}, bf16[192,1152]{1,0:T(8,128)(2,1)}, u32[]{:S(2)}, u32[]{:S(2)}) collective-permute-start(bf16[192,1152]{1,0:T(8,128)(2,1)} %collective-permute-done.5.refs_4_), channel_id=1, source_target_pairs={{0,2},{2,0},{4,6},{6,4},{8,10},{10,8},{12,14},{14,12},{16,18},{18,... | collective-permute-start | bytes 1327112 | tf_op jit(solution)/shard_map/ppermute | solution.py:331
  77.6 11.4 %collective-permute-start.8 = (bf16[192,1152]{1,0:T(8,128)(2,1)}, bf16[192,1152]{1,0:T(8,128)(2,1)}, u32[]{:S(2)}, u32[]{:S(2)}) collective-permute-start(bf16[192,1152]{1,0:T(8,128)(2,1)} %collective-permute-done.7.refs_6_), channel_id=1, source_target_pairs={{0,2},{2,0},{4,6},{6,4},{8,10},{10,8},{12,14},{14,12},{16,18},{18,... | collective-permute-start | bytes 1327112 | tf_op jit(solution)/shard_map/ppermute | solution.py:331
  77.9 11.1 %collective-permute-start.15 = (bf16[192,1152]{1,0:T(8,128)(2,1)}, bf16[192,1152]{1,0:T(8,128)(2,1)}, u32[]{:S(2)}, u32[]{:S(2)}) collective-permute-start(bf16[192,1152]{1,0:T(8,128)(2,1)} %collective-permute-done.14.refs_14_), channel_id=1, source_target_pairs={{0,2},{2,0},{4,6},{6,4},{8,10},{10,8},{12,14},{14,12},{16,18},{18,... | collective-permute-start | bytes 1327112 | tf_op jit(solution)/shard_map/ppermute | solution.py:331
  78.1 10.9 %copy-start.13 = (bf16[192,1152]{1,0:T(8,128)(2,1)}, bf16[192,1152]{1,0:T(8,128)(2,1)S(1)}, u32[]{:S(2)}) copy-start(bf16[192,1152]{1,0:T(8,128)(2,1)S(1)} %collective-permute-done.11.refs_11_) | copy-start | bytes 1327108
  78.1 18.4 %collective-permute-start.17 = (bf16[384,384]{1,0:T(8,128)(2,1)S(1)}, bf16[384,384]{1,0:T(8,128)(2,1)S(1)}, u32[]{:S(2)}, u32[]{:S(2)}) collective-permute-start(bf16[384,384]{1,0:T(8,128)(2,1)S(1)} %pad_maximum_fusion.3.refs_0_), channel_id=1, source_target_pairs={{0,4},{2,6},{4,0},{6,2},{8,12},{10,14},{12,8},{14,10},{16,20},{18,... | collective-permute-start | bytes 884744 | tf_op jit(solution)/shard_map/ppermute | solution.py:331
  85.4 15.0 %collective-permute-start.23 = (bf16[384,384]{1,0:T(8,128)(2,1)S(1)}, bf16[384,384]{1,0:T(8,128)(2,1)S(1)}, u32[]{:S(2)}, u32[]{:S(2)}) collective-permute-start(bf16[384,384]{1,0:T(8,128)(2,1)S(1)} %collective-permute-done.18.refs_4_), channel_id=1, source_target_pairs={{0,4},{2,6},{4,0},{6,2},{8,12},{10,14},{12,8},{14,10},{16,20},{18,... | collective-permute-start | bytes 884744 | tf_op jit(solution)/shard_map/ppermute | solution.py:331
  87.6 0.8 copy-start.4
  88.4 0.6 copy-start.5
  95.0 15.9 %collective-permute-start.16 = (bf16[64,2432]{1,0:T(8,128)(2,1)}, bf16[64,2432]{1,0:T(8,128)(2,1)S(1)}, u32[]{:S(2)}, u32[]{:S(2)}) collective-permute-start(bf16[64,2432]{1,0:T(8,128)(2,1)} %get-tuple-element.33), channel_id=1, source_target_pairs={{0,16},{2,18},{4,20},{6,22},{8,24},{10,26},{12,28},{14,30},{16,0},... | collective-permute-start | bytes 933896 | tf_op jit(solution)/shard_map/ppermute | solution.py:331
  96.5 19.8 %collective-permute-start.20 = (bf16[384,384]{1,0:T(8,128)(2,1)S(1)}, bf16[384,384]{1,0:T(8,128)(2,1)S(1)}, u32[]{:S(2)}, u32[]{:S(2)}) collective-permute-start(bf16[384,384]{1,0:T(8,128)(2,1)S(1)} %pad_maximum_fusion.3.refs_0_), channel_id=1, source_target_pairs={{0,2},{2,0},{4,6},{6,4},{8,10},{10,8},{12,14},{14,12},{16,18},{18,... | collective-permute-start | bytes 884744 | tf_op jit(solution)/shard_map/ppermute | solution.py:331
  96.5 19.8 %collective-permute-start.21 = (bf16[384,384]{1,0:T(8,128)(2,1)S(1)}, bf16[384,384]{1,0:T(8,128)(2,1)S(1)}, u32[]{:S(2)}, u32[]{:S(2)}) collective-permute-start(bf16[384,384]{1,0:T(8,128)(2,1)S(1)} %collective-permute-done.17.refs_2_), channel_id=1, source_target_pairs={{0,2},{2,0},{4,6},{6,4},{8,10},{10,8},{12,14},{14,12},{16,18},{18,... | collective-permute-start | bytes 884744 | tf_op jit(solution)/shard_map/ppermute | solution.py:331
  97.0 19.3 %collective-permute-start.22 = (bf16[384,384]{1,0:T(8,128)(2,1)S(1)}, bf16[384,384]{1,0:T(8,128)(2,1)S(1)}, u32[]{:S(2)}, u32[]{:S(2)}) collective-permute-start(bf16[384,384]{1,0:T(8,128)(2,1)S(1)} %collective-permute-done.18.refs_4_), channel_id=1, source_target_pairs={{0,2},{2,0},{4,6},{6,4},{8,10},{10,8},{12,14},{14,12},{16,18},{18,... | collective-permute-start | bytes 884744 | tf_op jit(solution)/shard_map/ppermute | solution.py:331
  100.4 20.1 %collective-permute-start.24 = (bf16[384,384]{1,0:T(8,128)(2,1)S(1)}, bf16[384,384]{1,0:T(8,128)(2,1)}, u32[]{:S(2)}, u32[]{:S(2)}) collective-permute-start(bf16[384,384]{1,0:T(8,128)(2,1)S(1)} %collective-permute-done.23.refs_6_), channel_id=1, source_target_pairs={{0,2},{2,0},{4,6},{6,4},{8,10},{10,8},{12,14},{14,12},{16,18},{18,... | collective-permute-start | bytes 884744 | tf_op jit(solution)/shard_map/ppermute | solution.py:331
  110.9 1.1 copy-start.3
  113.6 6.8 %collective-permute-start.19 = (bf16[64,768]{1,0:T(8,128)(2,1)S(1)}, bf16[64,768]{1,0:T(8,128)(2,1)S(1)}, u32[]{:S(2)}, u32[]{:S(2)}) collective-permute-start(bf16[64,768]{1,0:T(8,128)(2,1)S(1)} %get-tuple-element.38.own_ref), channel_id=1, source_target_pairs={{0,16},{2,18},{4,20},{6,22},{8,24},{10,26},{12,28},{14,30},{16,0},... | collective-permute-start | bytes 294920 | tf_op jit(solution)/shard_map/ppermute | solution.py:331
  122.6 8.7 %collective-permute-start.25 = (bf16[128,1536]{1,0:T(8,128)(2,1)S(1)}, bf16[128,1536]{1,0:T(8,128)(2,1)S(1)}, u32[]{:S(2)}, u32[]{:S(2)}) collective-permute-start(bf16[128,1536]{1,0:T(8,128)(2,1)S(1)} %shard_map.142.terms_ref), channel_id=1, source_target_pairs={{0,1},{1,0},{2,3},{3,2},{4,5},{5,4},{6,7},{7,6},{8,9},{9,8},{10,11... | collective-permute-start | bytes 1179656 | tf_op jit(solution)/shard_map/ppermute | solution.py:337
  131.7 3.3 %copy-start.2 = (bf16[1536,2048]{1,0:T(8,128)(2,1)S(1)}, bf16[1536,2048]{1,0:T(8,128)(2,1)}, u32[]{:S(2)}) copy-start(bf16[1536,2048]{1,0:T(8,128)(2,1)} %all-gather.4.cloned.1.call-done.w_ref) | copy-start | bytes 18874372
  137.0 16.6 %collective-permute-start.26 = (bf16[64,2176]{1,0:T(8,128)(2,1)S(1)}, bf16[64,2176]{1,0:T(8,128)(2,1)S(1)}, u32[]{:S(2)}, u32[]{:S(2)}) collective-permute-start(bf16[64,2176]{1,0:T(8,128)(2,1)S(1)} %get-tuple-element.43), channel_id=1, source_target_pairs={{0,16},{2,18},{4,20},{6,22},{8,24},{10,26},{12,28},{14,30},{16,0},... | collective-permute-start | bytes 835592 | tf_op jit(solution)/shard_map/ppermute | solution.py:331
  140.6 2.8 %copy-start.1 = (bf16[1536,2048]{1,0:T(8,128)(2,1)S(1)}, bf16[1536,2048]{1,0:T(8,128)(2,1)}, u32[]{:S(2)}) copy-start(bf16[1536,2048]{1,0:T(8,128)(2,1)} %all-gather.6.cloned.1.call-done.w_ref) | copy-start | bytes 18874372
  145.5 18.0 %collective-permute-start.27 = (bf16[64,2048]{1,0:T(8,128)(2,1)S(1)}, bf16[64,2048]{1,0:T(8,128)(2,1)S(1)}, u32[]{:S(2)}, u32[]{:S(2)}) collective-permute-start(bf16[64,2048]{1,0:T(8,128)(2,1)S(1)} %get-tuple-element.47), channel_id=1, source_target_pairs={{0,16},{2,18},{4,20},{6,22},{8,24},{10,26},{12,28},{14,30},{16,0},... | collective-permute-start | bytes 786440 | tf_op jit(solution)/shard_map/ppermute | solution.py:331
  163.8 17.1 %collective-permute-start.28 = (bf16[64,2048]{1,0:T(8,128)(2,1)S(1)}, bf16[64,2048]{1,0:T(8,128)(2,1)S(1)}, u32[]{:S(2)}, u32[]{:S(2)}) collective-permute-start(bf16[64,2048]{1,0:T(8,128)(2,1)S(1)} %multiply_convert_fusion.own_ref), channel_id=1, source_target_pairs={{0,16},{2,18},{4,20},{6,22},{8,24},{10,26},{12,28},{14,30},{16,0},... | collective-permute-start | bytes 786440 | tf_op jit(solution)/shard_map/ppermute | solution.py:331
  180.9 2.8 %copy-start = (bf16[8192,384]{1,0:T(8,128)(2,1)S(1)}, bf16[8192,384]{1,0:T(8,128)(2,1)}, u32[]{:S(2)}) copy-start(bf16[8192,384]{1,0:T(8,128)(2,1)} %all-gather.8.cloned.1.call-done.refs_0_.refs_1_.refs_2_.refs_3_.refs_4_.refs_5_.refs_6_.refs_7_) | copy-start | bytes 18874372
  185.8 7.1 %collective-permute-start.29 = (bf16[2,32,1536]{2,1,0:T(8,128)(2,1)S(1)}, bf16[2,32,1536]{2,1,0:T(8,128)(2,1)S(1)}, u32[]{:S(2)}, u32[]{:S(2)}) collective-permute-start(bf16[2,32,1536]{2,1,0:T(8,128)(2,1)S(1)} %dynamic-slice_bitcast_fusion), channel_id=1, source_target_pairs={{0,1},{1,0},{2,3},{3,2},{4,5},{5,4},{6,7},{7,6},{8,9},{9,8},{10,11... | collective-permute-start | bytes 589832 | tf_op jit(solution)/shard_map/ppermute | solution.py:337
  193.0 7.2 %collective-permute-start.30 = (bf16[32,1536]{1,0:T(8,128)(2,1)S(1)}, bf16[32,1536]{1,0:T(8,128)(2,1)S(1)}, u32[]{:S(2)}, u32[]{:S(2)}) collective-permute-start(bf16[32,1536]{1,0:T(8,128)(2,1)S(1)} %get-tuple-element.58), channel_id=1, source_target_pairs={{0,16},{2,18},{4,20},{6,22},{8,24},{10,26},{12,28},{14,30},{16,0},... | collective-permute-start | bytes 294920 | tf_op jit(solution)/shard_map/ppermute | solution.py:331
Sparse Core Ops, SparseCore 0:
  9.7 65.7 all-gather.3
  77.1 46.7 all-gather.5
  125.6 55.2 all-gather.7

commit v3 on v2

v3 whole, which is shorter than its diff:
```python
import functools

import jax
import jax.numpy as jnp
from jax import lax
from jax.experimental import pallas as pl
from jax.experimental.pallas import tpu as pltpu
from jax.sharding import PartitionSpec as P

HEAD_DIM = 96
EPS = 1e-05
OCT = 8
QUAD = 4
BF = jnp.bfloat16
F32 = jnp.float32
VMEM = 24 * 1024 * 1024
VMEM_ALL = 60 * 1024 * 1024


def norm_rows(rows, gain):
    values = rows.astype(F32)
    scale = lax.rsqrt(jnp.mean(values * values, axis=-1, keepdims=True) + EPS)
    return (values * scale * gain).astype(BF)


def positions(segment):
    count = segment.shape[0]
    index = jnp.arange(count, dtype=jnp.int32)
    before = jnp.concatenate([jnp.full((1,), -1, jnp.int32), segment[:-1]])
    starts = jnp.where(segment != before, index, jnp.zeros_like(index))
    return index - lax.cummax(starts, axis=0)


def rotate(heads, place):
    half = heads.shape[-1] // 2
    freq = 10000.0 ** (-2.0 * jnp.arange(half, dtype=F32) / heads.shape[-1])
    angle = place.astype(F32)[:, None] * freq[None, :]
    cosine = jnp.cos(angle)[:, None, :]
    sine = jnp.sin(angle)[:, None, :]
    first = heads[..., :half]
    second = heads[..., half:]
    return jnp.concatenate(
        [first * cosine - second * sine, second * cosine + first * sine], axis=-1
    )


def dot(a, b):
    return jnp.dot(a, b, preferred_element_type=F32)


def attention(query, key, v_b, segment, slots):
    count, width = v_b.shape
    heads_here = width // HEAD_DIM
    index = jnp.arange(count, dtype=jnp.int32)
    place = positions(segment)
    q_rot = rotate(query.reshape(count, heads_here, HEAD_DIM), place).astype(BF)
    k_rot = rotate(key.reshape(count, heads_here, HEAD_DIM), place).astype(BF)
    k_flat = k_rot.reshape(count, width)
    cache_keys = jnp.zeros_like(k_flat).at[slots].set(k_flat)
    cache_values = jnp.zeros_like(v_b).at[slots].set(v_b)
    allowed = (segment[:, None] == segment[None, :]) & (index[None, :] <= index[:, None])
    scores = jnp.einsum("qhd,khd->hqk", q_rot, k_rot, preferred_element_type=F32)
    scores = scores * (1.0 / HEAD_DIM**0.5)
    scores = jnp.where(allowed[None, :, :], scores, -1e30)
    top = jnp.max(scores, axis=-1, keepdims=True)
    expo = jnp.exp(scores - top)
    probs = (expo / jnp.sum(expo, axis=-1, keepdims=True)).astype(BF)
    v_heads = v_b.reshape(count, heads_here, HEAD_DIM)
    attended = jnp.einsum("hqk,khd->qhd", probs, v_heads, preferred_element_type=F32)
    return attended.astype(BF).reshape(count, width), cache_keys, cache_values


def gathered_plan(
    tokens, attn_gain, w_query, w_key, w_value, w_out, mlp_gain, w_gate, w_up, w_down, segment_ids, cache_slot,
):
    whole = lax.all_gather(norm_rows(tokens, attn_gain), "head", axis=0, tiled=True)
    query, key, value = (
        dot(whole, lax.all_gather(w, "group", axis=0, tiled=True)) for w in (w_query, w_key, w_value)
    )
    attended, cache_keys, cache_values = attention(
        query, key, value.astype(BF), segment_ids[0], cache_slot[0]
    )
    out_terms = dot(attended, lax.all_gather(w_out, "group", axis=1, tiled=True))
    attn_rows = lax.psum_scatter(out_terms.astype(BF), "head", scatter_dimension=0, tiled=True)
    middle = (tokens.astype(F32) + attn_rows.astype(F32)).astype(BF)
    mlp_in = lax.all_gather(norm_rows(middle, mlp_gain), "head", axis=0, tiled=True)
    gate, up = (dot(mlp_in, lax.all_gather(w, "group", axis=0, tiled=True)) for w in (w_gate, w_up))
    hidden = (jax.nn.silu(gate) * up).astype(BF)
    down_terms = dot(hidden, lax.all_gather(w_down, "group", axis=1, tiled=True))
    mlp_rows = lax.psum_scatter(down_terms.astype(BF), "head", scatter_dimension=0, tiled=True)
    layer_out = (middle.astype(F32) + mlp_rows.astype(F32)).astype(BF)
    return (layer_out, cache_keys, cache_values)


def prepared(x, keep, gain_ref, lhs_ref, coded_ref, squares_ref):
    rows, depth = x.shape
    cuts = lhs_ref.shape[0]
    wide = depth // cuts
    squares = jnp.broadcast_to(jnp.sum(x * x, axis=1, keepdims=True), (rows, 128))
    scaled = (x * gain_ref[...]).astype(BF)
    for i in range(cuts):
        lhs_ref[i] = scaled[:, i * wide : (i + 1) * wide]
    high = squares.astype(BF).astype(F32)
    lane = lax.broadcasted_iota(jnp.int32, (rows, 128), 1)
    coded_ref[...] = jnp.where(lane < 64, high, squares - high)[keep:].astype(BF)
    squares_ref[...] = squares[:keep]


def arranged(row, rows_ref, mine_ref, others_ref):
    groups, mine, _ = mine_ref.shape
    for g in range(groups):
        rows_ref[pl.ds(pl.multiple_of(2 * mine * g + row[0] * mine, mine), mine)] = mine_ref[g]
        rows_ref[pl.ds(pl.multiple_of(2 * mine * g + (1 - row[0]) * mine, mine), mine)] = others_ref[g]


def first_kernel(row, mine_ref, others_ref, gain_ref, rows_ref, lhs_ref, coded_ref, squares_ref):
    arranged(row, rows_ref, mine_ref, others_ref)
    prepared(rows_ref[...].astype(F32), squares_ref.shape[0], gain_ref, lhs_ref, coded_ref, squares_ref)


def middle_kernel(row, mine_ref, others_ref, a_ref, b_ref, gain_ref, middle_ref, lhs_ref, coded_ref, squares_ref):
    arranged(row, middle_ref, mine_ref, others_ref)
    total = a_ref[...].astype(F32) + b_ref[...].astype(F32)
    middle_ref[...] = (middle_ref[...].astype(F32) + total).astype(BF)
    prepared(middle_ref[...].astype(F32), squares_ref.shape[0], gain_ref, lhs_ref, coded_ref, squares_ref)


def prepare(kernel, row, operands, rows, depth, keep, cuts):
    shapes = [
        jax.ShapeDtypeStruct((rows, depth), BF),
        jax.ShapeDtypeStruct((cuts, rows, depth // cuts), BF),
        jax.ShapeDtypeStruct((rows - keep, 128), BF),
        jax.ShapeDtypeStruct((keep, 128), F32),
    ]
    def spec(x):
        return pl.BlockSpec(x.shape, lambda j, p: (0,) * len(x.shape))
    return pl.pallas_call(
        kernel,
        grid_spec=pltpu.PrefetchScalarGridSpec(
            num_scalar_prefetch=1,
            grid=(1,),
            in_specs=[spec(x) for x in operands],
            out_specs=[spec(x) for x in shapes],
        ),
        out_shape=shapes,
        compiler_params=pltpu.CompilerParams(vmem_limit_bytes=VMEM),
    )(row, *operands)


def rows_kernel(place, lhs, coded_ref, *refs):
    weights, (sent_ref, own_ref, held, sems) = refs[:-4], refs[-4:]
    block = held.shape[-1]
    keep, width = own_ref.shape
    parts = len(weights) // OCT
    steps = width // parts // block

    def copies(step):
        return [
            pltpu.make_async_copy(
                w.at[:, step * block : (step + 1) * block], held.at[step % 2, n], sems.at[step % 2, n]
            )
            for n, w in enumerate(weights)
        ]

    pending = copies(0)
    for c in pending:
        c.start()
    if sent_ref.shape[1] > width:
        sent_ref[:, width:] = coded_ref[...]
    for step in range(steps):
        following = copies(step + 1) if step + 1 < steps else []
        for c in following:
            c.start()
        for i in range(parts):
            total = None
            for k in range(OCT):
                pending[OCT * i + k].wait()
                term = dot(lhs[place[0] ^ k], held[step % 2, OCT * i + k])
                total = term if total is None else total + term
            at = i * (width // parts) + step * block
            own_ref[:, at : at + block] = total[:keep]
            sent_ref[:, at : at + block] = total[keep:].astype(BF)
        pending = following


def in_hbm(pieces):
    return [pl.BlockSpec(memory_space=pltpu.HBM)] * len(pieces)


def rows_product(place, lhs, coded, pieces, each, block, with_squares):
    _, rows, wide = lhs.shape
    keep = rows // 2
    count = len(pieces)
    width = count // OCT * each
    sent = width + (128 if with_squares else 0)
    whole = lambda j, p: (0, 0)
    return pl.pallas_call(
        rows_kernel,
        grid_spec=pltpu.PrefetchScalarGridSpec(
            num_scalar_prefetch=1,
            grid=(1,),
            in_specs=[pl.BlockSpec(lhs.shape, lambda j, p: (0, 0, 0)), pl.BlockSpec(coded.shape, whole)]
            + in_hbm(pieces),
            out_specs=[pl.BlockSpec((keep, sent), whole), pl.BlockSpec((keep, width), whole)],
            scratch_shapes=[pltpu.VMEM((2, count, wide, block), BF), pltpu.SemaphoreType.DMA((2, count))],
        ),
        out_shape=[jax.ShapeDtypeStruct((keep, sent), BF), jax.ShapeDtypeStruct((keep, width), F32)],
        compiler_params=pltpu.CompilerParams(vmem_limit_bytes=VMEM),
    )(place, lhs, coded, *pieces)


def first_rows_kernel(place, lhs, coded_ref, *refs):
    weights, sent_refs, own_ref = refs[:12], refs[12:15], refs[15]
    step = pl.program_id(0)
    block = weights[0].shape[-1]
    keep, width = own_ref.shape

    @pl.when(step == 0)
    def _():
        for g, sent_ref in enumerate(sent_refs):
            sent_ref[:, width:] = coded_ref[g * keep : (g + 1) * keep]

    for i in range(3):
        total = None
        for k in range(4):
            term = dot(lhs[place[0] ^ k], weights[4 * i + k][...])
            total = term if total is None else total + term
        columns = pl.ds(pl.multiple_of(i * (width // 3) + step * block, 128), block)
        own_ref[:, columns] = total[:keep]
        for g, sent_ref in enumerate(sent_refs):
            sent_ref[:, columns] = total[(g + 1) * keep : (g + 2) * keep].astype(BF)


def first_rows_product(place, lhs, coded, pieces, block):
    _, rows, wide = lhs.shape
    keep = rows // 4
    each = pieces[0].shape[1]
    width = 3 * each
    whole = lambda j, p: (0, 0)
    sent = jax.ShapeDtypeStruct((keep, width + 128), BF)
    return pl.pallas_call(
        first_rows_kernel,
        grid_spec=pltpu.PrefetchScalarGridSpec(
            num_scalar_prefetch=1,
            grid=(each // block,),
            in_specs=[pl.BlockSpec(lhs.shape, lambda j, p: (0, 0, 0)), pl.BlockSpec(coded.shape, whole)]
            + [pl.BlockSpec((wide, block), lambda j, p: (0, j))] * len(pieces),
            out_specs=[pl.BlockSpec(sent.shape, whole)] * 3 + [pl.BlockSpec((keep, width), whole)],
        ),
        out_shape=[sent] * 3 + [jax.ShapeDtypeStruct((keep, width), F32)],
        compiler_params=pltpu.CompilerParams(vmem_limit_bytes=VMEM_ALL),
    )(place, lhs, coded, *pieces)


def columns_kernel(place, own_ref, got_ref, *refs):
    weights, (out_ref, parts, a_ref, held, sems) = refs[:OCT], refs[OCT:]
    keep, depth = own_ref.shape
    wide = held.shape[2] // 2
    copies = [pltpu.make_async_copy(w, held.at[n], sems.at[n]) for n, w in enumerate(weights)]
    for c in copies:
        c.start()
    a_ref[:keep] = own_ref[...]
    a_ref[keep:] = got_ref[...]
    for k in range(OCT):
        copies[k].wait()
        lower = dot(a_ref[:, : depth // 2], held[k])
        upper = dot(a_ref[:, depth // 2 :], held[k])
        parts[place[0] ^ k] = (lower[:, :wide] + upper[:, wide:]).astype(BF)
    for i in range(OCT):
        out_ref[:, i * wide : (i + 1) * wide] = parts[i]


def columns_product(place, own, got, pieces):
    keep, depth = own.shape
    rows = 2 * keep
    deep, double = pieces[0].shape
    wide = double // 2
    whole = lambda j, p: (0, 0)
    return pl.pallas_call(
        columns_kernel,
        grid_spec=pltpu.PrefetchScalarGridSpec(
            num_scalar_prefetch=1,
            grid=(1,),
            in_specs=[pl.BlockSpec((keep, depth), whole)] * 2 + in_hbm(pieces),
            out_specs=pl.BlockSpec((rows, OCT * wide), whole),
            scratch_shapes=[
                pltpu.VMEM((OCT, rows, wide), BF),
                pltpu.VMEM((rows, depth), BF),
                pltpu.VMEM((OCT, deep, double), BF),
                pltpu.SemaphoreType.DMA((OCT,)),
            ],
        ),
        out_shape=jax.ShapeDtypeStruct((rows, OCT * wide), BF),
        compiler_params=pltpu.CompilerParams(vmem_limit_bytes=VMEM),
    )(place, own, got, *pieces)


def out_kernel(place, own_ref, got_ref, *refs):
    weights, (out_ref, parts, a_ref) = refs[:OCT], refs[OCT:]
    keep, depth = own_ref.shape
    a_ref[:keep] = own_ref[...]
    a_ref[keep:] = got_ref[...]
    wide = weights[0].shape[-1] // 2
    for k in range(OCT):
        lower = dot(a_ref[:, : depth // 2], weights[k][...])
        upper = dot(a_ref[:, depth // 2 :], weights[k][...])
        parts[place[0] ^ k] = (lower[:, :wide] + upper[:, wide:]).astype(BF)
    for i in range(OCT):
        out_ref[:, i * wide : (i + 1) * wide] = parts[i]


def out_product(place, own, got, pieces):
    keep, depth = own.shape
    rows = 2 * keep
    deep, double = pieces[0].shape
    wide = double // 2
    whole = lambda j, p: (0, 0)
    return pl.pallas_call(
        out_kernel,
        grid_spec=pltpu.PrefetchScalarGridSpec(
            num_scalar_prefetch=1,
            grid=(1,),
            in_specs=[pl.BlockSpec((keep, depth), whole)] * 2 + [pl.BlockSpec((deep, double), whole)] * OCT,
            out_specs=pl.BlockSpec((rows, OCT * wide), whole),
            scratch_shapes=[pltpu.VMEM((OCT, rows, wide), BF), pltpu.VMEM((rows, depth), BF)],
        ),
        out_shape=jax.ShapeDtypeStruct((rows, OCT * wide), BF),
        compiler_params=pltpu.CompilerParams(vmem_limit_bytes=VMEM_ALL),
    )(place, own, got, *pieces)


def attention_kernel(model, *refs):
    own, *got = refs[:4]
    squares, cosine, left, right, seg_row, seg_col, slot, out_ref, keys_ref, values_ref = refs[4:]
    count, width = out_ref.shape
    heads_here = width // HEAD_DIM
    total = squares[:, :1]
    for g in got:
        last = g[:, 3 * width :].astype(F32)
        total = total + last[:, :1] + last[:, 64:65]
    scale = lax.rsqrt(total / model + EPS)

    def part(i):
        columns = slice(i * width, (i + 1) * width)
        x = own[:, columns]
        for g in got:
            x = x + g[:, columns].astype(F32)
        return x * scale

    query, key, value = part(0), part(1), part(2)

    def rotated(x):
        ahead = pltpu.roll(x, width - HEAD_DIM // 2, 1)
        behind = pltpu.roll(x, HEAD_DIM // 2, 1)
        return (x * cosine[...] + ahead * left[...] + behind * right[...]).astype(BF)

    q_rot, k_rot, v_b = rotated(query), rotated(key), value.astype(BF)
    spot = lax.broadcasted_iota(jnp.int32, (count, count), 0)
    hot = jnp.where(spot == slot[...], 1.0, 0.0).astype(BF)
    keys_ref[...] = dot(hot, k_rot).astype(BF)
    values_ref[...] = dot(hot, v_b).astype(BF)
    lane = lax.broadcasted_iota(jnp.int32, (count, width), 1)
    within = [(lane >= h * HEAD_DIM) & (lane < (h + 1) * HEAD_DIM) for h in range(heads_here)]
    zero = jnp.zeros((count, width), BF)
    spread_q = jnp.concatenate([jnp.where(w, q_rot, zero) for w in within], axis=0)
    scores = lax.dot_general(spread_q, k_rot, (((1,), (1,)), ((), ())), preferred_element_type=F32)
    scores = (scores * (1.0 / HEAD_DIM**0.5)).reshape(heads_here, count, count)
    other = lax.broadcasted_iota(jnp.int32, (count, count), 1)
    allowed = (seg_col[...] == seg_row[...]) & (other <= spot)
    scores = jnp.where(allowed[None], scores, -1e30)
    expo = jnp.exp(scores - jnp.max(scores, axis=-1, keepdims=True))
    probs = (expo / jnp.sum(expo, axis=-1, keepdims=True)).astype(BF)
    mixed = dot(probs.reshape(heads_here * count, count), v_b)
    total = jnp.zeros((count, width), F32)
    for h in range(heads_here):
        total = total + jnp.where(within[h], mixed[h * count : (h + 1) * count], 0.0)
    out_ref[...] = total.astype(BF)


def attend(model, own, got, squares, tables, segment, slots):
    count, width = own.shape[0], own.shape[1] // 3
    out = jax.ShapeDtypeStruct((count, width), BF)
    return pl.pallas_call(
        functools.partial(attention_kernel, model),
        out_shape=[out, out, out],
        compiler_params=pltpu.CompilerParams(vmem_limit_bytes=VMEM_ALL),
    )(own, *got, squares, *tables, segment.reshape(1, count), segment.reshape(count, 1), slots.reshape(1, count))


def rotation_tables(segment, width):
    half = HEAD_DIM // 2
    lane = jnp.arange(width, dtype=jnp.int32)
    freq = 10000.0 ** (-2.0 * (lane % half).astype(F32) / HEAD_DIM)
    angle = positions(segment).astype(F32)[:, None] * freq[None, :]
    first = ((lane % HEAD_DIM) < half)[None, :]
    sine = jnp.sin(angle)
    return jnp.cos(angle), jnp.where(first, -sine, 0.0), jnp.where(first, 0.0, sine)


def after(x, *others):
    return lax.optimization_barrier((x,) + others)[0]


def octet_plan(n_group):
    def swap(bit):
        pairs = [(g, g ^ bit) for g in range(n_group)]
        return lambda x: lax.ppermute(x, "group", pairs)

    core, near, next_to, across = swap(1), swap(2), swap(4), swap(OCT)

    def other_head(x):
        return lax.ppermute(x, "head", [(0, 1), (1, 0)])

    def beside(w):
        depth = w.shape[0]
        return jnp.concatenate([w[: depth // 2], w[depth // 2 :]], axis=1)

    def all_pieces(own, x, z, diagonal, early=(), late=()):
        return [
            own, core(after(own, *early)), x, core(after(x, *early)), z, core(after(z, *early)),
            diagonal, core(after(diagonal, *late)),
        ]

    def turn(k):
        pairs = [(g, (g + k * QUAD) % n_group) for g in range(n_group)]
        return lambda x: lax.ppermute(x, "group", pairs)

    turns = [turn(k) for k in range(4)]

    def per_device(
        tokens, attn_gain, w_query, w_key, w_value, w_out, mlp_gain, w_gate, w_up, w_down, segment_ids, cache_slot,
    ):
        group = lax.axis_index("group")
        side, fourth = group // OCT, group // QUAD
        place = (group % OCT).astype(jnp.int32).reshape(1)
        place4 = (group % QUAD).astype(jnp.int32).reshape(1)
        row = lax.axis_index("head")
        at_row = row.astype(jnp.int32).reshape(1)
        mine, model = tokens.shape
        half, quarter = model // 2, model // 4
        units = w_gate.shape[1]
        width = w_query.shape[1]
        tables = rotation_tables(segment_ids[0], width)
        gain1 = lax.dynamic_slice(attn_gain, (fourth * quarter,), (quarter,)).reshape(1, quarter)
        gain2 = lax.dynamic_slice(mlp_gain, (side * half,), (half,)).reshape(1, half)

        def columns_of(place, wide):
            return lax.dynamic_slice(tokens, (0, place * wide), (mine, wide))

        cut = [columns_of((fourth + k) % 4, quarter) for k in range(4)]
        given = columns_of(1 - side, half)
        cut = lax.optimization_barrier((*cut, given))
        came = [turns[k](cut[k]) for k in (3, 2, 1)]
        x_q, x_k, x_v = near(w_query), near(w_key), near(w_value)
        o_own, d_own = lax.optimization_barrier((beside(w_out), beside(w_down)))
        x_o = near(o_own)
        both = jnp.stack([cut[0], *came])
        gate, down, z_own, given = lax.optimization_barrier((w_gate, d_own, o_own, cut[4], both))[:4]
        partner = across(given)
        z_o, z_g, z_d = next_to(z_own), next_to(gate), next_to(down)
        mine_too = jnp.stack([columns_of(side, half), partner])
        others_too = other_head(mine_too)
        others = other_head(after(both, x_q, gain1, gain2, *tables, z_g, others_too))
        _, lhs, coded, squares = prepare(
            first_kernel, at_row, (both, others, gain1), 8 * mine, quarter, 2 * mine, QUAD
        )
        x_gate, x_up, x_down = lax.optimization_barrier((w_gate, w_up, d_own, x_q, x_k, x_v, x_o, both))[:3]
        x_g, x_u, x_d = near(x_gate), near(x_up), near(x_down)
        pieces = [p for w, x in ((w_query, x_q), (w_key, x_k), (w_value, x_v)) for p in (w, core(w), x, core(x))]
        *sent, own = first_rows_product(place4, after(lhs, partner), coded, pieces, 384)
        *sent, _ = lax.optimization_barrier((*sent, z_o, z_d))[:4]
        got = [turns[k + 1](sent[k]) for k in range(3)]
        d_o = near(after(z_o, sent[0]))
        got = lax.optimization_barrier((*got, d_o, x_g, x_u, x_d))[:3]
        p_o = all_pieces(o_own, x_o, z_o, d_o, (sent[0],), (sent[0],))
        attended, cache_keys, cache_values = attend(model, own, got, squares, tables, segment_ids[0], cache_slot[0])
        d_g = near(after(z_g, attended))
        got = across(attended)
        z_u = next_to(after(w_up, got))
        terms = out_product(place, attended, got, p_o)
        others = other_head(terms)
        p_g = all_pieces(w_gate, x_g, z_g, d_g, (attended,), (others,))
        middle, lhs, coded, squares = prepare(
            middle_kernel, at_row, (mine_too, others_too, terms, after(others, z_u, d_g), gain2), 4 * mine, half, 2 * mine, OCT
        )
        d_u = near(after(z_u, lhs))
        sent_g, own_g = rows_product(place, lhs, coded, p_g, units, 512, True)
        got_g = across(sent_g)
        p_u = all_pieces(w_up, x_u, z_u, d_u, (lhs,), (got_g,))
        sent_u, own_u = rows_product(place, after(lhs, sent_g), coded, p_u, units, 512, False)
        got_u = across(sent_u)
        d_d = near(after(z_d, sent_g))
        p_d = all_pieces(d_own, x_d, z_d, d_d, (sent_u,), (got_u,))
        last = got_g[:, units:].astype(F32)
        scale = lax.rsqrt((squares[:, :1] + last[:, :1] + last[:, 64:65]) / model + EPS)
        gate = (own_g + got_g[:, :units].astype(F32)) * scale
        up = (own_u + got_u.astype(F32)) * scale
        hidden = (jax.nn.silu(gate) * up).astype(BF)
        terms = columns_product(place, hidden, across(hidden), p_d).reshape(2, 2, mine, half)
        given = other_head(lax.dynamic_index_in_dim(terms, 1 - row, 1, keepdims=False))
        mlp = lax.dynamic_index_in_dim(terms, row, 1, keepdims=False).astype(F32) + given.astype(F32)
        kept = lax.dynamic_index_in_dim(middle.reshape(2, 2, mine, half), row, 1, keepdims=False)
        out = (kept.astype(F32) + mlp).astype(BF)
        got = across(out[1])
        layer_out = jnp.where(
            side == 0, jnp.concatenate([out[0], got], axis=1), jnp.concatenate([got, out[0]], axis=1)
        )
        return (layer_out, cache_keys, cache_values)

    return per_device


def solution(mesh):
    n_group = mesh.shape["group"]
    in_specs = (
        P(("group", "head"), None),
        P(),
        P("group", "head"),
        P("group", "head"),
        P("group", "head"),
        P("head", "group"),
        P(),
        P("group", "head"),
        P("group", "head"),
        P("head", "group"),
        P("group", None),
        P("group", None),
    )
    out_specs = (P(("group", "head"), None), P("group", "head"), P("group", "head"))
    body = octet_plan(n_group) if n_group == 2 * OCT else gathered_plan
    return jax.shard_map(body, mesh=mesh, in_specs=in_specs, out_specs=out_specs, check_vma=False)
```

time: 208 us -> 206 us (level)
  between operations: 14.1 us -> 1.04 us
  Pallas kernels: 16.5 us -> 26.5 us
  waiting for transfers between devices: 120 us -> 124 us
  local copies, waits for them, and re-layouts: 14.7 us -> 11.8 us
  other arithmetic: 4.73 us -> 7.31 us
  starting transfers between devices: 37.3 us -> 34.9 us
    all_gather x3 -> x0, waiting for transfers between devices: 13.7 us -> none  [gathered(): lax.all_gather(w, 'group', axis=0, tiled=True, axis_index_groups=octets)]
    ppermute x28 -> x43, starting transfers between devices: 32.2 us -> 19.5 us  [swap(): return lambda x: lax.ppermute(x, 'group', pairs)]
    ppermute x28 -> x43, waiting for transfers between devices: 90.2 us -> 101 us  [swap(): return lambda x: lax.ppermute(x, 'group', pairs)]
    ppermute x0 -> x6, starting transfers between devices: none -> 9.96 us  [turn(): return lambda x: lax.ppermute(x, 'group', pairs)]
    ppermute x3 -> x4, waiting for transfers between devices: 14.8 us -> 22.2 us  [other_head(): return lax.ppermute(x, 'head', [(0, 1), (1, 0)])]
    unnamed x42 -> x50, local copies, waits for them, and re-layouts: 12.1 us -> 6.16 us
    pallas_call x4 -> x3, Pallas kernels: 8.36 us -> 13.3 us  [the longest x1 5.09 us: first_rows_product(): pl.pallas_call(first_rows_kernel, grid_spec=pltpu.PrefetchScalarGridSpec(...]
    dynamic_slice x3, local copies, waits for them, and re-layouts: 0.18 us -> 3.15 us  [the longest x1 1.59 us: columns_of(): return lax.dynamic_slice(tokens, (0, place * wide), (mine, wide))]
  transfers between devices with their start and end apart: 34 -> 53, of which waited for: 17 -> 23; matrix products, arithmetic and copies ran while one was open for 3% -> 6% of each run, Pallas kernels for 7% -> 11%
where the time goes in v3:
time: 206 us; the launch traced here: 205 us
  waiting for transfers between devices  124 us (60%)
  starting transfers between devices  34.9 us (17%)
  Pallas kernels  26.5 us (13%)
  local copies, waits for them, and re-layouts  11.8 us (6%)
  other arithmetic  7.31 us (4%)
    ppermute x43, waiting for transfers between devices, swap(): return lambda x: lax.ppermute(x, 'group', pairs)  101 us
    ppermute x4, waiting for transfers between devices, other_head(): return lax.ppermute(x, 'head', [(0, 1), (1, 0)])  22.2 us
    ppermute x43, starting transfers between devices, swap(): return lambda x: lax.ppermute(x, 'group', pairs)  19.5 us
    ppermute x6, starting transfers between devices, turn(): return lambda x: lax.ppermute(x, 'group', pairs)  9.96 us
    pallas_call x2, Pallas kernels, rows_product(): pl.pallas_call(rows_kernel, grid_spec=pltpu.PrefetchScalarGridSpec(num_sc...  8.11 us
    unnamed x50, local copies, waits for them, and re-layouts  6.16 us
    ppermute x4, starting transfers between devices, other_head(): return lax.ppermute(x, 'head', [(0, 1), (1, 0)])  5.43 us
    pallas_call x1, Pallas kernels, first_rows_product(): pl.pallas_call(first_rows_kernel, grid_spec=pltpu.PrefetchScalarGridSpec(...  5.09 us
  transfers between devices with their start and end apart: 53, of which 23 were waited for; matrix products, arithmetic and copies ran while one was open for 6% of the time, Pallas kernels for 11%

profile of v3, /device:TPU:0, one launch (start us, length us, event | category | flops | bytes accessed | tf_op | source)
XLA Modules:
  0.0 205.4 jit_solution(14834658246836784537)
XLA Ops:
  0.6 3.0 %collective-permute-start.5 = (bf16[192,768]{1,0:T(8,128)(2,1)}, bf16[192,768]{1,0:T(8,128)(2,1)}, u32[]{:S(2)}, u32[]{:S(2)}) collective-permute-start(bf16[192,768]{1,0:T(8,128)(2,1)} %refs_0_.3), channel_id=1, source_target_pairs={{0,4},{2,6},{4,0},{6,2},{8,12},{10,14},{12,8},{14,10},{16,20},{18,... | collective-permute-start | bytes 884744 | tf_op jit(solution)/shard_map/ppermute | solution.py:407
  3.6 1.6 dynamic-slice_bitcast_fusion.1
  5.2 1.6 constant_dynamic-slice_fusion.1
  6.8 1.6 collective-permute-start.2
  8.4 2.6 %collective-permute-start.1 = (bf16[32,768]{1,0:T(8,128)(2,1)}, bf16[32,768]{1,0:T(8,128)(2,1)}, u32[]{:S(2)}, u32[]{:S(2)}) collective-permute-start(bf16[32,768]{1,0:T(8,128)(2,1)} %get-tuple-element.68), channel_id=1, source_target_pairs={{0,16},{2,18},{4,20},{6,22},{8,24},{10,26},{12,28},{14,30},{16,0},... | collective-permute-start | bytes 147464 | tf_op jit(solution)/shard_map/ppermute | solution.py:426
  11.0 1.3 collective-permute-start
  13.5 0.9 pad_maximum_fusion.1.refs_0_
  15.3 1.1 collective-permute-start.14
  16.4 0.9 pad_maximum_fusion.2.mine_ref
  17.3 0.9 collective-permute-start.3
  18.2 6.0 %collective-permute-done.3 = bf16[32,1536]{1,0:T(8,128)(2,1)S(1)} collective-permute-done((bf16[32,1536]{1,0:T(8,128)(2,1)S(1)}, bf16[32,1536]{1,0:T(8,128)(2,1)S(1)}, u32[]{:S(2)}, u32[]{:S(2)}) %collective-permute-start.3) | collective-permute-done | bytes 98336 | tf_op jit(solution)/shard_map/ppermute | solution.py:407
  24.6 1.4 collective-permute-start.22
  26.6 4.0 %collective-permute-done.14.refs_10_ = bf16[192,768]{1,0:T(8,128)(2,1)S(1)} collective-permute-done((bf16[192,768]{1,0:T(8,128)(2,1)S(1)}, bf16[192,768]{1,0:T(8,128)(2,1)S(1)}, u32[]{:S(2)}, u32[]{:S(2)}) %collective-permute-start.14) | collective-permute-done | bytes 294944 | tf_op jit(solution)/shard_map/ppermute | solution.py:407
  30.7 5.0 %collective-permute-done.22.refs_2_ = bf16[384,384]{1,0:T(8,128)(2,1)} collective-permute-done((bf16[384,384]{1,0:T(8,128)(2,1)}, bf16[384,384]{1,0:T(8,128)(2,1)}, u32[]{:S(2)}, u32[]{:S(2)}) %collective-permute-start.22) | collective-permute-done | bytes 294944 | tf_op jit(solution)/shard_map/ppermute | solution.py:407
  35.7 1.5 collective-permute-start.4
  37.8 0.7 collective-permute-start.17
  39.1 2.3 %collective-permute-done.4.others_ref = bf16[2,32,1536]{2,1,0:T(8,128)(2,1)S(1)} collective-permute-done((bf16[2,32,1536]{2,1,0:T(8,128)(2,1)S(1)}, bf16[2,32,1536]{2,1,0:T(8,128)(2,1)S(1)}, u32[]{:S(2)}, u32[]{:S(2)}) %collective-permute-start.4) | collective-permute-done | bytes 196640 | tf_op jit(solution)/shard_map/ppermute | solution.py:412
  41.4 0.9 collective-permute-start.24
  42.3 2.7 %collective-permute-done.6.refs_4_ = bf16[192,2048]{1,0:T(8,128)(2,1)S(1)} collective-permute-done((bf16[192,2048]{1,0:T(8,128)(2,1)}, bf16[192,2048]{1,0:T(8,128)(2,1)S(1)}, u32[]{:S(2)}, u32[]{:S(2)}) %collective-permute-start.6) | collective-permute-done | bytes 786464 | tf_op jit(solution)/shard_map/ppermute | solution.py:407
  45.0 0.8 dynamic_slice.40
  45.7 0.8 dynamic_slice.41
  46.5 2.2 %fusion.2 = (f32[64,768]{1,0:T(8,128)}, f32[64,768]{1,0:T(8,128)}, f32[64,768]{1,0:T(8,128)}) fusion(f32[768]{0:T(1024)S(1)} %fusion.11, f32[64]{0:T(128)} %subtract_convert_fusion, pred[768]{0:T(1024)(128)(4,1)S(1)} %fusion.12), kind=kLoop, calls=%fused_computation.8 | loop fusion | flops 196608 | bytes 593920 | tf_op jit(solution)/shard_map/jit(_where)/select_n | solution.py:397
  48.8 1.5 collective-permute-start.7
  50.3 1.3 collective-permute-start.25
  51.6 4.5 %collective-permute-done.7.others_ref = bf16[4,32,768]{2,1,0:T(8,128)(2,1)S(1)} collective-permute-done((bf16[4,32,768]{2,1,0:T(8,128)(2,1)S(1)}, bf16[4,32,768]{2,1,0:T(8,128)(2,1)S(1)}, u32[]{:S(2)}, u32[]{:S(2)}) %collective-permute-start.7) | collective-permute-done | bytes 196640 | tf_op jit(solution)/shard_map/ppermute | solution.py:412
  56.1 0.7 copy-done.2
  56.8 0.9 copy-done.3
  57.7 0.9 shard_map.139
  58.6 0.8 copy-done.1
  59.5 0.6 copy-done.7
  60.1 0.6 copy-done.8
  60.7 5.1 %shard_map.140 = (bf16[64,2432]{1,0:T(8,128)(2,1)}, bf16[64,2432]{1,0:T(8,128)(2,1)}, bf16[64,2432]{1,0:T(8,128)(2,1)}, f32[64,2304]{1,0:T(8,128)}) custom-call(s32[1]{0:T(128)} %bitcast.8.place, bf16[4,256,192]{2,1,0:T(8,128)(2,1)} %copy-done.1, bf16[192,128]{1,0:T(8,128)(2,1)} %copy-done.7, bf16[192,768]{1,0:T(8,128)(2,1)} %refs_0_.3, ...), custom_call_target="tpu_custom_call" | custom-call | tf_op jit(solution)/shard_map/pallas_call | solution.py:241
  66.3 1.6 collective-permute-start.18
  67.9 2.8 %collective-permute-start.20 = (bf16[64,2432]{1,0:T(8,128)(2,1)}, bf16[64,2432]{1,0:T(8,128)(2,1)}, u32[]{:S(2)}, u32[]{:S(2)}) collective-permute-start(bf16[64,2432]{1,0:T(8,128)(2,1)} %get-tuple-element.84), channel_id=1, source_target_pairs={{0,24},{2,26},{4,28},{6,30},{8,0},{10,2},{12,4},{14,6},{16,8},{18,... | collective-permute-start | bytes 933896 | tf_op jit(solution)/shard_map/ppermute | solution.py:426
  70.8 5.3 %collective-permute-done.24.refs_2_ = bf16[192,2048]{1,0:T(8,128)(2,1)} collective-permute-done((bf16[192,2048]{1,0:T(8,128)(2,1)}, bf16[192,2048]{1,0:T(8,128)(2,1)}, u32[]{:S(2)}, u32[]{:S(2)}) %collective-permute-start.24) | collective-permute-done | bytes 786464 | tf_op jit(solution)/shard_map/ppermute | solution.py:407
  76.7 16.1 %collective-permute-done.25.refs_2_ = bf16[1024,384]{1,0:T(8,128)(2,1)S(1)} collective-permute-done((bf16[1024,384]{1,0:T(8,128)(2,1)S(1)}, bf16[1024,384]{1,0:T(8,128)(2,1)S(1)}, u32[]{:S(2)}, u32[]{:S(2)}) %collective-permute-start.25) | collective-permute-done | bytes 786464 | tf_op jit(solution)/shard_map/ppermute | solution.py:407
  92.8 0.7 copy.28.refs_9_
  93.6 3.2 %collective-permute-done.21.refs_6_ = bf16[384,384]{1,0:T(8,128)(2,1)} collective-permute-done((bf16[384,384]{1,0:T(8,128)(2,1)}, bf16[384,384]{1,0:T(8,128)(2,1)}, u32[]{:S(2)}, u32[]{:S(2)}) %collective-permute-start.21) | collective-permute-done | bytes 294944 | tf_op jit(solution)/shard_map/ppermute | solution.py:407
  96.7 3.7 %shard_map.141 = (bf16[64,768]{1,0:T(8,128)(2,1)}, bf16[64,768]{1,0:T(8,128)(2,1)}, bf16[64,768]{1,0:T(8,128)(2,1)}) custom-call(f32[64,2304]{1,0:T(8,128)} %get-tuple-element.76.refs_0_, bf16[64,2432]{1,0:T(8,128)(2,1)} %collective-permute-done.18.refs_1_, bf16[64,2432]{1,0:T(8,128)(2,1)} %collective-permute-done.19.refs_2_, ...), custom_call_target="tpu_custom_call" | custom-call | tf_op jit(solution)/shard_map/pallas_call | solution.py:383
  100.5 1.7 collective-permute-start.33
  102.7 5.1 %collective-permute-done.26.got_ref = bf16[64,768]{1,0:T(8,128)(2,1)S(1)} collective-permute-done((bf16[64,768]{1,0:T(8,128)(2,1)}, bf16[64,768]{1,0:T(8,128)(2,1)S(1)}, u32[]{:S(2)}, u32[]{:S(2)}) %collective-permute-start.26) | collective-permute-done | bytes 98336 | tf_op jit(solution)/shard_map/ppermute | solution.py:407
  107.9 1.8 collective-permute-done.30.refs_7_
  109.7 3.7 %shard_map.142.a_ref = bf16[128,1536]{1,0:T(8,128)(2,1)} custom-call(s32[1]{0:T(128)} %bitcast.7.place, bf16[64,768]{1,0:T(8,128)(2,1)} %get-tuple-element.93.own_ref, bf16[64,768]{1,0:T(8,128)(2,1)} %copy-done.19, bf16[384,384]{1,0:T(8,128)(2,1)} %pad_maximum_fusion.1.refs_0_, bf16[384,384]{1,0:T(8,128)(2,1)} %collective-permute-done.27.refs_1_, ...), custom_call_target="tpu_custom_call" | custom-call | tf_op jit(solution)/shard_map/pallas_call | solution.py:318
  113.4 1.0 collective-permute-start.31
  114.9 9.9 %collective-permute-done.31.b_ref = bf16[128,1536]{1,0:T(8,128)(2,1)S(1)} collective-permute-done((bf16[128,1536]{1,0:T(8,128)(2,1)}, bf16[128,1536]{1,0:T(8,128)(2,1)S(1)}, u32[]{:S(2)}, u32[]{:S(2)}) %collective-permute-start.31) | collective-permute-done | bytes 393248 | tf_op jit(solution)/shard_map/ppermute | solution.py:412
  125.3 2.8 %collective-permute-done.32.refs_4_ = bf16[192,2048]{1,0:T(8,128)(2,1)} collective-permute-done((bf16[192,2048]{1,0:T(8,128)(2,1)}, bf16[192,2048]{1,0:T(8,128)(2,1)}, u32[]{:S(2)}, u32[]{:S(2)}) %collective-permute-start.32) | collective-permute-done | bytes 786464 | tf_op jit(solution)/shard_map/ppermute | solution.py:407
  128.1 1.0 copy-done
  129.5 0.7 copy-done.6
  130.2 0.9 collective-permute-start.42
  131.1 4.1 %shard_map.144 = (bf16[64,2176]{1,0:T(8,128)(2,1)S(1)}, f32[64,2048]{1,0:T(8,128)S(1)}) custom-call(s32[1]{0:T(128)} %bitcast.7.place, bf16[8,128,192]{2,1,0:T(8,128)(2,1)S(1)} %get-tuple-element.109.lhs, bf16[64,128]{1,0:T(8,128)(2,1)S(1)} %get-tuple-element.102.coded_ref, bf16[192,2048]{1,0:T(8,128)(2,1)} %refs_0_.4, ...), custom_call_target="tpu_custom_call" | custom-call | tf_op jit(solution)/shard_map/pallas_call | solution.py:197
  135.2 0.9 collective-permute-start.38
  136.6 12.9 %collective-permute-done.42.refs_6_ = bf16[192,2048]{1,0:T(8,128)(2,1)S(1)} collective-permute-done((bf16[192,2048]{1,0:T(8,128)(2,1)}, bf16[192,2048]{1,0:T(8,128)(2,1)S(1)}, u32[]{:S(2)}, u32[]{:S(2)}) %collective-permute-start.42) | collective-permute-done | bytes 786464 | tf_op jit(solution)/shard_map/ppermute | solution.py:407
  149.8 1.3 collective-permute-start.49
  151.2 0.9 collective-permute-done.43.refs_7_
  152.1 4.1 %shard_map.145 = (bf16[64,2048]{1,0:T(8,128)(2,1)S(1)}, f32[64,2048]{1,0:T(8,128)S(1)}) custom-call(s32[1]{0:T(128)} %bitcast.7.place, bf16[8,128,192]{2,1,0:T(8,128)(2,1)S(1)} %get-tuple-element.109.lhs, bf16[64,128]{1,0:T(8,128)(2,1)S(1)} %get-tuple-element.102.coded_ref, bf16[192,2048]{1,0:T(8,128)(2,1)} %refs_0_.5, ...), custom_call_target="tpu_custom_call" | custom-call | tf_op jit(solution)/shard_map/pallas_call | solution.py:197
  157.0 12.9 %collective-permute-done.49.refs_6_ = bf16[1024,384]{1,0:T(8,128)(2,1)} collective-permute-done((bf16[1024,384]{1,0:T(8,128)(2,1)S(1)}, bf16[1024,384]{1,0:T(8,128)(2,1)}, u32[]{:S(2)}, u32[]{:S(2)}) %collective-permute-start.49) | collective-permute-done | bytes 786464 | tf_op jit(solution)/shard_map/ppermute | solution.py:407
  169.9 0.9 collective-permute-done.44
  171.3 14.1 %collective-permute-done.45.got_ref = bf16[64,2048]{1,0:T(8,128)(2,1)S(1)} collective-permute-done((bf16[64,2048]{1,0:T(8,128)(2,1)S(1)}, bf16[64,2048]{1,0:T(8,128)(2,1)S(1)}, u32[]{:S(2)}, u32[]{:S(2)}) %collective-permute-start.45) | collective-permute-done | bytes 262176 | tf_op jit(solution)/shard_map/ppermute | solution.py:407
  185.4 4.6 %shard_map.146 = bf16[128,1536]{1,0:T(8,128)(2,1)S(1)} custom-call(s32[1]{0:T(128)} %bitcast.7.place, bf16[64,2048]{1,0:T(8,128)(2,1)S(1)} %multiply_convert_fusion.own_ref, bf16[64,2048]{1,0:T(8,128)(2,1)S(1)} %collective-permute-done.45.got_ref, bf16[1024,384]{1,0:T(8,128)(2,1)S(1)} %pad_maximum_fusion.refs_0_, ...), custom_call_target="tpu_custom_call" | custom-call | tf_op jit(solution)/shard_map/pallas_call | solution.py:279
  190.1 1.4 collective-permute-start.51
  191.5 5.5 %collective-permute-done.51 = bf16[2,32,1536]{2,1,0:T(8,128)(2,1)S(1)} collective-permute-done((bf16[2,32,1536]{2,1,0:T(8,128)(2,1)S(1)}, bf16[2,32,1536]{2,1,0:T(8,128)(2,1)S(1)}, u32[]{:S(2)}, u32[]{:S(2)}) %collective-permute-start.51) | collective-permute-done | bytes 196640 | tf_op jit(solution)/shard_map/ppermute | solution.py:412
  197.0 1.0 fusion.1
  198.1 6.6 %collective-permute-done.52 = bf16[32,1536]{1,0:T(8,128)(2,1)S(1)} collective-permute-done((bf16[32,1536]{1,0:T(8,128)(2,1)S(1)}, bf16[32,1536]{1,0:T(8,128)(2,1)S(1)}, u32[]{:S(2)}, u32[]{:S(2)}) %collective-permute-start.52) | collective-permute-done | bytes 98336 | tf_op jit(solution)/shard_map/ppermute | solution.py:407
  204.7 0.7 maximum_select_fusion
  (129 shorter events, 9.8 us)
Async XLA Ops:
  0.6 11.7 %copy-start.17 = (bf16[768,192]{0,1:T(8,128)(2,1)S(1)}, bf16[768,192]{0,1:T(8,128)(2,1)}, u32[]{:S(2)}) copy-start(bf16[768,192]{0,1:T(8,128)(2,1)} %param.17) | copy-start | bytes 884740
  0.6 24.0 %collective-permute-start.5 = (bf16[192,768]{1,0:T(8,128)(2,1)}, bf16[192,768]{1,0:T(8,128)(2,1)}, u32[]{:S(2)}, u32[]{:S(2)}) collective-permute-start(bf16[192,768]{1,0:T(8,128)(2,1)} %refs_0_.3), channel_id=1, source_target_pairs={{0,4},{2,6},{4,0},{6,2},{8,12},{10,14},{12,8},{14,10},{16,20},{18,... | collective-permute-start | bytes 884744 | tf_op jit(solution)/shard_map/ppermute | solution.py:407
  3.6 22.4 %collective-permute-start.8 = (bf16[192,768]{1,0:T(8,128)(2,1)}, bf16[192,768]{1,0:T(8,128)(2,1)}, u32[]{:S(2)}, u32[]{:S(2)}) collective-permute-start(bf16[192,768]{1,0:T(8,128)(2,1)} %refs_0_.3), channel_id=1, source_target_pairs={{0,2},{2,0},{4,6},{6,4},{8,10},{10,8},{12,14},{14,12},{16,18},{18,... | collective-permute-start | bytes 884744 | tf_op jit(solution)/shard_map/ppermute | solution.py:407
  5.2 7.4 %copy-start.9 = (bf16[2048,192]{0,1:T(8,128)(2,1)S(1)}, bf16[2048,192]{0,1:T(8,128)(2,1)}, u32[]{:S(2)}) copy-start(bf16[2048,192]{0,1:T(8,128)(2,1)} %param.21) | copy-start | bytes 2359300
  6.8 7.6 %collective-permute-start.2 = (bf16[32,768]{1,0:T(8,128)(2,1)}, bf16[32,768]{1,0:T(8,128)(2,1)}, u32[]{:S(2)}, u32[]{:S(2)}) collective-permute-start(bf16[32,768]{1,0:T(8,128)(2,1)} %get-tuple-element.69), channel_id=1, source_target_pairs={{0,8},{2,10},{4,12},{6,14},{8,16},{10,18},{12,20},{14,22},{16,24},... | collective-permute-start | bytes 147464 | tf_op jit(solution)/shard_map/ppermute | solution.py:426
  8.4 6.9 %collective-permute-start.1 = (bf16[32,768]{1,0:T(8,128)(2,1)}, bf16[32,768]{1,0:T(8,128)(2,1)}, u32[]{:S(2)}, u32[]{:S(2)}) collective-permute-start(bf16[32,768]{1,0:T(8,128)(2,1)} %get-tuple-element.68), channel_id=1, source_target_pairs={{0,16},{2,18},{4,20},{6,22},{8,24},{10,26},{12,28},{14,30},{16,0},... | collective-permute-start | bytes 147464 | tf_op jit(solution)/shard_map/ppermute | solution.py:426
  11.0 5.4 %collective-permute-start = (bf16[32,768]{1,0:T(8,128)(2,1)S(1)}, bf16[32,768]{1,0:T(8,128)(2,1)}, u32[]{:S(2)}, u32[]{:S(2)}) collective-permute-start(bf16[32,768]{1,0:T(8,128)(2,1)S(1)} %get-tuple-element.67), channel_id=1, source_target_pairs={{0,24},{2,26},{4,28},{6,30},{8,0},{10,2},{12,4},{14,6},{16,8},{18,... | collective-permute-start | bytes 147464 | tf_op jit(solution)/shard_map/ppermute | solution.py:426
  13.2 3.2 %copy-start.18 = (bf16[32,768]{1,0:T(8,128)(2,1)S(1)}, bf16[32,768]{1,0:T(8,128)(2,1)}, u32[]{:S(2)}) copy-start(bf16[32,768]{1,0:T(8,128)(2,1)} %get-tuple-element.66) | copy-start | bytes 147460
  13.5 3.8 %copy-start.20 = (bf16[32,1536]{1,0:T(8,128)(2,1)S(1)}, bf16[32,1536]{1,0:T(8,128)(2,1)}, u32[]{:S(2)}) copy-start(bf16[32,1536]{1,0:T(8,128)(2,1)} %get-tuple-element.70) | copy-start | bytes 294916
  13.5 4.7 %copy-start.21 = (s32[1,64]{1,0:T(1,128)S(1)}, s32[1,64]{1,0:T(1,128)}, u32[]{:S(2)}) copy-start(s32[1,64]{1,0:T(1,128)} %refs_8_.3) | copy-start | bytes 772
  14.4 11.7 %collective-permute-start.11 = (bf16[192,768]{1,0:T(8,128)(2,1)S(1)}, bf16[192,768]{1,0:T(8,128)(2,1)S(1)}, u32[]{:S(2)}, u32[]{:S(2)}) collective-permute-start(bf16[192,768]{1,0:T(8,128)(2,1)S(1)} %copy-done.10), channel_id=1, source_target_pairs={{0,4},{2,6},{4,0},{6,2},{8,12},{10,14},{12,8},{14,10},{16,20},{18,... | collective-permute-start | bytes 884744 | tf_op jit(solution)/shard_map/ppermute | solution.py:407
  15.3 15.3 %collective-permute-start.14 = (bf16[192,768]{1,0:T(8,128)(2,1)S(1)}, bf16[192,768]{1,0:T(8,128)(2,1)S(1)}, u32[]{:S(2)}, u32[]{:S(2)}) collective-permute-start(bf16[192,768]{1,0:T(8,128)(2,1)S(1)} %copy-done.11), channel_id=1, source_target_pairs={{0,4},{2,6},{4,0},{6,2},{8,12},{10,14},{12,8},{14,10},{16,20},{18,... | collective-permute-start | bytes 884744 | tf_op jit(solution)/shard_map/ppermute | solution.py:407
  17.3 6.9 %collective-permute-start.3 = (bf16[32,1536]{1,0:T(8,128)(2,1)S(1)}, bf16[32,1536]{1,0:T(8,128)(2,1)S(1)}, u32[]{:S(2)}, u32[]{:S(2)}) collective-permute-start(bf16[32,1536]{1,0:T(8,128)(2,1)S(1)} %copy-done.20), channel_id=1, source_target_pairs={{0,16},{2,18},{4,20},{6,22},{8,24},{10,26},{12,28},{14,30},{16,0},... | collective-permute-start | bytes 294920 | tf_op jit(solution)/shard_map/ppermute | solution.py:407
  24.2 20.7 %collective-permute-start.6 = (bf16[192,2048]{1,0:T(8,128)(2,1)}, bf16[192,2048]{1,0:T(8,128)(2,1)S(1)}, u32[]{:S(2)}, u32[]{:S(2)}) collective-permute-start(bf16[192,2048]{1,0:T(8,128)(2,1)} %refs_0_.4), channel_id=1, source_target_pairs={{0,8},{2,10},{4,12},{6,14},{8,0},{10,2},{12,4},{14,6},{16,24},{18,... | collective-permute-start | bytes 2359304 | tf_op jit(solution)/shard_map/ppermute | solution.py:407
  24.6 11.1 %collective-permute-start.22 = (bf16[384,384]{1,0:T(8,128)(2,1)}, bf16[384,384]{1,0:T(8,128)(2,1)}, u32[]{:S(2)}, u32[]{:S(2)}) collective-permute-start(bf16[384,384]{1,0:T(8,128)(2,1)} %pad_maximum_fusion.1.refs_0_), channel_id=1, source_target_pairs={{0,4},{2,6},{4,0},{6,2},{8,12},{10,14},{12,8},{14,10},{16,20},{18,... | collective-permute-start | bytes 884744 | tf_op jit(solution)/shard_map/ppermute | solution.py:407
  26.0 11.7 %collective-permute-start.10 = (bf16[192,768]{1,0:T(8,128)(2,1)S(1)}, bf16[192,768]{1,0:T(8,128)(2,1)}, u32[]{:S(2)}, u32[]{:S(2)}) collective-permute-start(bf16[192,768]{1,0:T(8,128)(2,1)S(1)} %copy-done.10), channel_id=1, source_target_pairs={{0,2},{2,0},{4,6},{6,4},{8,10},{10,8},{12,14},{14,12},{16,18},{18,... | collective-permute-start | bytes 884744 | tf_op jit(solution)/shard_map/ppermute | solution.py:407
  26.1 4.5 %copy-start.12 = (bf16[192,768]{1,0:T(8,128)(2,1)}, bf16[192,768]{1,0:T(8,128)(2,1)S(1)}, u32[]{:S(2)}) copy-start(bf16[192,768]{1,0:T(8,128)(2,1)S(1)} %collective-permute-done.11.refs_6_) | copy-start | bytes 884740
  26.1 12.3 %collective-permute-start.13 = (bf16[192,768]{1,0:T(8,128)(2,1)S(1)}, bf16[192,768]{1,0:T(8,128)(2,1)S(1)}, u32[]{:S(2)}, u32[]{:S(2)}) collective-permute-start(bf16[192,768]{1,0:T(8,128)(2,1)S(1)} %copy-done.11), channel_id=1, source_target_pairs={{0,2},{2,0},{4,6},{6,4},{8,10},{10,8},{12,14},{14,12},{16,18},{18,... | collective-permute-start | bytes 884744 | tf_op jit(solution)/shard_map/ppermute | solution.py:407
  30.6 7.1 %copy-start.13 = (bf16[192,768]{1,0:T(8,128)(2,1)}, bf16[192,768]{1,0:T(8,128)(2,1)S(1)}, u32[]{:S(2)}) copy-start(bf16[192,768]{1,0:T(8,128)(2,1)S(1)} %collective-permute-done.14.refs_10_) | copy-start | bytes 884740
  30.6 11.6 %collective-permute-start.9 = (bf16[192,768]{1,0:T(8,128)(2,1)}, bf16[192,768]{1,0:T(8,128)(2,1)S(1)}, u32[]{:S(2)}, u32[]{:S(2)}) collective-permute-start(bf16[192,768]{1,0:T(8,128)(2,1)} %collective-permute-done.5.refs_2_), channel_id=1, source_target_pairs={{0,2},{2,0},{4,6},{6,4},{8,10},{10,8},{12,14},{14,12},{16,18},{18,... | collective-permute-start | bytes 884744 | tf_op jit(solution)/shard_map/ppermute | solution.py:407
  35.7 5.7 %collective-permute-start.4 = (bf16[2,32,1536]{2,1,0:T(8,128)(2,1)S(1)}, bf16[2,32,1536]{2,1,0:T(8,128)(2,1)S(1)}, u32[]{:S(2)}, u32[]{:S(2)}) collective-permute-start(bf16[2,32,1536]{2,1,0:T(8,128)(2,1)S(1)} %pad_maximum_fusion.3.mine_ref), channel_id=1, source_target_pairs={{0,1},{1,0},{2,3},{3,2},{4,5},{5,4},{6,7},{7,6},{8,9},{9,8},{10,11... | collective-permute-start | bytes 589832 | tf_op jit(solution)/shard_map/ppermute | solution.py:412
  37.8 28.6 %collective-permute-start.17 = (bf16[1024,384]{1,0:T(8,128)(2,1)S(1)}, bf16[1024,384]{1,0:T(8,128)(2,1)S(1)}, u32[]{:S(2)}, u32[]{:S(2)}) collective-permute-start(bf16[1024,384]{1,0:T(8,128)(2,1)S(1)} %pad_maximum_fusion.refs_0_), channel_id=1, source_target_pairs={{0,8},{2,10},{4,12},{6,14},{8,0},{10,2},{12,4},{14,6},{16,24},{18,... | collective-permute-start | bytes 2359304 | tf_op jit(solution)/shard_map/ppermute | solution.py:407
  38.4 6.5 %copy-start.14 = (bf16[192,768]{1,0:T(8,128)(2,1)}, bf16[192,768]{1,0:T(8,128)(2,1)S(1)}, u32[]{:S(2)}) copy-start(bf16[192,768]{1,0:T(8,128)(2,1)S(1)} %collective-permute-done.13.refs_9_) | copy-start | bytes 884740
  38.4 29.5 %collective-permute-start.23 = (bf16[192,2048]{1,0:T(8,128)(2,1)}, bf16[192,2048]{1,0:T(8,128)(2,1)}, u32[]{:S(2)}, u32[]{:S(2)}) collective-permute-start(bf16[192,2048]{1,0:T(8,128)(2,1)} %refs_0_.4), channel_id=1, source_target_pairs={{0,4},{2,6},{4,0},{6,2},{8,12},{10,14},{12,8},{14,10},{16,20},{18,... | collective-permute-start | bytes 2359304 | tf_op jit(solution)/shard_map/ppermute | solution.py:407
  41.4 8.9 %copy-start.4 = (bf16[2,32,1536]{2,1,0:T(8,128)(2,1)}, bf16[2,32,1536]{2,1,0:T(8,128)(2,1)S(1)}, u32[]{:S(2)}) copy-start(bf16[2,32,1536]{2,1,0:T(8,128)(2,1)S(1)} %collective-permute-done.4.others_ref) | copy-start | bytes 589828
  41.4 34.7 %collective-permute-start.24 = (bf16[192,2048]{1,0:T(8,128)(2,1)}, bf16[192,2048]{1,0:T(8,128)(2,1)}, u32[]{:S(2)}, u32[]{:S(2)}) collective-permute-start(bf16[192,2048]{1,0:T(8,128)(2,1)} %refs_0_.5), channel_id=1, source_target_pairs={{0,4},{2,6},{4,0},{6,2},{8,12},{10,14},{12,8},{14,10},{16,20},{18,... | collective-permute-start | bytes 2359304 | tf_op jit(solution)/shard_map/ppermute | solution.py:407
  42.3 6.5 %collective-permute-start.12 = (bf16[192,768]{1,0:T(8,128)(2,1)}, bf16[192,768]{1,0:T(8,128)(2,1)S(1)}, u32[]{:S(2)}, u32[]{:S(2)}) collective-permute-start(bf16[192,768]{1,0:T(8,128)(2,1)} %copy-done.12), channel_id=1, source_target_pairs={{0,2},{2,0},{4,6},{6,4},{8,10},{10,8},{12,14},{14,12},{16,18},{18,... | collective-permute-start | bytes 884744 | tf_op jit(solution)/shard_map/ppermute | solution.py:407
  44.9 5.4 %collective-permute-start.15 = (bf16[192,768]{1,0:T(8,128)(2,1)}, bf16[192,768]{1,0:T(8,128)(2,1)}, u32[]{:S(2)}, u32[]{:S(2)}) collective-permute-start(bf16[192,768]{1,0:T(8,128)(2,1)} %copy-done.13), channel_id=1, source_target_pairs={{0,2},{2,0},{4,6},{6,4},{8,10},{10,8},{12,14},{14,12},{16,18},{18,... | collective-permute-start | bytes 884744 | tf_op jit(solution)/shard_map/ppermute | solution.py:407
  48.8 7.3 %collective-permute-start.7 = (bf16[4,32,768]{2,1,0:T(8,128)(2,1)S(1)}, bf16[4,32,768]{2,1,0:T(8,128)(2,1)S(1)}, u32[]{:S(2)}, u32[]{:S(2)}) collective-permute-start(bf16[4,32,768]{2,1,0:T(8,128)(2,1)S(1)} %pad_maximum_fusion.2.mine_ref), channel_id=1, source_target_pairs={{0,1},{1,0},{2,3},{3,2},{4,5},{5,4},{6,7},{7,6},{8,9},{9,8},{10,11... | collective-permute-start | bytes 589832 | tf_op jit(solution)/shard_map/ppermute | solution.py:412
  50.3 42.5 %collective-permute-start.25 = (bf16[1024,384]{1,0:T(8,128)(2,1)S(1)}, bf16[1024,384]{1,0:T(8,128)(2,1)S(1)}, u32[]{:S(2)}, u32[]{:S(2)}) collective-permute-start(bf16[1024,384]{1,0:T(8,128)(2,1)S(1)} %pad_maximum_fusion.refs_0_), channel_id=1, source_target_pairs={{0,4},{2,6},{4,0},{6,2},{8,12},{10,14},{12,8},{14,10},{16,20},{18,... | collective-permute-start | bytes 2359304 | tf_op jit(solution)/shard_map/ppermute | solution.py:407
  56.8 9.6 %collective-permute-start.16 = (bf16[384,384]{1,0:T(8,128)(2,1)}, bf16[384,384]{1,0:T(8,128)(2,1)}, u32[]{:S(2)}, u32[]{:S(2)}) collective-permute-start(bf16[384,384]{1,0:T(8,128)(2,1)} %pad_maximum_fusion.1.refs_0_), channel_id=1, source_target_pairs={{0,8},{2,10},{4,12},{6,14},{8,0},{10,2},{12,4},{14,6},{16,24},{18,... | collective-permute-start | bytes 884744 | tf_op jit(solution)/shard_map/ppermute | solution.py:407
  60.7 32.1 %copy-start.22 = (s32[1,64]{1,0:T(1,128)S(1)}, s32[1,64]{1,0:T(1,128)}, u32[]{:S(2)}) copy-start(s32[1,64]{1,0:T(1,128)} %refs_8_.3) | copy-start | bytes 772
  66.3 30.4 %collective-permute-start.18 = (bf16[64,2432]{1,0:T(8,128)(2,1)}, bf16[64,2432]{1,0:T(8,128)(2,1)}, u32[]{:S(2)}, u32[]{:S(2)}) collective-permute-start(bf16[64,2432]{1,0:T(8,128)(2,1)} %get-tuple-element.82), channel_id=1, source_target_pairs={{0,8},{2,10},{4,12},{6,14},{8,16},{10,18},{12,20},{14,22},{16,24},... | collective-permute-start | bytes 933896 | tf_op jit(solution)/shard_map/ppermute | solution.py:426
  67.9 28.8 %collective-permute-start.19 = (bf16[64,2432]{1,0:T(8,128)(2,1)}, bf16[64,2432]{1,0:T(8,128)(2,1)}, u32[]{:S(2)}, u32[]{:S(2)}) collective-permute-start(bf16[64,2432]{1,0:T(8,128)(2,1)} %get-tuple-element.83), channel_id=1, source_target_pairs={{0,16},{2,18},{4,20},{6,22},{8,24},{10,26},{12,28},{14,30},{16,0},... | collective-permute-start | bytes 933896 | tf_op jit(solution)/shard_map/ppermute | solution.py:426
  67.9 28.8 %collective-permute-start.20 = (bf16[64,2432]{1,0:T(8,128)(2,1)}, bf16[64,2432]{1,0:T(8,128)(2,1)}, u32[]{:S(2)}, u32[]{:S(2)}) collective-permute-start(bf16[64,2432]{1,0:T(8,128)(2,1)} %get-tuple-element.84), channel_id=1, source_target_pairs={{0,24},{2,26},{4,28},{6,30},{8,0},{10,2},{12,4},{14,6},{16,8},{18,... | collective-permute-start | bytes 933896 | tf_op jit(solution)/shard_map/ppermute | solution.py:426
  76.1 20.6 %collective-permute-start.21 = (bf16[384,384]{1,0:T(8,128)(2,1)}, bf16[384,384]{1,0:T(8,128)(2,1)}, u32[]{:S(2)}, u32[]{:S(2)}) collective-permute-start(bf16[384,384]{1,0:T(8,128)(2,1)} %collective-permute-done.16.refs_4_), channel_id=1, source_target_pairs={{0,4},{2,6},{4,0},{6,2},{8,12},{10,14},{12,8},{14,10},{16,20},{18,... | collective-permute-start | bytes 884744 | tf_op jit(solution)/shard_map/ppermute | solution.py:407
  92.8 15.0 %collective-permute-start.27 = (bf16[384,384]{1,0:T(8,128)(2,1)}, bf16[384,384]{1,0:T(8,128)(2,1)}, u32[]{:S(2)}, u32[]{:S(2)}) collective-permute-start(bf16[384,384]{1,0:T(8,128)(2,1)} %pad_maximum_fusion.1.refs_0_), channel_id=1, source_target_pairs={{0,2},{2,0},{4,6},{6,4},{8,10},{10,8},{12,14},{14,12},{16,18},{18,... | collective-permute-start | bytes 884744 | tf_op jit(solution)/shard_map/ppermute | solution.py:407
  100.4 7.4 %collective-permute-start.26 = (bf16[64,768]{1,0:T(8,128)(2,1)}, bf16[64,768]{1,0:T(8,128)(2,1)S(1)}, u32[]{:S(2)}, u32[]{:S(2)}) collective-permute-start(bf16[64,768]{1,0:T(8,128)(2,1)} %get-tuple-element.93.own_ref), channel_id=1, source_target_pairs={{0,16},{2,18},{4,20},{6,22},{8,24},{10,26},{12,28},{14,30},{16,0},... | collective-permute-start | bytes 294920 | tf_op jit(solution)/shard_map/ppermute | solution.py:407
  100.5 24.3 %collective-permute-start.33 = (bf16[192,2048]{1,0:T(8,128)(2,1)S(1)}, bf16[192,2048]{1,0:T(8,128)(2,1)}, u32[]{:S(2)}, u32[]{:S(2)}) collective-permute-start(bf16[192,2048]{1,0:T(8,128)(2,1)S(1)} %collective-permute-done.6.refs_4_), channel_id=1, source_target_pairs={{0,4},{2,6},{4,0},{6,2},{8,12},{10,14},{12,8},{14,10},{16,20},{18,... | collective-permute-start | bytes 2359304 | tf_op jit(solution)/shard_map/ppermute | solution.py:407
  102.2 5.7 %collective-permute-start.29 = (bf16[384,384]{1,0:T(8,128)(2,1)}, bf16[384,384]{1,0:T(8,128)(2,1)}, u32[]{:S(2)}, u32[]{:S(2)}) collective-permute-start(bf16[384,384]{1,0:T(8,128)(2,1)} %collective-permute-done.16.refs_4_), channel_id=1, source_target_pairs={{0,2},{2,0},{4,6},{6,4},{8,10},{10,8},{12,14},{14,12},{16,18},{18,... | collective-permute-start | bytes 884744 | tf_op jit(solution)/shard_map/ppermute | solution.py:407
  102.2 5.7 %collective-permute-start.28 = (bf16[384,384]{1,0:T(8,128)(2,1)}, bf16[384,384]{1,0:T(8,128)(2,1)}, u32[]{:S(2)}, u32[]{:S(2)}) collective-permute-start(bf16[384,384]{1,0:T(8,128)(2,1)} %collective-permute-done.22.refs_2_), channel_id=1, source_target_pairs={{0,2},{2,0},{4,6},{6,4},{8,10},{10,8},{12,14},{14,12},{16,18},{18,... | collective-permute-start | bytes 884744 | tf_op jit(solution)/shard_map/ppermute | solution.py:407
  107.8 1.9 collective-permute-start.30
  107.8 20.3 %collective-permute-start.32 = (bf16[192,2048]{1,0:T(8,128)(2,1)}, bf16[192,2048]{1,0:T(8,128)(2,1)}, u32[]{:S(2)}, u32[]{:S(2)}) collective-permute-start(bf16[192,2048]{1,0:T(8,128)(2,1)} %refs_0_.5), channel_id=1, source_target_pairs={{0,8},{2,10},{4,12},{6,14},{8,0},{10,2},{12,4},{14,6},{16,24},{18,... | collective-permute-start | bytes 2359304 | tf_op jit(solution)/shard_map/ppermute | solution.py:407
  109.7 18.4 %copy-start.5 = (bf16[2,32,1536]{2,1,0:T(8,128)(2,1)S(1)}, bf16[2,32,1536]{2,1,0:T(8,128)(2,1)}, u32[]{:S(2)}) copy-start(bf16[2,32,1536]{2,1,0:T(8,128)(2,1)} %copy-done.4) | copy-start | bytes 589828
  113.4 11.4 %collective-permute-start.31 = (bf16[128,1536]{1,0:T(8,128)(2,1)}, bf16[128,1536]{1,0:T(8,128)(2,1)S(1)}, u32[]{:S(2)}, u32[]{:S(2)}) collective-permute-start(bf16[128,1536]{1,0:T(8,128)(2,1)} %shard_map.142.a_ref), channel_id=1, source_target_pairs={{0,1},{1,0},{2,3},{3,2},{4,5},{5,4},{6,7},{7,6},{8,9},{9,8},{10,11... | collective-permute-start | bytes 1179656 | tf_op jit(solution)/shard_map/ppermute | solution.py:412
  114.4 16.7 %collective-permute-start.36 = (bf16[192,2048]{1,0:T(8,128)(2,1)S(1)}, bf16[192,2048]{1,0:T(8,128)(2,1)S(1)}, u32[]{:S(2)}, u32[]{:S(2)}) collective-permute-start(bf16[192,2048]{1,0:T(8,128)(2,1)S(1)} %collective-permute-done.6.refs_4_), channel_id=1, source_target_pairs={{0,2},{2,0},{4,6},{6,4},{8,10},{10,8},{12,14},{14,12},{16,18},{18,... | collective-permute-start | bytes 2359304 | tf_op jit(solution)/shard_map/ppermute | solution.py:407
  114.4 16.7 %collective-permute-start.34 = (bf16[192,2048]{1,0:T(8,128)(2,1)}, bf16[192,2048]{1,0:T(8,128)(2,1)S(1)}, u32[]{:S(2)}, u32[]{:S(2)}) collective-permute-start(bf16[192,2048]{1,0:T(8,128)(2,1)} %refs_0_.4), channel_id=1, source_target_pairs={{0,2},{2,0},{4,6},{6,4},{8,10},{10,8},{12,14},{14,12},{16,18},{18,... | collective-permute-start | bytes 2359304 | tf_op jit(solution)/shard_map/ppermute | solution.py:407
  124.8 6.4 %collective-permute-start.35 = (bf16[192,2048]{1,0:T(8,128)(2,1)}, bf16[192,2048]{1,0:T(8,128)(2,1)S(1)}, u32[]{:S(2)}, u32[]{:S(2)}) collective-permute-start(bf16[192,2048]{1,0:T(8,128)(2,1)} %collective-permute-done.23.refs_2_), channel_id=1, source_target_pairs={{0,2},{2,0},{4,6},{6,4},{8,10},{10,8},{12,14},{14,12},{16,18},{18,... | collective-permute-start | bytes 2359304 | tf_op jit(solution)/shard_map/ppermute | solution.py:407
  124.8 6.4 %collective-permute-start.37 = (bf16[192,2048]{1,0:T(8,128)(2,1)}, bf16[192,2048]{1,0:T(8,128)(2,1)S(1)}, u32[]{:S(2)}, u32[]{:S(2)}) collective-permute-start(bf16[192,2048]{1,0:T(8,128)(2,1)} %collective-permute-done.33.refs_6_), channel_id=1, source_target_pairs={{0,2},{2,0},{4,6},{6,4},{8,10},{10,8},{12,14},{14,12},{16,18},{18,... | collective-permute-start | bytes 2359304 | tf_op jit(solution)/shard_map/ppermute | solution.py:407
  130.2 19.3 %collective-permute-start.42 = (bf16[192,2048]{1,0:T(8,128)(2,1)}, bf16[192,2048]{1,0:T(8,128)(2,1)S(1)}, u32[]{:S(2)}, u32[]{:S(2)}) collective-permute-start(bf16[192,2048]{1,0:T(8,128)(2,1)} %collective-permute-done.32.refs_4_), channel_id=1, source_target_pairs={{0,4},{2,6},{4,0},{6,2},{8,12},{10,14},{12,8},{14,10},{16,20},{18,... | collective-permute-start | bytes 2359304 | tf_op jit(solution)/shard_map/ppermute | solution.py:407
  135.2 14.6 %collective-permute-start.38 = (bf16[64,2176]{1,0:T(8,128)(2,1)S(1)}, bf16[64,2176]{1,0:T(8,128)(2,1)S(1)}, u32[]{:S(2)}, u32[]{:S(2)}) collective-permute-start(bf16[64,2176]{1,0:T(8,128)(2,1)S(1)} %get-tuple-element.107), channel_id=1, source_target_pairs={{0,16},{2,18},{4,20},{6,22},{8,24},{10,26},{12,28},{14,30},{16,0},... | collective-permute-start | bytes 835592 | tf_op jit(solution)/shard_map/ppermute | solution.py:407
  136.1 15.1 %collective-permute-start.41 = (bf16[192,2048]{1,0:T(8,128)(2,1)}, bf16[192,2048]{1,0:T(8,128)(2,1)S(1)}, u32[]{:S(2)}, u32[]{:S(2)}) collective-permute-start(bf16[192,2048]{1,0:T(8,128)(2,1)} %collective-permute-done.32.refs_4_), channel_id=1, source_target_pairs={{0,2},{2,0},{4,6},{6,4},{8,10},{10,8},{12,14},{14,12},{16,18},{18,... | collective-permute-start | bytes 2359304 | tf_op jit(solution)/shard_map/ppermute | solution.py:407
  136.1 15.1 %collective-permute-start.39 = (bf16[192,2048]{1,0:T(8,128)(2,1)}, bf16[192,2048]{1,0:T(8,128)(2,1)S(1)}, u32[]{:S(2)}, u32[]{:S(2)}) collective-permute-start(bf16[192,2048]{1,0:T(8,128)(2,1)} %refs_0_.5), channel_id=1, source_target_pairs={{0,2},{2,0},{4,6},{6,4},{8,10},{10,8},{12,14},{14,12},{16,18},{18,... | collective-permute-start | bytes 2359304 | tf_op jit(solution)/shard_map/ppermute | solution.py:407
  136.6 14.6 %collective-permute-start.40 = (bf16[192,2048]{1,0:T(8,128)(2,1)}, bf16[192,2048]{1,0:T(8,128)(2,1)S(1)}, u32[]{:S(2)}, u32[]{:S(2)}) collective-permute-start(bf16[192,2048]{1,0:T(8,128)(2,1)} %collective-permute-done.24.refs_2_), channel_id=1, source_target_pairs={{0,2},{2,0},{4,6},{6,4},{8,10},{10,8},{12,14},{14,12},{16,18},{18,... | collective-permute-start | bytes 2359304 | tf_op jit(solution)/shard_map/ppermute | solution.py:407
  149.8 2.3 %collective-permute-start.43 = (bf16[192,2048]{1,0:T(8,128)(2,1)S(1)}, bf16[192,2048]{1,0:T(8,128)(2,1)S(1)}, u32[]{:S(2)}, u32[]{:S(2)}) collective-permute-start(bf16[192,2048]{1,0:T(8,128)(2,1)S(1)} %collective-permute-done.42.refs_6_), channel_id=1, source_target_pairs={{0,2},{2,0},{4,6},{6,4},{8,10},{10,8},{12,14},{14,12},{16,18},{18,... | collective-permute-start | bytes 2359304 | tf_op jit(solution)/shard_map/ppermute | solution.py:407
  149.8 20.0 %collective-permute-start.49 = (bf16[1024,384]{1,0:T(8,128)(2,1)S(1)}, bf16[1024,384]{1,0:T(8,128)(2,1)}, u32[]{:S(2)}, u32[]{:S(2)}) collective-permute-start(bf16[1024,384]{1,0:T(8,128)(2,1)S(1)} %collective-permute-done.17.refs_4_), channel_id=1, source_target_pairs={{0,4},{2,6},{4,0},{6,2},{8,12},{10,14},{12,8},{14,10},{16,20},{18,... | collective-permute-start | bytes 2359304 | tf_op jit(solution)/shard_map/ppermute | solution.py:407
  156.2 14.6 %collective-permute-start.44 = (bf16[64,2048]{1,0:T(8,128)(2,1)S(1)}, bf16[64,2048]{1,0:T(8,128)(2,1)S(1)}, u32[]{:S(2)}, u32[]{:S(2)}) collective-permute-start(bf16[64,2048]{1,0:T(8,128)(2,1)S(1)} %get-tuple-element.115), channel_id=1, source_target_pairs={{0,16},{2,18},{4,20},{6,22},{8,24},{10,26},{12,28},{14,30},{16,0},... | collective-permute-start | bytes 786440 | tf_op jit(solution)/shard_map/ppermute | solution.py:407
  156.3 29.1 %collective-permute-start.46 = (bf16[1024,384]{1,0:T(8,128)(2,1)S(1)}, bf16[1024,384]{1,0:T(8,128)(2,1)}, u32[]{:S(2)}, u32[]{:S(2)}) collective-permute-start(bf16[1024,384]{1,0:T(8,128)(2,1)S(1)} %pad_maximum_fusion.refs_0_), channel_id=1, source_target_pairs={{0,2},{2,0},{4,6},{6,4},{8,10},{10,8},{12,14},{14,12},{16,18},{18,... | collective-permute-start | bytes 2359304 | tf_op jit(solution)/shard_map/ppermute | solution.py:407
  156.5 29.0 %collective-permute-start.47 = (bf16[1024,384]{1,0:T(8,128)(2,1)S(1)}, bf16[1024,384]{1,0:T(8,128)(2,1)}, u32[]{:S(2)}, u32[]{:S(2)}) collective-permute-start(bf16[1024,384]{1,0:T(8,128)(2,1)S(1)} %collective-permute-done.25.refs_2_), channel_id=1, source_target_pairs={{0,2},{2,0},{4,6},{6,4},{8,10},{10,8},{12,14},{14,12},{16,18},{18,... | collective-permute-start | bytes 2359304 | tf_op jit(solution)/shard_map/ppermute | solution.py:407
  156.8 28.6 %collective-permute-start.48 = (bf16[1024,384]{1,0:T(8,128)(2,1)S(1)}, bf16[1024,384]{1,0:T(8,128)(2,1)}, u32[]{:S(2)}, u32[]{:S(2)}) collective-permute-start(bf16[1024,384]{1,0:T(8,128)(2,1)S(1)} %collective-permute-done.17.refs_4_), channel_id=1, source_target_pairs={{0,2},{2,0},{4,6},{6,4},{8,10},{10,8},{12,14},{14,12},{16,18},{18,... | collective-permute-start | bytes 2359304 | tf_op jit(solution)/shard_map/ppermute | solution.py:407
  170.8 14.7 %collective-permute-start.50 = (bf16[1024,384]{1,0:T(8,128)(2,1)}, bf16[1024,384]{1,0:T(8,128)(2,1)}, u32[]{:S(2)}, u32[]{:S(2)}) collective-permute-start(bf16[1024,384]{1,0:T(8,128)(2,1)} %collective-permute-done.49.refs_6_), channel_id=1, source_target_pairs={{0,2},{2,0},{4,6},{6,4},{8,10},{10,8},{12,14},{14,12},{16,18},{18,... | collective-permute-start | bytes 2359304 | tf_op jit(solution)/shard_map/ppermute | solution.py:407
  171.3 14.2 %collective-permute-start.45 = (bf16[64,2048]{1,0:T(8,128)(2,1)S(1)}, bf16[64,2048]{1,0:T(8,128)(2,1)S(1)}, u32[]{:S(2)}, u32[]{:S(2)}) collective-permute-start(bf16[64,2048]{1,0:T(8,128)(2,1)S(1)} %multiply_convert_fusion.own_ref), channel_id=1, source_target_pairs={{0,16},{2,18},{4,20},{6,22},{8,24},{10,26},{12,28},{14,30},{16,0},... | collective-permute-start | bytes 786440 | tf_op jit(solution)/shard_map/ppermute | solution.py:407
  190.1 6.9 %collective-permute-start.51 = (bf16[2,32,1536]{2,1,0:T(8,128)(2,1)S(1)}, bf16[2,32,1536]{2,1,0:T(8,128)(2,1)S(1)}, u32[]{:S(2)}, u32[]{:S(2)}) collective-permute-start(bf16[2,32,1536]{2,1,0:T(8,128)(2,1)S(1)} %dynamic-slice_bitcast_fusion), channel_id=1, source_target_pairs={{0,1},{1,0},{2,3},{3,2},{4,5},{5,4},{6,7},{7,6},{8,9},{9,8},{10,11... | collective-permute-start | bytes 589832 | tf_op jit(solution)/shard_map/ppermute | solution.py:412
  198.0 6.7 %collective-permute-start.52 = (bf16[32,1536]{1,0:T(8,128)(2,1)S(1)}, bf16[32,1536]{1,0:T(8,128)(2,1)S(1)}, u32[]{:S(2)}, u32[]{:S(2)}) collective-permute-start(bf16[32,1536]{1,0:T(8,128)(2,1)S(1)} %get-tuple-element.128), channel_id=1, source_target_pairs={{0,16},{2,18},{4,20},{6,22},{8,24},{10,26},{12,28},{14,30},{16,0},... | collective-permute-start | bytes 294920 | tf_op jit(solution)/shard_map/ppermute | solution.py:407
  (12 other events, 14.9 us)

commit v4 on v3

--- a/solution.py
+++ b/solution.py
@@ -94,12 +94,14 @@
 
 def prepared(x, keep, gain_ref, lhs_ref, coded_ref, squares_ref):
     rows, depth = x.shape
-    cuts = lhs_ref.shape[0]
-    wide = depth // cuts
     squares = jnp.broadcast_to(jnp.sum(x * x, axis=1, keepdims=True), (rows, 128))
     scaled = (x * gain_ref[...]).astype(BF)
-    for i in range(cuts):
-        lhs_ref[i] = scaled[:, i * wide : (i + 1) * wide]
+    if len(lhs_ref.shape) == 2:
+        lhs_ref[...] = scaled
+    else:
+        wide = lhs_ref.shape[2]
+        for i in range(lhs_ref.shape[0]):
+            lhs_ref[i] = scaled[:, i * wide : (i + 1) * wide]
     high = squares.astype(BF).astype(F32)
     lane = lax.broadcasted_iota(jnp.int32, (rows, 128), 1)
     coded_ref[...] = jnp.where(lane < 64, high, squares - high)[keep:].astype(BF)
@@ -125,10 +127,10 @@
     prepared(middle_ref[...].astype(F32), squares_ref.shape[0], gain_ref, lhs_ref, coded_ref, squares_ref)
 
 
-def prepare(kernel, row, operands, rows, depth, keep, cuts):
+def prepare(kernel, row, operands, rows, depth, keep, cuts, limit=VMEM):
     shapes = [
         jax.ShapeDtypeStruct((rows, depth), BF),
-        jax.ShapeDtypeStruct((cuts, rows, depth // cuts), BF),
+        jax.ShapeDtypeStruct((cuts, rows, depth // cuts) if cuts > 1 else (rows, depth), BF),
         jax.ShapeDtypeStruct((rows - keep, 128), BF),
         jax.ShapeDtypeStruct((keep, 128), F32),
     ]
@@ -143,55 +145,48 @@
             out_specs=[spec(x) for x in shapes],
         ),
         out_shape=shapes,
-        compiler_params=pltpu.CompilerParams(vmem_limit_bytes=VMEM),
+        compiler_params=pltpu.CompilerParams(vmem_limit_bytes=limit),
     )(row, *operands)
 
 
 def rows_kernel(place, lhs, coded_ref, *refs):
-    weights, (sent_ref, own_ref, held, sems) = refs[:-4], refs[-4:]
+    weights, (sent_ref, own_ref, held, sems) = refs[:OCT], refs[OCT:]
     block = held.shape[-1]
     keep, width = own_ref.shape
-    parts = len(weights) // OCT
-    steps = width // parts // block
+    wide = weights[0].shape[0]
+    steps = width // block
 
     def copies(step):
-        return [
-            pltpu.make_async_copy(
-                w.at[:, step * block : (step + 1) * block], held.at[step % 2, n], sems.at[step % 2, n]
+        for k, w in enumerate(weights):
+            at = pl.multiple_of((place[0] ^ k) * wide, wide)
+            yield pltpu.make_async_copy(
+                w.at[:, step * block : (step + 1) * block], held.at[step % 2, pl.ds(at, wide)], sems.at[step % 2, k]
             )
-            for n, w in enumerate(weights)
-        ]
-
-    pending = copies(0)
-    for c in pending:
+
+    for c in copies(0):
         c.start()
     if sent_ref.shape[1] > width:
         sent_ref[:, width:] = coded_ref[...]
     for step in range(steps):
-        following = copies(step + 1) if step + 1 < steps else []
-        for c in following:
-            c.start()
-        for i in range(parts):
-            total = None
-            for k in range(OCT):
-                pending[OCT * i + k].wait()
-                term = dot(lhs[place[0] ^ k], held[step % 2, OCT * i + k])
-                total = term if total is None else total + term
-            at = i * (width // parts) + step * block
-            own_ref[:, at : at + block] = total[:keep]
-            sent_ref[:, at : at + block] = total[keep:].astype(BF)
-        pending = following
+        if step + 1 < steps:
+            for c in copies(step + 1):
+                c.start()
+        for c in copies(step):
+            c.wait()
+        total = dot(lhs[...], held[step % 2])
+        at = step * block
+        own_ref[:, at : at + block] = total[:keep]
+        sent_ref[:, at : at + block] = total[keep:].astype(BF)
 
 
 def in_hbm(pieces):
     return [pl.BlockSpec(memory_space=pltpu.HBM)] * len(pieces)
 
 
-def rows_product(place, lhs, coded, pieces, each, block, with_squares):
-    _, rows, wide = lhs.shape
+def rows_product(place, lhs, coded, pieces, block, with_squares):
+    rows, depth = lhs.shape
     keep = rows // 2
-    count = len(pieces)
-    width = count // OCT * each
+    width = pieces[0].shape[1]
     sent = width + (128 if with_squares else 0)
     whole = lambda j, p: (0, 0)
     return pl.pallas_call(
@@ -199,10 +194,9 @@
         grid_spec=pltpu.PrefetchScalarGridSpec(
             num_scalar_prefetch=1,
             grid=(1,),
-            in_specs=[pl.BlockSpec(lhs.shape, lambda j, p: (0, 0, 0)), pl.BlockSpec(coded.shape, whole)]
-            + in_hbm(pieces),
+            in_specs=[pl.BlockSpec(lhs.shape, whole), pl.BlockSpec(coded.shape, whole)] + in_hbm(pieces),
             out_specs=[pl.BlockSpec((keep, sent), whole), pl.BlockSpec((keep, width), whole)],
-            scratch_shapes=[pltpu.VMEM((2, count, wide, block), BF), pltpu.SemaphoreType.DMA((2, count))],
+            scratch_shapes=[pltpu.VMEM((2, depth, block), BF), pltpu.SemaphoreType.DMA((2, OCT))],
         ),
         out_shape=[jax.ShapeDtypeStruct((keep, sent), BF), jax.ShapeDtypeStruct((keep, width), F32)],
         compiler_params=pltpu.CompilerParams(vmem_limit_bytes=VMEM),
@@ -252,6 +246,14 @@
     )(place, lhs, coded, *pieces)
 
 
+def stacked(a_ref, own_ref, got_ref):
+    keep, depth = own_ref.shape
+    for h in range(2):
+        columns = slice(h * depth // 2, (h + 1) * depth // 2)
+        a_ref[2 * h * keep : (2 * h + 1) * keep] = own_ref[:, columns]
+        a_ref[(2 * h + 1) * keep : (2 * h + 2) * keep] = got_ref[:, columns]
+
+
 def columns_kernel(place, own_ref, got_ref, *refs):
     weights, (out_ref, parts, a_ref, held, sems) = refs[:OCT], refs[OCT:]
     keep, depth = own_ref.shape
@@ -259,13 +261,11 @@
     copies = [pltpu.make_async_copy(w, held.at[n], sems.at[n]) for n, w in enumerate(weights)]
     for c in copies:
         c.start()
-    a_ref[:keep] = own_ref[...]
-    a_ref[keep:] = got_ref[...]
+    stacked(a_ref, own_ref, got_ref)
     for k in range(OCT):
         copies[k].wait()
-        lower = dot(a_ref[:, : depth // 2], held[k])
-        upper = dot(a_ref[:, depth // 2 :], held[k])
-        parts[place[0] ^ k] = (lower[:, :wide] + upper[:, wide:]).astype(BF)
+        both = dot(a_ref[...], held[k])
+        parts[place[0] ^ k] = (both[: 2 * keep, :wide] + both[2 * keep :, wide:]).astype(BF)
     for i in range(OCT):
         out_ref[:, i * wide : (i + 1) * wide] = parts[i]
 
@@ -285,7 +285,7 @@
             out_specs=pl.BlockSpec((rows, OCT * wide), whole),
             scratch_shapes=[
                 pltpu.VMEM((OCT, rows, wide), BF),
-                pltpu.VMEM((rows, depth), BF),
+                pltpu.VMEM((2 * rows, depth // 2), BF),
                 pltpu.VMEM((OCT, deep, double), BF),
                 pltpu.SemaphoreType.DMA((OCT,)),
             ],
@@ -298,13 +298,11 @@
 def out_kernel(place, own_ref, got_ref, *refs):
     weights, (out_ref, parts, a_ref) = refs[:OCT], refs[OCT:]
     keep, depth = own_ref.shape
-    a_ref[:keep] = own_ref[...]
-    a_ref[keep:] = got_ref[...]
+    stacked(a_ref, own_ref, got_ref)
     wide = weights[0].shape[-1] // 2
     for k in range(OCT):
-        lower = dot(a_ref[:, : depth // 2], weights[k][...])
-        upper = dot(a_ref[:, depth // 2 :], weights[k][...])
-        parts[place[0] ^ k] = (lower[:, :wide] + upper[:, wide:]).astype(BF)
+        both = dot(a_ref[...], weights[k][...])
+        parts[place[0] ^ k] = (both[: 2 * keep, :wide] + both[2 * keep :, wide:]).astype(BF)
     for i in range(OCT):
         out_ref[:, i * wide : (i + 1) * wide] = parts[i]
 
@@ -322,7 +320,7 @@
             grid=(1,),
             in_specs=[pl.BlockSpec((keep, depth), whole)] * 2 + [pl.BlockSpec((deep, double), whole)] * OCT,
             out_specs=pl.BlockSpec((rows, OCT * wide), whole),
-            scratch_shapes=[pltpu.VMEM((OCT, rows, wide), BF), pltpu.VMEM((rows, depth), BF)],
+            scratch_shapes=[pltpu.VMEM((OCT, rows, wide), BF), pltpu.VMEM((2 * rows, depth // 2), BF)],
         ),
         out_shape=jax.ShapeDtypeStruct((rows, OCT * wide), BF),
         compiler_params=pltpu.CompilerParams(vmem_limit_bytes=VMEM_ALL),
@@ -455,39 +453,38 @@
         o_own, d_own = lax.optimization_barrier((beside(w_out), beside(w_down)))
         x_o = near(o_own)
         both = jnp.stack([cut[0], *came])
-        gate, down, z_own, given = lax.optimization_barrier((w_gate, d_own, o_own, cut[4], both))[:4]
+        gate, up, z_own, given = lax.optimization_barrier((w_gate, w_up, o_own, cut[4], both))[:4]
         partner = across(given)
-        z_o, z_g, z_d = next_to(z_own), next_to(gate), next_to(down)
+        z_o, z_g, z_u = next_to(z_own), next_to(gate), next_to(up)
         mine_too = jnp.stack([columns_of(side, half), partner])
         others_too = other_head(mine_too)
         others = other_head(after(both, x_q, gain1, gain2, *tables, z_g, others_too))
         _, lhs, coded, squares = prepare(
-            first_kernel, at_row, (both, others, gain1), 8 * mine, quarter, 2 * mine, QUAD
+            first_kernel, at_row, (both, others, gain1), 8 * mine, quarter, 2 * mine, QUAD, VMEM_ALL
         )
         x_gate, x_up, x_down = lax.optimization_barrier((w_gate, w_up, d_own, x_q, x_k, x_v, x_o, both))[:3]
         x_g, x_u, x_d = near(x_gate), near(x_up), near(x_down)
         pieces = [p for w, x in ((w_query, x_q), (w_key, x_k), (w_value, x_v)) for p in (w, core(w), x, core(x))]
         *sent, own = first_rows_product(place4, after(lhs, partner), coded, pieces, 384)
-        *sent, _ = lax.optimization_barrier((*sent, z_o, z_d))[:4]
+        *sent, _ = lax.optimization_barrier((*sent, z_o, z_u))[:4]
         got = [turns[k + 1](sent[k]) for k in range(3)]
         d_o = near(after(z_o, sent[0]))
         got = lax.optimization_barrier((*got, d_o, x_g, x_u, x_d))[:3]
         p_o = all_pieces(o_own, x_o, z_o, d_o, (sent[0],), (sent[0],))
         attended, cache_keys, cache_values = attend(model, own, got, squares, tables, segment_ids[0], cache_slot[0])
-        d_g = near(after(z_g, attended))
+        d_g, d_u = near(after(z_g, attended)), near(after(z_u, attended))
         got = across(attended)
-        z_u = next_to(after(w_up, got))
+        z_d = next_to(after(d_own, got))
         terms = out_product(place, attended, got, p_o)
         others = other_head(terms)
         p_g = all_pieces(w_gate, x_g, z_g, d_g, (attended,), (others,))
         middle, lhs, coded, squares = prepare(
-            middle_kernel, at_row, (mine_too, others_too, terms, after(others, z_u, d_g), gain2), 4 * mine, half, 2 * mine, OCT
+            middle_kernel, at_row, (mine_too, others_too, terms, after(others, z_d, d_g), gain2), 4 * mine, half, 2 * mine, 1
         )
-        d_u = near(after(z_u, lhs))
-        sent_g, own_g = rows_product(place, lhs, coded, p_g, units, 512, True)
+        sent_g, own_g = rows_product(place, lhs, coded, p_g, 512, True)
         got_g = across(sent_g)
         p_u = all_pieces(w_up, x_u, z_u, d_u, (lhs,), (got_g,))
-        sent_u, own_u = rows_product(place, after(lhs, sent_g), coded, p_u, units, 512, False)
+        sent_u, own_u = rows_product(place, after(lhs, sent_g), coded, p_u, 512, False)
         got_u = across(sent_u)
         d_d = near(after(z_d, sent_g))
         p_d = all_pieces(d_own, x_d, z_d, d_d, (sent_u,), (got_u,))

time: 206 us -> 203 us (0.985)
  local copies, waits for them, and re-layouts: 11.8 us -> 8.53 us
  starting transfers between devices: 34.9 us -> 38 us
  waiting for transfers between devices: 124 us -> 121 us
    ppermute x43, waiting for transfers between devices: 101 us -> 97.6 us  [swap(): return lambda x: lax.ppermute(x, 'group', pairs)]
    unnamed x50 -> x34, local copies, waits for them, and re-layouts: 6.16 us -> 3.67 us
    ppermute x43, starting transfers between devices: 19.5 us -> 21.8 us  [swap(): return lambda x: lax.ppermute(x, 'group', pairs)]
  transfers between devices with their start and end apart: 53 -> 53, of which waited for: 23 -> 22; matrix products, arithmetic and copies ran while one was open for 6% -> 5% of each run, Pallas kernels for 11% -> 11%
where the time goes in v4:
time: 203 us
  waiting for transfers between devices  121 us (60%)
  starting transfers between devices  38 us (19%)
  Pallas kernels  27.5 us (14%)
  local copies, waits for them, and re-layouts  8.53 us (4%)
  other arithmetic  6.75 us (3%)
    ppermute x43, waiting for transfers between devices, swap(): return lambda x: lax.ppermute(x, 'group', pairs)  97.6 us
    ppermute x43, starting transfers between devices, swap(): return lambda x: lax.ppermute(x, 'group', pairs)  21.8 us
    ppermute x4, waiting for transfers between devices, other_head(): return lax.ppermute(x, 'head', [(0, 1), (1, 0)])  21.2 us
    ppermute x6, starting transfers between devices, turn(): return lambda x: lax.ppermute(x, 'group', pairs)  10.9 us
    pallas_call x2, Pallas kernels, rows_product(): pl.pallas_call(rows_kernel, grid_spec=pltpu.PrefetchScalarGridSpec(num_sc...  7.6 us
    ppermute x4, starting transfers between devices, other_head(): return lax.ppermute(x, 'head', [(0, 1), (1, 0)])  5.29 us
    pallas_call x1, Pallas kernels, first_rows_product(): pl.pallas_call(first_rows_kernel, grid_spec=pltpu.PrefetchScalarGridSpec(...  5.09 us
    pallas_call x1, Pallas kernels, columns_product(): pl.pallas_call(columns_kernel, grid_spec=pltpu.PrefetchScalarGridSpec(num...  4.95 us
  transfers between devices with their start and end apart: 53, of which 22 were waited for; matrix products, arithmetic and copies ran while one was open for 5% of the time, Pallas kernels for 11%

profile of v4, /device:TPU:0, one launch (start us, length us, event | category | flops | bytes accessed | tf_op | source)
XLA Modules:
  0.0 202.8 jit_solution(81975528711375255)
XLA Ops:
  0.6 3.0 %collective-permute-start.11 = (bf16[192,768]{1,0:T(8,128)(2,1)}, bf16[192,768]{1,0:T(8,128)(2,1)}, u32[]{:S(2)}, u32[]{:S(2)}) collective-permute-start(bf16[192,768]{1,0:T(8,128)(2,1)} %refs_4_.1), channel_id=1, source_target_pairs={{0,4},{2,6},{4,0},{6,2},{8,12},{10,14},{12,8},{14,10},{16,20},{18,... | collective-permute-start | bytes 884744 | tf_op jit(solution)/shard_map/ppermute | solution.py:405
  3.6 1.0 dynamic-slice_bitcast_fusion.1
  4.6 1.5 constant_dynamic-slice_fusion.1
  6.1 3.6 %collective-permute-start = (bf16[32,768]{1,0:T(8,128)(2,1)}, bf16[32,768]{1,0:T(8,128)(2,1)S(1)}, u32[]{:S(2)}, u32[]{:S(2)}) collective-permute-start(bf16[32,768]{1,0:T(8,128)(2,1)} %get-tuple-element.67), channel_id=1, source_target_pairs={{0,24},{2,26},{4,28},{6,30},{8,0},{10,2},{12,4},{14,6},{16,8},{18,... | collective-permute-start | bytes 147464 | tf_op jit(solution)/shard_map/ppermute | solution.py:424
  9.7 1.0 collective-permute-start.2
  11.2 0.5 copy-done.11
  12.5 0.8 pad_maximum_fusion.1.refs_0_
  13.3 0.5 collective-permute-start.5
  13.8 2.2 %collective-permute-done.1 = bf16[32,768]{1,0:T(8,128)(2,1)} collective-permute-done((bf16[32,768]{1,0:T(8,128)(2,1)}, bf16[32,768]{1,0:T(8,128)(2,1)}, u32[]{:S(2)}, u32[]{:S(2)}) %collective-permute-start.1) | collective-permute-done | bytes 49184 | tf_op jit(solution)/shard_map/ppermute | solution.py:424
  16.0 0.5 collective-permute-start.14
  16.6 1.5 pad_maximum_fusion.2.mine_ref
  18.1 1.2 collective-permute-start.3
  19.3 5.5 %collective-permute-done.3 = bf16[32,1536]{1,0:T(8,128)(2,1)S(1)} collective-permute-done((bf16[32,1536]{1,0:T(8,128)(2,1)S(1)}, bf16[32,1536]{1,0:T(8,128)(2,1)S(1)}, u32[]{:S(2)}, u32[]{:S(2)}) %collective-permute-start.3) | collective-permute-done | bytes 98336 | tf_op jit(solution)/shard_map/ppermute | solution.py:405
  25.4 1.1 collective-permute-start.22
  26.6 3.2 %collective-permute-done.14.refs_10_ = bf16[192,768]{1,0:T(8,128)(2,1)S(1)} collective-permute-done((bf16[192,768]{1,0:T(8,128)(2,1)}, bf16[192,768]{1,0:T(8,128)(2,1)S(1)}, u32[]{:S(2)}, u32[]{:S(2)}) %collective-permute-start.14) | collective-permute-done | bytes 294944 | tf_op jit(solution)/shard_map/ppermute | solution.py:405
  30.3 4.5 %collective-permute-done.22.refs_2_ = bf16[384,384]{1,0:T(8,128)(2,1)} collective-permute-done((bf16[384,384]{1,0:T(8,128)(2,1)}, bf16[384,384]{1,0:T(8,128)(2,1)}, u32[]{:S(2)}, u32[]{:S(2)}) %collective-permute-start.22) | collective-permute-done | bytes 294944 | tf_op jit(solution)/shard_map/ppermute | solution.py:405
  34.8 1.5 collective-permute-start.4
  36.4 2.5 %collective-permute-start.17 = (bf16[192,2048]{1,0:T(8,128)(2,1)S(1)}, bf16[192,2048]{1,0:T(8,128)(2,1)}, u32[]{:S(2)}, u32[]{:S(2)}) collective-permute-start(bf16[192,2048]{1,0:T(8,128)(2,1)S(1)} %copy-done.2), channel_id=1, source_target_pairs={{0,8},{2,10},{4,12},{6,14},{8,0},{10,2},{12,4},{14,6},{16,24},{18,... | collective-permute-start | bytes 2359304 | tf_op jit(solution)/shard_map/ppermute | solution.py:405
  38.9 0.5 collective-permute-start.23
  39.5 1.0 collective-permute-done.4.others_ref
  40.5 0.5 collective-permute-start.24
  41.1 2.3 %collective-permute-done.6.refs_4_ = bf16[192,2048]{1,0:T(8,128)(2,1)} collective-permute-done((bf16[192,2048]{1,0:T(8,128)(2,1)S(1)}, bf16[192,2048]{1,0:T(8,128)(2,1)}, u32[]{:S(2)}, u32[]{:S(2)}) %collective-permute-start.6) | collective-permute-done | bytes 786464 | tf_op jit(solution)/shard_map/ppermute | solution.py:405
  43.4 0.8 dynamic_slice.40
  44.2 0.6 reshape.121.gain_ref
  44.9 1.6 fusion.2
  46.5 2.5 %collective-permute-start.7 = (bf16[4,32,768]{2,1,0:T(8,128)(2,1)}, bf16[4,32,768]{2,1,0:T(8,128)(2,1)}, u32[]{:S(2)}, u32[]{:S(2)}) collective-permute-start(bf16[4,32,768]{2,1,0:T(8,128)(2,1)} %pad_maximum_fusion.2.mine_ref), channel_id=1, source_target_pairs={{0,1},{1,0},{2,3},{3,2},{4,5},{5,4},{6,7},{7,6},{8,9},{9,8},{10,11... | collective-permute-start | bytes 589832 | tf_op jit(solution)/shard_map/ppermute | solution.py:410
  49.0 2.2 %collective-permute-start.25 = (bf16[1024,384]{1,0:T(8,128)(2,1)S(1)}, bf16[1024,384]{1,0:T(8,128)(2,1)S(1)}, u32[]{:S(2)}, u32[]{:S(2)}) collective-permute-start(bf16[1024,384]{1,0:T(8,128)(2,1)S(1)} %pad_maximum_fusion.refs_0_), channel_id=1, source_target_pairs={{0,4},{2,6},{4,0},{6,2},{8,12},{10,14},{12,8},{14,10},{16,20},{18,... | collective-permute-start | bytes 2359304 | tf_op jit(solution)/shard_map/ppermute | solution.py:405
  51.2 3.6 %collective-permute-done.7.others_ref = bf16[4,32,768]{2,1,0:T(8,128)(2,1)} collective-permute-done((bf16[4,32,768]{2,1,0:T(8,128)(2,1)}, bf16[4,32,768]{2,1,0:T(8,128)(2,1)}, u32[]{:S(2)}, u32[]{:S(2)}) %collective-permute-start.7) | collective-permute-done | bytes 196640 | tf_op jit(solution)/shard_map/ppermute | solution.py:410
  54.9 1.1 collective-permute-start.16
  56.0 2.1 %shard_map.139 = (bf16[256,768]{1,0:T(8,128)(2,1)}, bf16[4,256,192]{2,1,0:T(8,128)(2,1)}, bf16[192,128]{1,0:T(8,128)(2,1)}, f32[64,128]{1,0:T(8,128)}) custom-call(s32[1]{0:T(128)} %bitcast.row, bf16[4,32,768]{2,1,0:T(8,128)(2,1)} %pad_maximum_fusion.2.mine_ref, bf16[4,32,768]{2,1,0:T(8,128)(2,1)} %collective-permute-done.7.others_ref, ...), custom_call_target="tpu_custom_call" | custom-call | tf_op jit(solution)/shard_map/pallas_call | solution.py:139
  58.1 5.1 %shard_map.140 = (bf16[64,2432]{1,0:T(8,128)(2,1)}, bf16[64,2432]{1,0:T(8,128)(2,1)}, bf16[64,2432]{1,0:T(8,128)(2,1)}, f32[64,2304]{1,0:T(8,128)}) custom-call(s32[1]{0:T(128)} %bitcast.8.place, bf16[4,256,192]{2,1,0:T(8,128)(2,1)} %get-tuple-element.74.lhs, bf16[192,128]{1,0:T(8,128)(2,1)} %get-tuple-element.75.coded_ref, bf16[192,768]{1,0:T(8,128)(2,1)} %refs_0_.3, ...), custom_call_target="tpu_custom_call" | custom-call | tf_op jit(solution)/shard_map/pallas_call | solution.py:235
  63.2 0.9 collective-permute-done.16.refs_4_
  64.1 1.5 collective-permute-start.18
  65.5 3.6 %collective-permute-start.19 = (bf16[64,2432]{1,0:T(8,128)(2,1)}, bf16[64,2432]{1,0:T(8,128)(2,1)}, u32[]{:S(2)}, u32[]{:S(2)}) collective-permute-start(bf16[64,2432]{1,0:T(8,128)(2,1)} %get-tuple-element.83), channel_id=1, source_target_pairs={{0,16},{2,18},{4,20},{6,22},{8,24},{10,26},{12,28},{14,30},{16,0},... | collective-permute-start | bytes 933896 | tf_op jit(solution)/shard_map/ppermute | solution.py:424
  69.2 1.2 collective-permute-start.20
  70.4 6.0 %collective-permute-done.24.refs_2_ = bf16[192,2048]{1,0:T(8,128)(2,1)} collective-permute-done((bf16[192,2048]{1,0:T(8,128)(2,1)S(1)}, bf16[192,2048]{1,0:T(8,128)(2,1)}, u32[]{:S(2)}, u32[]{:S(2)}) %collective-permute-start.24) | collective-permute-done | bytes 786464 | tf_op jit(solution)/shard_map/ppermute | solution.py:405
  76.4 0.5 collective-permute-start.21
  76.9 16.2 %collective-permute-done.25.refs_2_ = bf16[1024,384]{1,0:T(8,128)(2,1)S(1)} collective-permute-done((bf16[1024,384]{1,0:T(8,128)(2,1)S(1)}, bf16[1024,384]{1,0:T(8,128)(2,1)S(1)}, u32[]{:S(2)}, u32[]{:S(2)}) %collective-permute-start.25) | collective-permute-done | bytes 786464 | tf_op jit(solution)/shard_map/ppermute | solution.py:405
  93.1 0.7 copy.28.refs_9_
  93.8 2.9 %collective-permute-done.21.refs_6_ = bf16[384,384]{1,0:T(8,128)(2,1)} collective-permute-done((bf16[384,384]{1,0:T(8,128)(2,1)}, bf16[384,384]{1,0:T(8,128)(2,1)}, u32[]{:S(2)}, u32[]{:S(2)}) %collective-permute-start.21) | collective-permute-done | bytes 294944 | tf_op jit(solution)/shard_map/ppermute | solution.py:405
  96.7 3.7 %shard_map.141 = (bf16[64,768]{1,0:T(8,128)(2,1)}, bf16[64,768]{1,0:T(8,128)(2,1)}, bf16[64,768]{1,0:T(8,128)(2,1)}) custom-call(f32[64,2304]{1,0:T(8,128)} %get-tuple-element.76.refs_0_, bf16[64,2432]{1,0:T(8,128)(2,1)} %collective-permute-done.18.refs_1_, bf16[64,2432]{1,0:T(8,128)(2,1)} %collective-permute-done.19.refs_2_, ...), custom_call_target="tpu_custom_call" | custom-call | tf_op jit(solution)/shard_map/pallas_call | solution.py:381
  100.4 1.2 collective-permute-start.26
  102.7 4.4 %collective-permute-done.26.got_ref = bf16[64,768]{1,0:T(8,128)(2,1)S(1)} collective-permute-done((bf16[64,768]{1,0:T(8,128)(2,1)}, bf16[64,768]{1,0:T(8,128)(2,1)S(1)}, u32[]{:S(2)}, u32[]{:S(2)}) %collective-permute-start.26) | collective-permute-done | bytes 98336 | tf_op jit(solution)/shard_map/ppermute | solution.py:405
  107.0 0.6 copy-done.12
  107.7 1.2 collective-permute-done.30.refs_7_
  108.9 3.7 %shard_map.142.a_ref = bf16[128,1536]{1,0:T(8,128)(2,1)} custom-call(s32[1]{0:T(128)} %bitcast.7.place, bf16[64,768]{1,0:T(8,128)(2,1)} %get-tuple-element.94.own_ref, bf16[64,768]{1,0:T(8,128)(2,1)} %copy-done.12, bf16[384,384]{1,0:T(8,128)(2,1)} %pad_maximum_fusion.1.refs_0_, bf16[384,384]{1,0:T(8,128)(2,1)} %collective-permute-done.27.refs_1_, ...), custom_call_target="tpu_custom_call" | custom-call | tf_op jit(solution)/shard_map/pallas_call | solution.py:316
  113.7 10.4 %collective-permute-done.31.b_ref = bf16[128,1536]{1,0:T(8,128)(2,1)S(1)} collective-permute-done((bf16[128,1536]{1,0:T(8,128)(2,1)}, bf16[128,1536]{1,0:T(8,128)(2,1)S(1)}, u32[]{:S(2)}, u32[]{:S(2)}) %collective-permute-start.31) | collective-permute-done | bytes 393248 | tf_op jit(solution)/shard_map/ppermute | solution.py:410
  124.6 2.4 %collective-permute-done.32.refs_4_ = bf16[1024,384]{1,0:T(8,128)(2,1)S(1)} collective-permute-done((bf16[1024,384]{1,0:T(8,128)(2,1)S(1)}, bf16[1024,384]{1,0:T(8,128)(2,1)S(1)}, u32[]{:S(2)}, u32[]{:S(2)}) %collective-permute-start.32) | collective-permute-done | bytes 786464 | tf_op jit(solution)/shard_map/ppermute | solution.py:405
  127.5 1.0 copy-done
  128.9 0.7 copy-done.4
  129.6 3.9 %shard_map.144 = (bf16[64,2176]{1,0:T(8,128)(2,1)S(1)}, f32[64,2048]{1,0:T(8,128)S(1)}) custom-call(s32[1]{0:T(128)} %bitcast.7.place, bf16[128,1536]{1,0:T(8,128)(2,1)S(1)} %get-tuple-element.110.lhs, bf16[64,128]{1,0:T(8,128)(2,1)S(1)} %get-tuple-element.103.coded_ref, bf16[192,2048]{1,0:T(8,128)(2,1)S(1)} %copy-done.1, ...), custom_call_target="tpu_custom_call" | custom-call | tf_op jit(solution)/shard_map/pallas_call | solution.py:192
  134.5 11.1 %collective-permute-done.42.refs_6_ = bf16[192,2048]{1,0:T(8,128)(2,1)S(1)} collective-permute-done((bf16[192,2048]{1,0:T(8,128)(2,1)}, bf16[192,2048]{1,0:T(8,128)(2,1)S(1)}, u32[]{:S(2)}, u32[]{:S(2)}) %collective-permute-start.42) | collective-permute-done | bytes 786464 | tf_op jit(solution)/shard_map/ppermute | solution.py:405
  145.6 2.1 %collective-permute-done.38 = bf16[64,2176]{1,0:T(8,128)(2,1)S(1)} collective-permute-done((bf16[64,2176]{1,0:T(8,128)(2,1)S(1)}, bf16[64,2176]{1,0:T(8,128)(2,1)S(1)}, u32[]{:S(2)}, u32[]{:S(2)}) %collective-permute-start.38) | collective-permute-done | bytes 278560 | tf_op jit(solution)/shard_map/ppermute | solution.py:405
  147.7 1.5 collective-permute-start.49
  149.2 0.8 collective-permute-done.43.refs_7_
  150.0 3.7 %shard_map.145 = (bf16[64,2048]{1,0:T(8,128)(2,1)S(1)}, f32[64,2048]{1,0:T(8,128)S(1)}) custom-call(s32[1]{0:T(128)} %bitcast.7.place, bf16[128,1536]{1,0:T(8,128)(2,1)S(1)} %get-tuple-element.110.lhs, bf16[64,128]{1,0:T(8,128)(2,1)S(1)} %get-tuple-element.103.coded_ref, bf16[192,2048]{1,0:T(8,128)(2,1)S(1)} %copy-done.3, ...), custom_call_target="tpu_custom_call" | custom-call | tf_op jit(solution)/shard_map/pallas_call | solution.py:192
  154.5 13.2 %collective-permute-done.49.refs_6_ = bf16[1024,384]{1,0:T(8,128)(2,1)} collective-permute-done((bf16[1024,384]{1,0:T(8,128)(2,1)S(1)}, bf16[1024,384]{1,0:T(8,128)(2,1)}, u32[]{:S(2)}, u32[]{:S(2)}) %collective-permute-start.49) | collective-permute-done | bytes 786464 | tf_op jit(solution)/shard_map/ppermute | solution.py:405
  168.3 14.6 %collective-permute-done.45.got_ref = bf16[64,2048]{1,0:T(8,128)(2,1)S(1)} collective-permute-done((bf16[64,2048]{1,0:T(8,128)(2,1)S(1)}, bf16[64,2048]{1,0:T(8,128)(2,1)S(1)}, u32[]{:S(2)}, u32[]{:S(2)}) %collective-permute-start.45) | collective-permute-done | bytes 262176 | tf_op jit(solution)/shard_map/ppermute | solution.py:405
  183.0 5.0 %shard_map.146 = bf16[128,1536]{1,0:T(8,128)(2,1)S(1)} custom-call(s32[1]{0:T(128)} %bitcast.7.place, bf16[64,2048]{1,0:T(8,128)(2,1)S(1)} %multiply_convert_fusion.own_ref, bf16[64,2048]{1,0:T(8,128)(2,1)S(1)} %collective-permute-done.45.got_ref, bf16[1024,384]{1,0:T(8,128)(2,1)S(1)} %pad_maximum_fusion.refs_0_, ...), custom_call_target="tpu_custom_call" | custom-call | tf_op jit(solution)/shard_map/pallas_call | solution.py:279
  188.0 0.7 collective-permute-start.51
  188.7 6.2 %collective-permute-done.51 = bf16[2,32,1536]{2,1,0:T(8,128)(2,1)S(1)} collective-permute-done((bf16[2,32,1536]{2,1,0:T(8,128)(2,1)S(1)}, bf16[2,32,1536]{2,1,0:T(8,128)(2,1)S(1)}, u32[]{:S(2)}, u32[]{:S(2)}) %collective-permute-start.51) | collective-permute-done | bytes 196640 | tf_op jit(solution)/shard_map/ppermute | solution.py:410
  194.9 1.0 fusion.1
  196.0 6.0 %collective-permute-done.52 = bf16[32,1536]{1,0:T(8,128)(2,1)S(1)} collective-permute-done((bf16[32,1536]{1,0:T(8,128)(2,1)S(1)}, bf16[32,1536]{1,0:T(8,128)(2,1)S(1)}, u32[]{:S(2)}, u32[]{:S(2)}) %collective-permute-start.52) | collective-permute-done | bytes 98336 | tf_op jit(solution)/shard_map/ppermute | solution.py:405
  202.1 0.7 maximum_select_fusion
  (113 shorter events, 8.4 us)
Async XLA Ops:
  0.6 10.1 %copy-start.5 = (bf16[2048,192]{0,1:T(8,128)(2,1)S(1)}, bf16[2048,192]{0,1:T(8,128)(2,1)}, u32[]{:S(2)}) copy-start(bf16[2048,192]{0,1:T(8,128)(2,1)} %param.21) | copy-start | bytes 2359300
  0.6 25.8 %collective-permute-start.11 = (bf16[192,768]{1,0:T(8,128)(2,1)}, bf16[192,768]{1,0:T(8,128)(2,1)}, u32[]{:S(2)}, u32[]{:S(2)}) collective-permute-start(bf16[192,768]{1,0:T(8,128)(2,1)} %refs_4_.1), channel_id=1, source_target_pairs={{0,4},{2,6},{4,0},{6,2},{8,12},{10,14},{12,8},{14,10},{16,20},{18,... | collective-permute-start | bytes 884744 | tf_op jit(solution)/shard_map/ppermute | solution.py:405
  3.6 26.1 %collective-permute-start.10 = (bf16[192,768]{1,0:T(8,128)(2,1)}, bf16[192,768]{1,0:T(8,128)(2,1)}, u32[]{:S(2)}, u32[]{:S(2)}) collective-permute-start(bf16[192,768]{1,0:T(8,128)(2,1)} %refs_4_.1), channel_id=1, source_target_pairs={{0,2},{2,0},{4,6},{6,4},{8,10},{10,8},{12,14},{14,12},{16,18},{18,... | collective-permute-start | bytes 884744 | tf_op jit(solution)/shard_map/ppermute | solution.py:405
  6.1 7.2 %collective-permute-start = (bf16[32,768]{1,0:T(8,128)(2,1)}, bf16[32,768]{1,0:T(8,128)(2,1)S(1)}, u32[]{:S(2)}, u32[]{:S(2)}) collective-permute-start(bf16[32,768]{1,0:T(8,128)(2,1)} %get-tuple-element.67), channel_id=1, source_target_pairs={{0,24},{2,26},{4,28},{6,30},{8,0},{10,2},{12,4},{14,6},{16,8},{18,... | collective-permute-start | bytes 147464 | tf_op jit(solution)/shard_map/ppermute | solution.py:424
  9.7 6.3 %collective-permute-start.1 = (bf16[32,768]{1,0:T(8,128)(2,1)}, bf16[32,768]{1,0:T(8,128)(2,1)}, u32[]{:S(2)}, u32[]{:S(2)}) collective-permute-start(bf16[32,768]{1,0:T(8,128)(2,1)} %get-tuple-element.68), channel_id=1, source_target_pairs={{0,16},{2,18},{4,20},{6,22},{8,24},{10,26},{12,28},{14,30},{16,0},... | collective-permute-start | bytes 147464 | tf_op jit(solution)/shard_map/ppermute | solution.py:424
  9.7 6.8 %collective-permute-start.2 = (bf16[32,768]{1,0:T(8,128)(2,1)S(1)}, bf16[32,768]{1,0:T(8,128)(2,1)}, u32[]{:S(2)}, u32[]{:S(2)}) collective-permute-start(bf16[32,768]{1,0:T(8,128)(2,1)S(1)} %get-tuple-element.69), channel_id=1, source_target_pairs={{0,8},{2,10},{4,12},{6,14},{8,16},{10,18},{12,20},{14,22},{16,24},... | collective-permute-start | bytes 147464 | tf_op jit(solution)/shard_map/ppermute | solution.py:424
  12.1 7.2 %copy-start.14 = (s32[1,64]{1,0:T(1,128)S(1)}, s32[1,64]{1,0:T(1,128)}, u32[]{:S(2)}) copy-start(s32[1,64]{1,0:T(1,128)} %refs_8_.3) | copy-start | bytes 772
  12.4 12.4 %copy-start.1 = (bf16[192,2048]{1,0:T(8,128)(2,1)S(1)}, bf16[192,2048]{1,0:T(8,128)(2,1)}, u32[]{:S(2)}) copy-start(bf16[192,2048]{1,0:T(8,128)(2,1)} %refs_0_.4) | copy-start | bytes 2359300
  12.4 23.9 %copy-start.2 = (bf16[192,2048]{1,0:T(8,128)(2,1)S(1)}, bf16[192,2048]{1,0:T(8,128)(2,1)}, u32[]{:S(2)}) copy-start(bf16[192,2048]{1,0:T(8,128)(2,1)} %refs_0_.5) | copy-start | bytes 2359300
  12.4 32.3 %copy-start.13 = (f32[3072]{0:T(1024)S(1)}, f32[3072]{0:T(1024)}, u32[]{:S(2)}) copy-start(f32[3072]{0:T(1024)} %param.18) | copy-start | bytes 36868
  13.3 12.0 %collective-permute-start.5 = (bf16[192,768]{1,0:T(8,128)(2,1)}, bf16[192,768]{1,0:T(8,128)(2,1)S(1)}, u32[]{:S(2)}, u32[]{:S(2)}) collective-permute-start(bf16[192,768]{1,0:T(8,128)(2,1)} %refs_0_.3), channel_id=1, source_target_pairs={{0,4},{2,6},{4,0},{6,2},{8,12},{10,14},{12,8},{14,10},{16,20},{18,... | collective-permute-start | bytes 884744 | tf_op jit(solution)/shard_map/ppermute | solution.py:405
  16.0 13.7 %collective-permute-start.14 = (bf16[192,768]{1,0:T(8,128)(2,1)}, bf16[192,768]{1,0:T(8,128)(2,1)S(1)}, u32[]{:S(2)}, u32[]{:S(2)}) collective-permute-start(bf16[192,768]{1,0:T(8,128)(2,1)} %refs_8_.2), channel_id=1, source_target_pairs={{0,4},{2,6},{4,0},{6,2},{8,12},{10,14},{12,8},{14,10},{16,20},{18,... | collective-permute-start | bytes 884744 | tf_op jit(solution)/shard_map/ppermute | solution.py:405
  18.1 6.7 %collective-permute-start.3 = (bf16[32,1536]{1,0:T(8,128)(2,1)S(1)}, bf16[32,1536]{1,0:T(8,128)(2,1)S(1)}, u32[]{:S(2)}, u32[]{:S(2)}) collective-permute-start(bf16[32,1536]{1,0:T(8,128)(2,1)S(1)} %get-tuple-element.70), channel_id=1, source_target_pairs={{0,16},{2,18},{4,20},{6,22},{8,24},{10,26},{12,28},{14,30},{16,0},... | collective-permute-start | bytes 294920 | tf_op jit(solution)/shard_map/ppermute | solution.py:405
  24.8 18.6 %collective-permute-start.6 = (bf16[192,2048]{1,0:T(8,128)(2,1)S(1)}, bf16[192,2048]{1,0:T(8,128)(2,1)}, u32[]{:S(2)}, u32[]{:S(2)}) collective-permute-start(bf16[192,2048]{1,0:T(8,128)(2,1)S(1)} %copy-done.1), channel_id=1, source_target_pairs={{0,8},{2,10},{4,12},{6,14},{8,0},{10,2},{12,4},{14,6},{16,24},{18,... | collective-permute-start | bytes 2359304 | tf_op jit(solution)/shard_map/ppermute | solution.py:405
  25.3 23.7 %copy-start.6 = (bf16[192,768]{1,0:T(8,128)(2,1)}, bf16[192,768]{1,0:T(8,128)(2,1)S(1)}, u32[]{:S(2)}) copy-start(bf16[192,768]{1,0:T(8,128)(2,1)S(1)} %collective-permute-done.5.refs_2_) | copy-start | bytes 884740
  25.4 9.5 %collective-permute-start.22 = (bf16[384,384]{1,0:T(8,128)(2,1)}, bf16[384,384]{1,0:T(8,128)(2,1)}, u32[]{:S(2)}, u32[]{:S(2)}) collective-permute-start(bf16[384,384]{1,0:T(8,128)(2,1)} %pad_maximum_fusion.1.refs_0_), channel_id=1, source_target_pairs={{0,4},{2,6},{4,0},{6,2},{8,12},{10,14},{12,8},{14,10},{16,20},{18,... | collective-permute-start | bytes 884744 | tf_op jit(solution)/shard_map/ppermute | solution.py:405
  26.5 9.9 %collective-permute-start.13 = (bf16[192,768]{1,0:T(8,128)(2,1)}, bf16[192,768]{1,0:T(8,128)(2,1)S(1)}, u32[]{:S(2)}, u32[]{:S(2)}) collective-permute-start(bf16[192,768]{1,0:T(8,128)(2,1)} %refs_8_.2), channel_id=1, source_target_pairs={{0,2},{2,0},{4,6},{6,4},{8,10},{10,8},{12,14},{14,12},{16,18},{18,... | collective-permute-start | bytes 884744 | tf_op jit(solution)/shard_map/ppermute | solution.py:405
  29.7 19.3 %copy-start.7 = (bf16[192,768]{1,0:T(8,128)(2,1)}, bf16[192,768]{1,0:T(8,128)(2,1)S(1)}, u32[]{:S(2)}) copy-start(bf16[192,768]{1,0:T(8,128)(2,1)S(1)} %collective-permute-done.14.refs_10_) | copy-start | bytes 884740
  29.8 9.2 %collective-permute-start.8 = (bf16[192,768]{1,0:T(8,128)(2,1)}, bf16[192,768]{1,0:T(8,128)(2,1)S(1)}, u32[]{:S(2)}, u32[]{:S(2)}) collective-permute-start(bf16[192,768]{1,0:T(8,128)(2,1)} %refs_0_.3), channel_id=1, source_target_pairs={{0,2},{2,0},{4,6},{6,4},{8,10},{10,8},{12,14},{14,12},{16,18},{18,... | collective-permute-start | bytes 884744 | tf_op jit(solution)/shard_map/ppermute | solution.py:405
  29.8 11.3 %collective-permute-start.9 = (bf16[192,768]{1,0:T(8,128)(2,1)S(1)}, bf16[192,768]{1,0:T(8,128)(2,1)S(1)}, u32[]{:S(2)}, u32[]{:S(2)}) collective-permute-start(bf16[192,768]{1,0:T(8,128)(2,1)S(1)} %collective-permute-done.5.refs_2_), channel_id=1, source_target_pairs={{0,2},{2,0},{4,6},{6,4},{8,10},{10,8},{12,14},{14,12},{16,18},{18,... | collective-permute-start | bytes 884744 | tf_op jit(solution)/shard_map/ppermute | solution.py:405
  34.8 5.7 %collective-permute-start.4 = (bf16[2,32,1536]{2,1,0:T(8,128)(2,1)S(1)}, bf16[2,32,1536]{2,1,0:T(8,128)(2,1)S(1)}, u32[]{:S(2)}, u32[]{:S(2)}) collective-permute-start(bf16[2,32,1536]{2,1,0:T(8,128)(2,1)S(1)} %pad_maximum_fusion.3.mine_ref), channel_id=1, source_target_pairs={{0,1},{1,0},{2,3},{3,2},{4,5},{5,4},{6,7},{7,6},{8,9},{9,8},{10,11... | collective-permute-start | bytes 589832 | tf_op jit(solution)/shard_map/ppermute | solution.py:410
  36.4 7.0 %copy-start.8 = (bf16[192,768]{1,0:T(8,128)(2,1)}, bf16[192,768]{1,0:T(8,128)(2,1)S(1)}, u32[]{:S(2)}) copy-start(bf16[192,768]{1,0:T(8,128)(2,1)S(1)} %collective-permute-done.13.refs_9_) | copy-start | bytes 884740
  36.4 27.7 %collective-permute-start.17 = (bf16[192,2048]{1,0:T(8,128)(2,1)S(1)}, bf16[192,2048]{1,0:T(8,128)(2,1)}, u32[]{:S(2)}, u32[]{:S(2)}) collective-permute-start(bf16[192,2048]{1,0:T(8,128)(2,1)S(1)} %copy-done.2), channel_id=1, source_target_pairs={{0,8},{2,10},{4,12},{6,14},{8,0},{10,2},{12,4},{14,6},{16,24},{18,... | collective-permute-start | bytes 2359304 | tf_op jit(solution)/shard_map/ppermute | solution.py:405
  38.9 4.5 %copy-start.9 = (bf16[192,768]{1,0:T(8,128)(2,1)}, bf16[192,768]{1,0:T(8,128)(2,1)S(1)}, u32[]{:S(2)}) copy-start(bf16[192,768]{1,0:T(8,128)(2,1)S(1)} %collective-permute-done.8.refs_1_) | copy-start | bytes 884740
  38.9 30.3 %collective-permute-start.23 = (bf16[192,2048]{1,0:T(8,128)(2,1)S(1)}, bf16[192,2048]{1,0:T(8,128)(2,1)}, u32[]{:S(2)}, u32[]{:S(2)}) collective-permute-start(bf16[192,2048]{1,0:T(8,128)(2,1)S(1)} %copy-done.1), channel_id=1, source_target_pairs={{0,4},{2,6},{4,0},{6,2},{8,12},{10,14},{12,8},{14,10},{16,20},{18,... | collective-permute-start | bytes 2359304 | tf_op jit(solution)/shard_map/ppermute | solution.py:405
  40.5 35.9 %collective-permute-start.24 = (bf16[192,2048]{1,0:T(8,128)(2,1)S(1)}, bf16[192,2048]{1,0:T(8,128)(2,1)}, u32[]{:S(2)}, u32[]{:S(2)}) collective-permute-start(bf16[192,2048]{1,0:T(8,128)(2,1)S(1)} %copy-done.2), channel_id=1, source_target_pairs={{0,4},{2,6},{4,0},{6,2},{8,12},{10,14},{12,8},{14,10},{16,20},{18,... | collective-permute-start | bytes 2359304 | tf_op jit(solution)/shard_map/ppermute | solution.py:405
  41.0 2.4 %copy-start.10 = (bf16[192,768]{1,0:T(8,128)(2,1)}, bf16[192,768]{1,0:T(8,128)(2,1)S(1)}, u32[]{:S(2)}) copy-start(bf16[192,768]{1,0:T(8,128)(2,1)S(1)} %collective-permute-done.9.refs_3_) | copy-start | bytes 884740
  41.0 5.4 %collective-permute-start.12 = (bf16[192,768]{1,0:T(8,128)(2,1)}, bf16[192,768]{1,0:T(8,128)(2,1)}, u32[]{:S(2)}, u32[]{:S(2)}) collective-permute-start(bf16[192,768]{1,0:T(8,128)(2,1)} %collective-permute-done.11.refs_6_), channel_id=1, source_target_pairs={{0,2},{2,0},{4,6},{6,4},{8,10},{10,8},{12,14},{14,12},{16,18},{18,... | collective-permute-start | bytes 884744 | tf_op jit(solution)/shard_map/ppermute | solution.py:405
  43.4 5.6 %collective-permute-start.15 = (bf16[192,768]{1,0:T(8,128)(2,1)S(1)}, bf16[192,768]{1,0:T(8,128)(2,1)}, u32[]{:S(2)}, u32[]{:S(2)}) collective-permute-start(bf16[192,768]{1,0:T(8,128)(2,1)S(1)} %collective-permute-done.14.refs_10_), channel_id=1, source_target_pairs={{0,2},{2,0},{4,6},{6,4},{8,10},{10,8},{12,14},{14,12},{16,18},{18,... | collective-permute-start | bytes 884744 | tf_op jit(solution)/shard_map/ppermute | solution.py:405
  46.5 8.4 %collective-permute-start.7 = (bf16[4,32,768]{2,1,0:T(8,128)(2,1)}, bf16[4,32,768]{2,1,0:T(8,128)(2,1)}, u32[]{:S(2)}, u32[]{:S(2)}) collective-permute-start(bf16[4,32,768]{2,1,0:T(8,128)(2,1)} %pad_maximum_fusion.2.mine_ref), channel_id=1, source_target_pairs={{0,1},{1,0},{2,3},{3,2},{4,5},{5,4},{6,7},{7,6},{8,9},{9,8},{10,11... | collective-permute-start | bytes 589832 | tf_op jit(solution)/shard_map/ppermute | solution.py:410
  49.0 44.1 %collective-permute-start.25 = (bf16[1024,384]{1,0:T(8,128)(2,1)S(1)}, bf16[1024,384]{1,0:T(8,128)(2,1)S(1)}, u32[]{:S(2)}, u32[]{:S(2)}) collective-permute-start(bf16[1024,384]{1,0:T(8,128)(2,1)S(1)} %pad_maximum_fusion.refs_0_), channel_id=1, source_target_pairs={{0,4},{2,6},{4,0},{6,2},{8,12},{10,14},{12,8},{14,10},{16,20},{18,... | collective-permute-start | bytes 2359304 | tf_op jit(solution)/shard_map/ppermute | solution.py:405
  54.9 9.2 %collective-permute-start.16 = (bf16[384,384]{1,0:T(8,128)(2,1)}, bf16[384,384]{1,0:T(8,128)(2,1)}, u32[]{:S(2)}, u32[]{:S(2)}) collective-permute-start(bf16[384,384]{1,0:T(8,128)(2,1)} %pad_maximum_fusion.1.refs_0_), channel_id=1, source_target_pairs={{0,8},{2,10},{4,12},{6,14},{8,0},{10,2},{12,4},{14,6},{16,24},{18,... | collective-permute-start | bytes 884744 | tf_op jit(solution)/shard_map/ppermute | solution.py:405
  64.1 32.6 %collective-permute-start.18 = (bf16[64,2432]{1,0:T(8,128)(2,1)}, bf16[64,2432]{1,0:T(8,128)(2,1)}, u32[]{:S(2)}, u32[]{:S(2)}) collective-permute-start(bf16[64,2432]{1,0:T(8,128)(2,1)} %get-tuple-element.82), channel_id=1, source_target_pairs={{0,8},{2,10},{4,12},{6,14},{8,16},{10,18},{12,20},{14,22},{16,24},... | collective-permute-start | bytes 933896 | tf_op jit(solution)/shard_map/ppermute | solution.py:424
  65.5 31.2 %collective-permute-start.19 = (bf16[64,2432]{1,0:T(8,128)(2,1)}, bf16[64,2432]{1,0:T(8,128)(2,1)}, u32[]{:S(2)}, u32[]{:S(2)}) collective-permute-start(bf16[64,2432]{1,0:T(8,128)(2,1)} %get-tuple-element.83), channel_id=1, source_target_pairs={{0,16},{2,18},{4,20},{6,22},{8,24},{10,26},{12,28},{14,30},{16,0},... | collective-permute-start | bytes 933896 | tf_op jit(solution)/shard_map/ppermute | solution.py:424
  69.2 27.5 %collective-permute-start.20 = (bf16[64,2432]{1,0:T(8,128)(2,1)}, bf16[64,2432]{1,0:T(8,128)(2,1)}, u32[]{:S(2)}, u32[]{:S(2)}) collective-permute-start(bf16[64,2432]{1,0:T(8,128)(2,1)} %get-tuple-element.84), channel_id=1, source_target_pairs={{0,24},{2,26},{4,28},{6,30},{8,0},{10,2},{12,4},{14,6},{16,8},{18,... | collective-permute-start | bytes 933896 | tf_op jit(solution)/shard_map/ppermute | solution.py:424
  76.4 20.4 %collective-permute-start.21 = (bf16[384,384]{1,0:T(8,128)(2,1)}, bf16[384,384]{1,0:T(8,128)(2,1)}, u32[]{:S(2)}, u32[]{:S(2)}) collective-permute-start(bf16[384,384]{1,0:T(8,128)(2,1)} %collective-permute-done.16.refs_4_), channel_id=1, source_target_pairs={{0,4},{2,6},{4,0},{6,2},{8,12},{10,14},{12,8},{14,10},{16,20},{18,... | collective-permute-start | bytes 884744 | tf_op jit(solution)/shard_map/ppermute | solution.py:405
  93.1 14.6 %collective-permute-start.28 = (bf16[384,384]{1,0:T(8,128)(2,1)}, bf16[384,384]{1,0:T(8,128)(2,1)}, u32[]{:S(2)}, u32[]{:S(2)}) collective-permute-start(bf16[384,384]{1,0:T(8,128)(2,1)} %collective-permute-done.22.refs_2_), channel_id=1, source_target_pairs={{0,2},{2,0},{4,6},{6,4},{8,10},{10,8},{12,14},{14,12},{16,18},{18,... | collective-permute-start | bytes 884744 | tf_op jit(solution)/shard_map/ppermute | solution.py:405
  100.4 6.6 %collective-permute-start.26 = (bf16[64,768]{1,0:T(8,128)(2,1)}, bf16[64,768]{1,0:T(8,128)(2,1)S(1)}, u32[]{:S(2)}, u32[]{:S(2)}) collective-permute-start(bf16[64,768]{1,0:T(8,128)(2,1)} %get-tuple-element.94.own_ref), channel_id=1, source_target_pairs={{0,16},{2,18},{4,20},{6,22},{8,24},{10,26},{12,28},{14,30},{16,0},... | collective-permute-start | bytes 294920 | tf_op jit(solution)/shard_map/ppermute | solution.py:405
  101.6 22.4 %collective-permute-start.33 = (bf16[192,2048]{1,0:T(8,128)(2,1)}, bf16[192,2048]{1,0:T(8,128)(2,1)}, u32[]{:S(2)}, u32[]{:S(2)}) collective-permute-start(bf16[192,2048]{1,0:T(8,128)(2,1)} %collective-permute-done.6.refs_4_), channel_id=1, source_target_pairs={{0,4},{2,6},{4,0},{6,2},{8,12},{10,14},{12,8},{14,10},{16,20},{18,... | collective-permute-start | bytes 2359304 | tf_op jit(solution)/shard_map/ppermute | solution.py:405
  102.2 5.5 %collective-permute-start.29 = (bf16[384,384]{1,0:T(8,128)(2,1)}, bf16[384,384]{1,0:T(8,128)(2,1)}, u32[]{:S(2)}, u32[]{:S(2)}) collective-permute-start(bf16[384,384]{1,0:T(8,128)(2,1)} %collective-permute-done.16.refs_4_), channel_id=1, source_target_pairs={{0,2},{2,0},{4,6},{6,4},{8,10},{10,8},{12,14},{14,12},{16,18},{18,... | collective-permute-start | bytes 884744 | tf_op jit(solution)/shard_map/ppermute | solution.py:405
  102.2 5.5 %collective-permute-start.27 = (bf16[384,384]{1,0:T(8,128)(2,1)}, bf16[384,384]{1,0:T(8,128)(2,1)}, u32[]{:S(2)}, u32[]{:S(2)}) collective-permute-start(bf16[384,384]{1,0:T(8,128)(2,1)} %pad_maximum_fusion.1.refs_0_), channel_id=1, source_target_pairs={{0,2},{2,0},{4,6},{6,4},{8,10},{10,8},{12,14},{14,12},{16,18},{18,... | collective-permute-start | bytes 884744 | tf_op jit(solution)/shard_map/ppermute | solution.py:405
  107.0 1.9 collective-permute-start.30
  107.7 19.3 %collective-permute-start.32 = (bf16[1024,384]{1,0:T(8,128)(2,1)S(1)}, bf16[1024,384]{1,0:T(8,128)(2,1)S(1)}, u32[]{:S(2)}, u32[]{:S(2)}) collective-permute-start(bf16[1024,384]{1,0:T(8,128)(2,1)S(1)} %pad_maximum_fusion.refs_0_), channel_id=1, source_target_pairs={{0,8},{2,10},{4,12},{6,14},{8,0},{10,2},{12,4},{14,6},{16,24},{18,... | collective-permute-start | bytes 2359304 | tf_op jit(solution)/shard_map/ppermute | solution.py:405
  112.7 11.4 %collective-permute-start.31 = (bf16[128,1536]{1,0:T(8,128)(2,1)}, bf16[128,1536]{1,0:T(8,128)(2,1)S(1)}, u32[]{:S(2)}, u32[]{:S(2)}) collective-permute-start(bf16[128,1536]{1,0:T(8,128)(2,1)} %shard_map.142.a_ref), channel_id=1, source_target_pairs={{0,1},{1,0},{2,3},{3,2},{4,5},{5,4},{6,7},{7,6},{8,9},{9,8},{10,11... | collective-permute-start | bytes 1179656 | tf_op jit(solution)/shard_map/ppermute | solution.py:410
  113.2 16.4 %collective-permute-start.36 = (bf16[192,2048]{1,0:T(8,128)(2,1)}, bf16[192,2048]{1,0:T(8,128)(2,1)S(1)}, u32[]{:S(2)}, u32[]{:S(2)}) collective-permute-start(bf16[192,2048]{1,0:T(8,128)(2,1)} %collective-permute-done.6.refs_4_), channel_id=1, source_target_pairs={{0,2},{2,0},{4,6},{6,4},{8,10},{10,8},{12,14},{14,12},{16,18},{18,... | collective-permute-start | bytes 2359304 | tf_op jit(solution)/shard_map/ppermute | solution.py:405
  113.2 16.4 %collective-permute-start.35 = (bf16[192,2048]{1,0:T(8,128)(2,1)}, bf16[192,2048]{1,0:T(8,128)(2,1)S(1)}, u32[]{:S(2)}, u32[]{:S(2)}) collective-permute-start(bf16[192,2048]{1,0:T(8,128)(2,1)} %collective-permute-done.23.refs_2_), channel_id=1, source_target_pairs={{0,2},{2,0},{4,6},{6,4},{8,10},{10,8},{12,14},{14,12},{16,18},{18,... | collective-permute-start | bytes 2359304 | tf_op jit(solution)/shard_map/ppermute | solution.py:405
  124.1 5.5 %collective-permute-start.34 = (bf16[192,2048]{1,0:T(8,128)(2,1)S(1)}, bf16[192,2048]{1,0:T(8,128)(2,1)S(1)}, u32[]{:S(2)}, u32[]{:S(2)}) collective-permute-start(bf16[192,2048]{1,0:T(8,128)(2,1)S(1)} %copy-done.1), channel_id=1, source_target_pairs={{0,2},{2,0},{4,6},{6,4},{8,10},{10,8},{12,14},{14,12},{16,18},{18,... | collective-permute-start | bytes 2359304 | tf_op jit(solution)/shard_map/ppermute | solution.py:405
  124.1 5.5 %collective-permute-start.37 = (bf16[192,2048]{1,0:T(8,128)(2,1)}, bf16[192,2048]{1,0:T(8,128)(2,1)S(1)}, u32[]{:S(2)}, u32[]{:S(2)}) collective-permute-start(bf16[192,2048]{1,0:T(8,128)(2,1)} %collective-permute-done.33.refs_6_), channel_id=1, source_target_pairs={{0,2},{2,0},{4,6},{6,4},{8,10},{10,8},{12,14},{14,12},{16,18},{18,... | collective-permute-start | bytes 2359304 | tf_op jit(solution)/shard_map/ppermute | solution.py:405
  127.0 18.6 %collective-permute-start.42 = (bf16[192,2048]{1,0:T(8,128)(2,1)}, bf16[192,2048]{1,0:T(8,128)(2,1)S(1)}, u32[]{:S(2)}, u32[]{:S(2)}) collective-permute-start(bf16[192,2048]{1,0:T(8,128)(2,1)} %collective-permute-done.17.refs_4_), channel_id=1, source_target_pairs={{0,4},{2,6},{4,0},{6,2},{8,12},{10,14},{12,8},{14,10},{16,20},{18,... | collective-permute-start | bytes 2359304 | tf_op jit(solution)/shard_map/ppermute | solution.py:405
  129.6 4.9 %copy-start.3 = (bf16[192,2048]{1,0:T(8,128)(2,1)S(1)}, bf16[192,2048]{1,0:T(8,128)(2,1)}, u32[]{:S(2)}) copy-start(bf16[192,2048]{1,0:T(8,128)(2,1)} %refs_0_.5) | copy-start | bytes 2359300
  133.5 14.2 %collective-permute-start.38 = (bf16[64,2176]{1,0:T(8,128)(2,1)S(1)}, bf16[64,2176]{1,0:T(8,128)(2,1)S(1)}, u32[]{:S(2)}, u32[]{:S(2)}) collective-permute-start(bf16[64,2176]{1,0:T(8,128)(2,1)S(1)} %get-tuple-element.108), channel_id=1, source_target_pairs={{0,16},{2,18},{4,20},{6,22},{8,24},{10,26},{12,28},{14,30},{16,0},... | collective-permute-start | bytes 835592 | tf_op jit(solution)/shard_map/ppermute | solution.py:405
  134.0 15.2 %collective-permute-start.41 = (bf16[192,2048]{1,0:T(8,128)(2,1)}, bf16[192,2048]{1,0:T(8,128)(2,1)S(1)}, u32[]{:S(2)}, u32[]{:S(2)}) collective-permute-start(bf16[192,2048]{1,0:T(8,128)(2,1)} %collective-permute-done.17.refs_4_), channel_id=1, source_target_pairs={{0,2},{2,0},{4,6},{6,4},{8,10},{10,8},{12,14},{14,12},{16,18},{18,... | collective-permute-start | bytes 2359304 | tf_op jit(solution)/shard_map/ppermute | solution.py:405
  134.0 15.2 %collective-permute-start.40 = (bf16[192,2048]{1,0:T(8,128)(2,1)}, bf16[192,2048]{1,0:T(8,128)(2,1)S(1)}, u32[]{:S(2)}, u32[]{:S(2)}) collective-permute-start(bf16[192,2048]{1,0:T(8,128)(2,1)} %collective-permute-done.24.refs_2_), channel_id=1, source_target_pairs={{0,2},{2,0},{4,6},{6,4},{8,10},{10,8},{12,14},{14,12},{16,18},{18,... | collective-permute-start | bytes 2359304 | tf_op jit(solution)/shard_map/ppermute | solution.py:405
  134.5 14.7 %collective-permute-start.39 = (bf16[192,2048]{1,0:T(8,128)(2,1)S(1)}, bf16[192,2048]{1,0:T(8,128)(2,1)S(1)}, u32[]{:S(2)}, u32[]{:S(2)}) collective-permute-start(bf16[192,2048]{1,0:T(8,128)(2,1)S(1)} %copy-done.3), channel_id=1, source_target_pairs={{0,2},{2,0},{4,6},{6,4},{8,10},{10,8},{12,14},{14,12},{16,18},{18,... | collective-permute-start | bytes 2359304 | tf_op jit(solution)/shard_map/ppermute | solution.py:405
  147.7 2.3 %collective-permute-start.43 = (bf16[192,2048]{1,0:T(8,128)(2,1)S(1)}, bf16[192,2048]{1,0:T(8,128)(2,1)S(1)}, u32[]{:S(2)}, u32[]{:S(2)}) collective-permute-start(bf16[192,2048]{1,0:T(8,128)(2,1)S(1)} %collective-permute-done.42.refs_6_), channel_id=1, source_target_pairs={{0,2},{2,0},{4,6},{6,4},{8,10},{10,8},{12,14},{14,12},{16,18},{18,... | collective-permute-start | bytes 2359304 | tf_op jit(solution)/shard_map/ppermute | solution.py:405
  147.7 20.1 %collective-permute-start.49 = (bf16[1024,384]{1,0:T(8,128)(2,1)S(1)}, bf16[1024,384]{1,0:T(8,128)(2,1)}, u32[]{:S(2)}, u32[]{:S(2)}) collective-permute-start(bf16[1024,384]{1,0:T(8,128)(2,1)S(1)} %collective-permute-done.32.refs_4_), channel_id=1, source_target_pairs={{0,4},{2,6},{4,0},{6,2},{8,12},{10,14},{12,8},{14,10},{16,20},{18,... | collective-permute-start | bytes 2359304 | tf_op jit(solution)/shard_map/ppermute | solution.py:405
  153.7 14.1 %collective-permute-start.44 = (bf16[64,2048]{1,0:T(8,128)(2,1)S(1)}, bf16[64,2048]{1,0:T(8,128)(2,1)S(1)}, u32[]{:S(2)}, u32[]{:S(2)}) collective-permute-start(bf16[64,2048]{1,0:T(8,128)(2,1)S(1)} %get-tuple-element.117), channel_id=1, source_target_pairs={{0,16},{2,18},{4,20},{6,22},{8,24},{10,26},{12,28},{14,30},{16,0},... | collective-permute-start | bytes 786440 | tf_op jit(solution)/shard_map/ppermute | solution.py:405
  153.8 29.2 %collective-permute-start.48 = (bf16[1024,384]{1,0:T(8,128)(2,1)S(1)}, bf16[1024,384]{1,0:T(8,128)(2,1)}, u32[]{:S(2)}, u32[]{:S(2)}) collective-permute-start(bf16[1024,384]{1,0:T(8,128)(2,1)S(1)} %collective-permute-done.32.refs_4_), channel_id=1, source_target_pairs={{0,2},{2,0},{4,6},{6,4},{8,10},{10,8},{12,14},{14,12},{16,18},{18,... | collective-permute-start | bytes 2359304 | tf_op jit(solution)/shard_map/ppermute | solution.py:405
  154.0 29.0 %collective-permute-start.47 = (bf16[1024,384]{1,0:T(8,128)(2,1)S(1)}, bf16[1024,384]{1,0:T(8,128)(2,1)}, u32[]{:S(2)}, u32[]{:S(2)}) collective-permute-start(bf16[1024,384]{1,0:T(8,128)(2,1)S(1)} %collective-permute-done.25.refs_2_), channel_id=1, source_target_pairs={{0,2},{2,0},{4,6},{6,4},{8,10},{10,8},{12,14},{14,12},{16,18},{18,... | collective-permute-start | bytes 2359304 | tf_op jit(solution)/shard_map/ppermute | solution.py:405
  154.4 28.6 %collective-permute-start.46 = (bf16[1024,384]{1,0:T(8,128)(2,1)S(1)}, bf16[1024,384]{1,0:T(8,128)(2,1)}, u32[]{:S(2)}, u32[]{:S(2)}) collective-permute-start(bf16[1024,384]{1,0:T(8,128)(2,1)S(1)} %pad_maximum_fusion.refs_0_), channel_id=1, source_target_pairs={{0,2},{2,0},{4,6},{6,4},{8,10},{10,8},{12,14},{14,12},{16,18},{18,... | collective-permute-start | bytes 2359304 | tf_op jit(solution)/shard_map/ppermute | solution.py:405
  167.8 15.2 %collective-permute-start.50 = (bf16[1024,384]{1,0:T(8,128)(2,1)}, bf16[1024,384]{1,0:T(8,128)(2,1)}, u32[]{:S(2)}, u32[]{:S(2)}) collective-permute-start(bf16[1024,384]{1,0:T(8,128)(2,1)} %collective-permute-done.49.refs_6_), channel_id=1, source_target_pairs={{0,2},{2,0},{4,6},{6,4},{8,10},{10,8},{12,14},{14,12},{16,18},{18,... | collective-permute-start | bytes 2359304 | tf_op jit(solution)/shard_map/ppermute | solution.py:405
  168.3 14.7 %collective-permute-start.45 = (bf16[64,2048]{1,0:T(8,128)(2,1)S(1)}, bf16[64,2048]{1,0:T(8,128)(2,1)S(1)}, u32[]{:S(2)}, u32[]{:S(2)}) collective-permute-start(bf16[64,2048]{1,0:T(8,128)(2,1)S(1)} %multiply_convert_fusion.own_ref), channel_id=1, source_target_pairs={{0,16},{2,18},{4,20},{6,22},{8,24},{10,26},{12,28},{14,30},{16,0},... | collective-permute-start | bytes 786440 | tf_op jit(solution)/shard_map/ppermute | solution.py:405
  188.0 6.9 %collective-permute-start.51 = (bf16[2,32,1536]{2,1,0:T(8,128)(2,1)S(1)}, bf16[2,32,1536]{2,1,0:T(8,128)(2,1)S(1)}, u32[]{:S(2)}, u32[]{:S(2)}) collective-permute-start(bf16[2,32,1536]{2,1,0:T(8,128)(2,1)S(1)} %dynamic-slice_bitcast_fusion), channel_id=1, source_target_pairs={{0,1},{1,0},{2,3},{3,2},{4,5},{5,4},{6,7},{7,6},{8,9},{9,8},{10,11... | collective-permute-start | bytes 589832 | tf_op jit(solution)/shard_map/ppermute | solution.py:410
  196.0 6.1 %collective-permute-start.52 = (bf16[32,1536]{1,0:T(8,128)(2,1)S(1)}, bf16[32,1536]{1,0:T(8,128)(2,1)S(1)}, u32[]{:S(2)}, u32[]{:S(2)}) collective-permute-start(bf16[32,1536]{1,0:T(8,128)(2,1)S(1)} %get-tuple-element.130), channel_id=1, source_target_pairs={{0,16},{2,18},{4,20},{6,22},{8,24},{10,26},{12,28},{14,30},{16,0},... | collective-permute-start | bytes 294920 | tf_op jit(solution)/shard_map/ppermute | solution.py:405
  (4 other events, 3.4 us)

commit v5 on v4

--- a/solution.py
+++ b/solution.py
@@ -160,20 +160,18 @@
         for k, w in enumerate(weights):
             at = pl.multiple_of((place[0] ^ k) * wide, wide)
             yield pltpu.make_async_copy(
-                w.at[:, step * block : (step + 1) * block], held.at[step % 2, pl.ds(at, wide)], sems.at[step % 2, k]
+                w.at[:, step * block : (step + 1) * block], held.at[step, pl.ds(at, wide)], sems.at[step, k]
             )
 
-    for c in copies(0):
-        c.start()
+    for step in range(steps):
+        for c in copies(step):
+            c.start()
     if sent_ref.shape[1] > width:
         sent_ref[:, width:] = coded_ref[...]
     for step in range(steps):
-        if step + 1 < steps:
-            for c in copies(step + 1):
-                c.start()
         for c in copies(step):
             c.wait()
-        total = dot(lhs[...], held[step % 2])
+        total = dot(lhs[...], held[step])
         at = step * block
         own_ref[:, at : at + block] = total[:keep]
         sent_ref[:, at : at + block] = total[keep:].astype(BF)
@@ -196,7 +194,7 @@
             grid=(1,),
             in_specs=[pl.BlockSpec(lhs.shape, whole), pl.BlockSpec(coded.shape, whole)] + in_hbm(pieces),
             out_specs=[pl.BlockSpec((keep, sent), whole), pl.BlockSpec((keep, width), whole)],
-            scratch_shapes=[pltpu.VMEM((2, depth, block), BF), pltpu.SemaphoreType.DMA((2, OCT))],
+            scratch_shapes=[pltpu.VMEM((width // block, depth, block), BF), pltpu.SemaphoreType.DMA((width // block, OCT))],
         ),
         out_shape=[jax.ShapeDtypeStruct((keep, sent), BF), jax.ShapeDtypeStruct((keep, width), F32)],
         compiler_params=pltpu.CompilerParams(vmem_limit_bytes=VMEM),
@@ -246,14 +244,6 @@
     )(place, lhs, coded, *pieces)
 
 
-def stacked(a_ref, own_ref, got_ref):
-    keep, depth = own_ref.shape
-    for h in range(2):
-        columns = slice(h * depth // 2, (h + 1) * depth // 2)
-        a_ref[2 * h * keep : (2 * h + 1) * keep] = own_ref[:, columns]
-        a_ref[(2 * h + 1) * keep : (2 * h + 2) * keep] = got_ref[:, columns]
-
-
 def columns_kernel(place, own_ref, got_ref, *refs):
     weights, (out_ref, parts, a_ref, held, sems) = refs[:OCT], refs[OCT:]
     keep, depth = own_ref.shape
@@ -261,11 +251,13 @@
     copies = [pltpu.make_async_copy(w, held.at[n], sems.at[n]) for n, w in enumerate(weights)]
     for c in copies:
         c.start()
-    stacked(a_ref, own_ref, got_ref)
+    a_ref[:keep] = own_ref[...]
+    a_ref[keep:] = got_ref[...]
     for k in range(OCT):
         copies[k].wait()
-        both = dot(a_ref[...], held[k])
-        parts[place[0] ^ k] = (both[: 2 * keep, :wide] + both[2 * keep :, wide:]).astype(BF)
+        lower = dot(a_ref[:, : depth // 2], held[k])
+        upper = dot(a_ref[:, depth // 2 :], held[k])
+        parts[place[0] ^ k] = (lower[:, :wide] + upper[:, wide:]).astype(BF)
     for i in range(OCT):
         out_ref[:, i * wide : (i + 1) * wide] = parts[i]
 
@@ -285,7 +277,7 @@
             out_specs=pl.BlockSpec((rows, OCT * wide), whole),
             scratch_shapes=[
                 pltpu.VMEM((OCT, rows, wide), BF),
-                pltpu.VMEM((2 * rows, depth // 2), BF),
+                pltpu.VMEM((rows, depth), BF),
                 pltpu.VMEM((OCT, deep, double), BF),
                 pltpu.SemaphoreType.DMA((OCT,)),
             ],
@@ -298,11 +290,13 @@
 def out_kernel(place, own_ref, got_ref, *refs):
     weights, (out_ref, parts, a_ref) = refs[:OCT], refs[OCT:]
     keep, depth = own_ref.shape
-    stacked(a_ref, own_ref, got_ref)
+    a_ref[:keep] = own_ref[...]
+    a_ref[keep:] = got_ref[...]
     wide = weights[0].shape[-1] // 2
     for k in range(OCT):
-        both = dot(a_ref[...], weights[k][...])
-        parts[place[0] ^ k] = (both[: 2 * keep, :wide] + both[2 * keep :, wide:]).astype(BF)
+        lower = dot(a_ref[:, : depth // 2], weights[k][...])
+        upper = dot(a_ref[:, depth // 2 :], weights[k][...])
+        parts[place[0] ^ k] = (lower[:, :wide] + upper[:, wide:]).astype(BF)
     for i in range(OCT):
         out_ref[:, i * wide : (i + 1) * wide] = parts[i]
 
@@ -320,7 +314,7 @@
             grid=(1,),
             in_specs=[pl.BlockSpec((keep, depth), whole)] * 2 + [pl.BlockSpec((deep, double), whole)] * OCT,
             out_specs=pl.BlockSpec((rows, OCT * wide), whole),
-            scratch_shapes=[pltpu.VMEM((OCT, rows, wide), BF), pltpu.VMEM((2 * rows, depth // 2), BF)],
+            scratch_shapes=[pltpu.VMEM((OCT, rows, wide), BF), pltpu.VMEM((rows, depth), BF)],
         ),
         out_shape=jax.ShapeDtypeStruct((rows, OCT * wide), BF),
         compiler_params=pltpu.CompilerParams(vmem_limit_bytes=VMEM_ALL),
@@ -453,8 +447,8 @@
         o_own, d_own = lax.optimization_barrier((beside(w_out), beside(w_down)))
         x_o = near(o_own)
         both = jnp.stack([cut[0], *came])
-        gate, up, z_own, given = lax.optimization_barrier((w_gate, w_up, o_own, cut[4], both))[:4]
-        partner = across(given)
+        partner = across(after(cut[4], both))
+        gate, up, z_own = lax.optimization_barrier((w_gate, w_up, o_own, both, partner))[:3]
         z_o, z_g, z_u = next_to(z_own), next_to(gate), next_to(up)
         mine_too = jnp.stack([columns_of(side, half), partner])
         others_too = other_head(mine_too)

time: 203 us -> 202 us (level)
  Pallas kernels: 27.5 us -> 25.3 us
    unnamed x34 -> x40, local copies, waits for them, and re-layouts: 3.67 us -> 4.28 us
  transfers between devices with their start and end apart: 53 -> 53, of which waited for: 22 -> 22; matrix products, arithmetic and copies ran while one was open for 5% -> 6% of each run, Pallas kernels for 11% -> 10%
where the time goes in v5:
time: 202 us; the launch traced here: 201 us
  waiting for transfers between devices  120 us (59%)
  starting transfers between devices  37.9 us (19%)
  Pallas kernels  25.3 us (13%)
  local copies, waits for them, and re-layouts  9.77 us (5%)
  other arithmetic  6.83 us (3%)
    ppermute x43, waiting for transfers between devices, swap(): return lambda x: lax.ppermute(x, 'group', pairs)  98.2 us
    ppermute x43, starting transfers between devices, swap(): return lambda x: lax.ppermute(x, 'group', pairs)  20.7 us
    ppermute x4, waiting for transfers between devices, other_head(): return lax.ppermute(x, 'head', [(0, 1), (1, 0)])  19.8 us
    ppermute x6, starting transfers between devices, turn(): return lambda x: lax.ppermute(x, 'group', pairs)  9.87 us
    ppermute x4, starting transfers between devices, other_head(): return lax.ppermute(x, 'head', [(0, 1), (1, 0)])  7.29 us
    pallas_call x2, Pallas kernels, rows_product(): pl.pallas_call(rows_kernel, grid_spec=pltpu.PrefetchScalarGridSpec(num_sc...  5.99 us
    pallas_call x1, Pallas kernels, first_rows_product(): pl.pallas_call(first_rows_kernel, grid_spec=pltpu.PrefetchScalarGridSpec(...  5.05 us
    pallas_call x1, Pallas kernels, columns_product(): pl.pallas_call(columns_kernel, grid_spec=pltpu.PrefetchScalarGridSpec(num...  4.56 us
  transfers between devices with their start and end apart: 53, of which 22 were waited for; matrix products, arithmetic and copies ran while one was open for 6% of the time, Pallas kernels for 10%

profile of v5, /device:TPU:0, one launch (start us, length us, event | category | flops | bytes accessed | tf_op | source)
XLA Modules:
  0.0 201.0 jit_solution(380050175245117436)
XLA Ops:
  0.6 3.0 %collective-permute-start.11 = (bf16[192,768]{1,0:T(8,128)(2,1)}, bf16[192,768]{1,0:T(8,128)(2,1)S(1)}, u32[]{:S(2)}, u32[]{:S(2)}) collective-permute-start(bf16[192,768]{1,0:T(8,128)(2,1)} %refs_4_.1), channel_id=1, source_target_pairs={{0,4},{2,6},{4,0},{6,2},{8,12},{10,14},{12,8},{14,10},{16,20},{18,... | collective-permute-start | bytes 884744 | tf_op jit(solution)/shard_map/ppermute | solution.py:399
  3.6 1.0 dynamic-slice_bitcast_fusion.1
  4.6 0.9 constant_dynamic-slice_fusion.1
  5.5 3.7 %collective-permute-start = (bf16[32,768]{1,0:T(8,128)(2,1)S(1)}, bf16[32,768]{1,0:T(8,128)(2,1)S(1)}, u32[]{:S(2)}, u32[]{:S(2)}) collective-permute-start(bf16[32,768]{1,0:T(8,128)(2,1)S(1)} %get-tuple-element.66), channel_id=1, source_target_pairs={{0,24},{2,26},{4,28},{6,30},{8,0},{10,2},{12,4},{14,6},{16,8},{18,... | collective-permute-start | bytes 147464 | tf_op jit(solution)/shard_map/ppermute | solution.py:418
  9.2 1.0 collective-permute-start.2
  11.2 0.6 slice_bitcast_fusion.2
  12.5 0.6 collective-permute-start.5
  13.1 2.1 %collective-permute-done.1 = bf16[32,768]{1,0:T(8,128)(2,1)S(1)} collective-permute-done((bf16[32,768]{1,0:T(8,128)(2,1)S(1)}, bf16[32,768]{1,0:T(8,128)(2,1)S(1)}, u32[]{:S(2)}, u32[]{:S(2)}) %collective-permute-start.1) | collective-permute-done | bytes 49184 | tf_op jit(solution)/shard_map/ppermute | solution.py:418
  15.8 0.5 copy-done.15
  16.4 1.6 pad_maximum_fusion.2.mine_ref
  18.0 1.1 collective-permute-start.3
  19.1 0.8 pad_maximum_fusion.1.refs_0_
  19.9 4.7 %collective-permute-done.3 = bf16[32,1536]{1,0:T(8,128)(2,1)S(1)} collective-permute-done((bf16[32,1536]{1,0:T(8,128)(2,1)S(1)}, bf16[32,1536]{1,0:T(8,128)(2,1)S(1)}, u32[]{:S(2)}, u32[]{:S(2)}) %collective-permute-start.3) | collective-permute-done | bytes 98336 | tf_op jit(solution)/shard_map/ppermute | solution.py:399
  25.3 1.1 collective-permute-start.22
  26.5 2.6 %collective-permute-done.14.refs_10_ = bf16[192,768]{1,0:T(8,128)(2,1)} collective-permute-done((bf16[192,768]{1,0:T(8,128)(2,1)}, bf16[192,768]{1,0:T(8,128)(2,1)}, u32[]{:S(2)}, u32[]{:S(2)}) %collective-permute-start.14) | collective-permute-done | bytes 294944 | tf_op jit(solution)/shard_map/ppermute | solution.py:399
  29.6 4.4 %collective-permute-done.22.refs_2_ = bf16[384,384]{1,0:T(8,128)(2,1)} collective-permute-done((bf16[384,384]{1,0:T(8,128)(2,1)}, bf16[384,384]{1,0:T(8,128)(2,1)}, u32[]{:S(2)}, u32[]{:S(2)}) %collective-permute-start.22) | collective-permute-done | bytes 294944 | tf_op jit(solution)/shard_map/ppermute | solution.py:399
  34.1 1.5 collective-permute-start.4
  35.6 2.5 %collective-permute-start.17 = (bf16[192,2048]{1,0:T(8,128)(2,1)S(1)}, bf16[192,2048]{1,0:T(8,128)(2,1)}, u32[]{:S(2)}, u32[]{:S(2)}) collective-permute-start(bf16[192,2048]{1,0:T(8,128)(2,1)S(1)} %copy-done.2), channel_id=1, source_target_pairs={{0,8},{2,10},{4,12},{6,14},{8,0},{10,2},{12,4},{14,6},{16,24},{18,... | collective-permute-start | bytes 2359304 | tf_op jit(solution)/shard_map/ppermute | solution.py:399
  38.7 1.0 collective-permute-done.4.others_ref
  40.3 3.6 %collective-permute-done.6.refs_4_ = bf16[192,2048]{1,0:T(8,128)(2,1)} collective-permute-done((bf16[192,2048]{1,0:T(8,128)(2,1)S(1)}, bf16[192,2048]{1,0:T(8,128)(2,1)}, u32[]{:S(2)}, u32[]{:S(2)}) %collective-permute-start.6) | collective-permute-done | bytes 786464 | tf_op jit(solution)/shard_map/ppermute | solution.py:399
  43.9 0.8 dynamic_slice.41
  44.7 0.8 dynamic_slice.40
  45.5 0.6 reshape.121.gain_ref
  46.1 1.6 fusion.2
  47.7 2.5 %collective-permute-start.7 = (bf16[4,32,768]{2,1,0:T(8,128)(2,1)}, bf16[4,32,768]{2,1,0:T(8,128)(2,1)}, u32[]{:S(2)}, u32[]{:S(2)}) collective-permute-start(bf16[4,32,768]{2,1,0:T(8,128)(2,1)} %pad_maximum_fusion.2.mine_ref), channel_id=1, source_target_pairs={{0,1},{1,0},{2,3},{3,2},{4,5},{5,4},{6,7},{7,6},{8,9},{9,8},{10,11... | collective-permute-start | bytes 589832 | tf_op jit(solution)/shard_map/ppermute | solution.py:404
  50.2 1.7 collective-permute-start.25
  51.9 4.2 %collective-permute-done.7.others_ref = bf16[4,32,768]{2,1,0:T(8,128)(2,1)} collective-permute-done((bf16[4,32,768]{2,1,0:T(8,128)(2,1)}, bf16[4,32,768]{2,1,0:T(8,128)(2,1)}, u32[]{:S(2)}, u32[]{:S(2)}) %collective-permute-start.7) | collective-permute-done | bytes 196640 | tf_op jit(solution)/shard_map/ppermute | solution.py:404
  56.1 0.6 collective-permute-start.16
  56.7 2.1 %shard_map.139 = (bf16[256,768]{1,0:T(8,128)(2,1)}, bf16[4,256,192]{2,1,0:T(8,128)(2,1)}, bf16[192,128]{1,0:T(8,128)(2,1)}, f32[64,128]{1,0:T(8,128)}) custom-call(s32[1]{0:T(128)} %bitcast.row, bf16[4,32,768]{2,1,0:T(8,128)(2,1)} %pad_maximum_fusion.2.mine_ref, bf16[4,32,768]{2,1,0:T(8,128)(2,1)} %collective-permute-done.7.others_ref, ...), custom_call_target="tpu_custom_call" | custom-call | tf_op jit(solution)/shard_map/pallas_call | solution.py:139
  58.7 5.0 %shard_map.140 = (bf16[64,2432]{1,0:T(8,128)(2,1)}, bf16[64,2432]{1,0:T(8,128)(2,1)}, bf16[64,2432]{1,0:T(8,128)(2,1)}, f32[64,2304]{1,0:T(8,128)}) custom-call(s32[1]{0:T(128)} %bitcast.8.place, bf16[4,256,192]{2,1,0:T(8,128)(2,1)} %get-tuple-element.74.lhs, bf16[192,128]{1,0:T(8,128)(2,1)} %get-tuple-element.75.coded_ref, bf16[192,768]{1,0:T(8,128)(2,1)} %refs_0_.3, ...), custom_call_target="tpu_custom_call" | custom-call | tf_op jit(solution)/shard_map/pallas_call | solution.py:233
  63.8 1.5 collective-permute-done.16.refs_4_
  65.7 3.6 %collective-permute-start.19 = (bf16[64,2432]{1,0:T(8,128)(2,1)}, bf16[64,2432]{1,0:T(8,128)(2,1)}, u32[]{:S(2)}, u32[]{:S(2)}) collective-permute-start(bf16[64,2432]{1,0:T(8,128)(2,1)} %get-tuple-element.83), channel_id=1, source_target_pairs={{0,16},{2,18},{4,20},{6,22},{8,24},{10,26},{12,28},{14,30},{16,0},... | collective-permute-start | bytes 933896 | tf_op jit(solution)/shard_map/ppermute | solution.py:418
  69.3 1.2 collective-permute-start.20
  70.4 5.2 %collective-permute-done.24.refs_2_ = bf16[192,2048]{1,0:T(8,128)(2,1)} collective-permute-done((bf16[192,2048]{1,0:T(8,128)(2,1)S(1)}, bf16[192,2048]{1,0:T(8,128)(2,1)}, u32[]{:S(2)}, u32[]{:S(2)}) %collective-permute-start.24) | collective-permute-done | bytes 786464 | tf_op jit(solution)/shard_map/ppermute | solution.py:399
  76.1 16.2 %collective-permute-done.25.refs_2_ = bf16[1024,384]{1,0:T(8,128)(2,1)S(1)} collective-permute-done((bf16[1024,384]{1,0:T(8,128)(2,1)S(1)}, bf16[1024,384]{1,0:T(8,128)(2,1)S(1)}, u32[]{:S(2)}, u32[]{:S(2)}) %collective-permute-start.25) | collective-permute-done | bytes 786464 | tf_op jit(solution)/shard_map/ppermute | solution.py:399
  92.3 0.7 copy.28.refs_9_
  93.0 2.9 %collective-permute-done.21.refs_6_ = bf16[384,384]{1,0:T(8,128)(2,1)} collective-permute-done((bf16[384,384]{1,0:T(8,128)(2,1)}, bf16[384,384]{1,0:T(8,128)(2,1)}, u32[]{:S(2)}, u32[]{:S(2)}) %collective-permute-start.21) | collective-permute-done | bytes 294944 | tf_op jit(solution)/shard_map/ppermute | solution.py:399
  96.0 3.7 %shard_map.141 = (bf16[64,768]{1,0:T(8,128)(2,1)}, bf16[64,768]{1,0:T(8,128)(2,1)}, bf16[64,768]{1,0:T(8,128)(2,1)}) custom-call(f32[64,2304]{1,0:T(8,128)} %get-tuple-element.76.refs_0_, bf16[64,2432]{1,0:T(8,128)(2,1)} %collective-permute-done.18.refs_1_, bf16[64,2432]{1,0:T(8,128)(2,1)} %collective-permute-done.19.refs_2_, ...), custom_call_target="tpu_custom_call" | custom-call | tf_op jit(solution)/shard_map/pallas_call | solution.py:375
  99.7 1.2 collective-permute-start.26
  100.9 0.5 collective-permute-start.33
  101.9 4.4 %collective-permute-done.26.got_ref = bf16[64,768]{1,0:T(8,128)(2,1)S(1)} collective-permute-done((bf16[64,768]{1,0:T(8,128)(2,1)}, bf16[64,768]{1,0:T(8,128)(2,1)S(1)}, u32[]{:S(2)}, u32[]{:S(2)}) %collective-permute-start.26) | collective-permute-done | bytes 98336 | tf_op jit(solution)/shard_map/ppermute | solution.py:399
  106.3 0.6 copy-done.12
  107.0 1.3 collective-permute-done.30.refs_7_
  108.2 3.6 %shard_map.142.a_ref = bf16[128,1536]{1,0:T(8,128)(2,1)} custom-call(s32[1]{0:T(128)} %bitcast.7.place, bf16[64,768]{1,0:T(8,128)(2,1)} %get-tuple-element.94.own_ref, bf16[64,768]{1,0:T(8,128)(2,1)} %copy-done.12, bf16[384,384]{1,0:T(8,128)(2,1)} %pad_maximum_fusion.1.refs_0_, bf16[384,384]{1,0:T(8,128)(2,1)} %collective-permute-done.27.refs_1_, ...), custom_call_target="tpu_custom_call" | custom-call | tf_op jit(solution)/shard_map/pallas_call | solution.py:310
  111.9 1.5 collective-permute-start.31
  113.9 9.4 %collective-permute-done.31.b_ref = bf16[128,1536]{1,0:T(8,128)(2,1)S(1)} collective-permute-done((bf16[128,1536]{1,0:T(8,128)(2,1)}, bf16[128,1536]{1,0:T(8,128)(2,1)S(1)}, u32[]{:S(2)}, u32[]{:S(2)}) %collective-permute-start.31) | collective-permute-done | bytes 393248 | tf_op jit(solution)/shard_map/ppermute | solution.py:404
  123.7 2.5 %collective-permute-done.32.refs_4_ = bf16[1024,384]{1,0:T(8,128)(2,1)S(1)} collective-permute-done((bf16[1024,384]{1,0:T(8,128)(2,1)S(1)}, bf16[1024,384]{1,0:T(8,128)(2,1)S(1)}, u32[]{:S(2)}, u32[]{:S(2)}) %collective-permute-start.32) | collective-permute-done | bytes 786464 | tf_op jit(solution)/shard_map/ppermute | solution.py:399
  126.3 0.6 collective-permute-start.42
  126.9 1.0 copy-done
  128.2 0.7 copy-done.4
  129.0 3.1 %shard_map.144 = (bf16[64,2176]{1,0:T(8,128)(2,1)S(1)}, f32[64,2048]{1,0:T(8,128)S(1)}) custom-call(s32[1]{0:T(128)} %bitcast.7.place, bf16[128,1536]{1,0:T(8,128)(2,1)S(1)} %get-tuple-element.110.lhs, bf16[64,128]{1,0:T(8,128)(2,1)S(1)} %get-tuple-element.103.coded_ref, bf16[192,2048]{1,0:T(8,128)(2,1)S(1)} %copy-done.1, ...), custom_call_target="tpu_custom_call" | custom-call | tf_op jit(solution)/shard_map/pallas_call | solution.py:190
  133.0 11.9 %collective-permute-done.42.refs_6_ = bf16[192,2048]{1,0:T(8,128)(2,1)S(1)} collective-permute-done((bf16[192,2048]{1,0:T(8,128)(2,1)}, bf16[192,2048]{1,0:T(8,128)(2,1)S(1)}, u32[]{:S(2)}, u32[]{:S(2)}) %collective-permute-start.42) | collective-permute-done | bytes 786464 | tf_op jit(solution)/shard_map/ppermute | solution.py:399
  144.9 1.4 collective-permute-done.38
  146.3 1.4 collective-permute-start.49
  147.7 0.9 collective-permute-done.43.refs_7_
  148.6 2.9 %shard_map.145 = (bf16[64,2048]{1,0:T(8,128)(2,1)S(1)}, f32[64,2048]{1,0:T(8,128)S(1)}) custom-call(s32[1]{0:T(128)} %bitcast.7.place, bf16[128,1536]{1,0:T(8,128)(2,1)S(1)} %get-tuple-element.110.lhs, bf16[64,128]{1,0:T(8,128)(2,1)S(1)} %get-tuple-element.103.coded_ref, bf16[192,2048]{1,0:T(8,128)(2,1)S(1)} %copy-done.3, ...), custom_call_target="tpu_custom_call" | custom-call | tf_op jit(solution)/shard_map/pallas_call | solution.py:190
  152.3 14.0 %collective-permute-done.49.refs_6_ = bf16[1024,384]{1,0:T(8,128)(2,1)} collective-permute-done((bf16[1024,384]{1,0:T(8,128)(2,1)S(1)}, bf16[1024,384]{1,0:T(8,128)(2,1)}, u32[]{:S(2)}, u32[]{:S(2)}) %collective-permute-start.49) | collective-permute-done | bytes 786464 | tf_op jit(solution)/shard_map/ppermute | solution.py:399
  166.9 13.9 %collective-permute-done.45.got_ref = bf16[64,2048]{1,0:T(8,128)(2,1)S(1)} collective-permute-done((bf16[64,2048]{1,0:T(8,128)(2,1)S(1)}, bf16[64,2048]{1,0:T(8,128)(2,1)S(1)}, u32[]{:S(2)}, u32[]{:S(2)}) %collective-permute-start.45) | collective-permute-done | bytes 262176 | tf_op jit(solution)/shard_map/ppermute | solution.py:399
  180.8 4.6 %shard_map.146 = bf16[128,1536]{1,0:T(8,128)(2,1)S(1)} custom-call(s32[1]{0:T(128)} %bitcast.7.place, bf16[64,2048]{1,0:T(8,128)(2,1)S(1)} %multiply_convert_fusion.own_ref, bf16[64,2048]{1,0:T(8,128)(2,1)S(1)} %collective-permute-done.45.got_ref, bf16[1024,384]{1,0:T(8,128)(2,1)S(1)} %pad_maximum_fusion.refs_0_, ...), custom_call_target="tpu_custom_call" | custom-call | tf_op jit(solution)/shard_map/pallas_call | solution.py:271
  185.4 1.8 collective-permute-start.51
  187.2 5.2 %collective-permute-done.51 = bf16[2,32,1536]{2,1,0:T(8,128)(2,1)S(1)} collective-permute-done((bf16[2,32,1536]{2,1,0:T(8,128)(2,1)S(1)}, bf16[2,32,1536]{2,1,0:T(8,128)(2,1)S(1)}, u32[]{:S(2)}, u32[]{:S(2)}) %collective-permute-start.51) | collective-permute-done | bytes 196640 | tf_op jit(solution)/shard_map/ppermute | solution.py:404
  192.4 1.0 fusion.1
  193.5 6.8 %collective-permute-done.52 = bf16[32,1536]{1,0:T(8,128)(2,1)S(1)} collective-permute-done((bf16[32,1536]{1,0:T(8,128)(2,1)S(1)}, bf16[32,1536]{1,0:T(8,128)(2,1)S(1)}, u32[]{:S(2)}, u32[]{:S(2)}) %collective-permute-start.52) | collective-permute-done | bytes 98336 | tf_op jit(solution)/shard_map/ppermute | solution.py:399
  200.3 0.7 maximum_select_fusion
  (119 shorter events, 9.9 us)
Async XLA Ops:
  0.6 9.5 %copy-start.5 = (bf16[2048,192]{0,1:T(8,128)(2,1)S(1)}, bf16[2048,192]{0,1:T(8,128)(2,1)}, u32[]{:S(2)}) copy-start(bf16[2048,192]{0,1:T(8,128)(2,1)} %param.21) | copy-start | bytes 2359300
  0.6 25.8 %collective-permute-start.11 = (bf16[192,768]{1,0:T(8,128)(2,1)}, bf16[192,768]{1,0:T(8,128)(2,1)S(1)}, u32[]{:S(2)}, u32[]{:S(2)}) collective-permute-start(bf16[192,768]{1,0:T(8,128)(2,1)} %refs_4_.1), channel_id=1, source_target_pairs={{0,4},{2,6},{4,0},{6,2},{8,12},{10,14},{12,8},{14,10},{16,20},{18,... | collective-permute-start | bytes 884744 | tf_op jit(solution)/shard_map/ppermute | solution.py:399
  3.6 25.4 %collective-permute-start.10 = (bf16[192,768]{1,0:T(8,128)(2,1)}, bf16[192,768]{1,0:T(8,128)(2,1)}, u32[]{:S(2)}, u32[]{:S(2)}) collective-permute-start(bf16[192,768]{1,0:T(8,128)(2,1)} %refs_4_.1), channel_id=1, source_target_pairs={{0,2},{2,0},{4,6},{6,4},{8,10},{10,8},{12,14},{14,12},{16,18},{18,... | collective-permute-start | bytes 884744 | tf_op jit(solution)/shard_map/ppermute | solution.py:399
  5.5 6.9 %collective-permute-start = (bf16[32,768]{1,0:T(8,128)(2,1)S(1)}, bf16[32,768]{1,0:T(8,128)(2,1)S(1)}, u32[]{:S(2)}, u32[]{:S(2)}) collective-permute-start(bf16[32,768]{1,0:T(8,128)(2,1)S(1)} %get-tuple-element.66), channel_id=1, source_target_pairs={{0,24},{2,26},{4,28},{6,30},{8,0},{10,2},{12,4},{14,6},{16,8},{18,... | collective-permute-start | bytes 147464 | tf_op jit(solution)/shard_map/ppermute | solution.py:418
  9.2 6.0 %collective-permute-start.1 = (bf16[32,768]{1,0:T(8,128)(2,1)S(1)}, bf16[32,768]{1,0:T(8,128)(2,1)S(1)}, u32[]{:S(2)}, u32[]{:S(2)}) collective-permute-start(bf16[32,768]{1,0:T(8,128)(2,1)S(1)} %get-tuple-element.67), channel_id=1, source_target_pairs={{0,16},{2,18},{4,20},{6,22},{8,24},{10,26},{12,28},{14,30},{16,0},... | collective-permute-start | bytes 147464 | tf_op jit(solution)/shard_map/ppermute | solution.py:418
  9.2 6.6 %collective-permute-start.2 = (bf16[32,768]{1,0:T(8,128)(2,1)S(1)}, bf16[32,768]{1,0:T(8,128)(2,1)S(1)}, u32[]{:S(2)}, u32[]{:S(2)}) collective-permute-start(bf16[32,768]{1,0:T(8,128)(2,1)S(1)} %get-tuple-element.68), channel_id=1, source_target_pairs={{0,8},{2,10},{4,12},{6,14},{8,16},{10,18},{12,20},{14,22},{16,24},... | collective-permute-start | bytes 147464 | tf_op jit(solution)/shard_map/ppermute | solution.py:418
  12.3 12.4 %copy-start.1 = (bf16[192,2048]{1,0:T(8,128)(2,1)S(1)}, bf16[192,2048]{1,0:T(8,128)(2,1)}, u32[]{:S(2)}) copy-start(bf16[192,2048]{1,0:T(8,128)(2,1)} %refs_0_.4) | copy-start | bytes 2359300
  12.3 12.6 %copy-start.17 = (s32[63,1]{0,1:T(1,128)S(1)}, s32[63,1]{0,1:T(1,128)}, u32[]{:S(2)}) copy-start(s32[63,1]{0,1:T(1,128)} %slice_bitcast_fusion.2) | copy-start | bytes 760
  12.5 3.3 %copy-start.13 = (bf16[32,768]{1,0:T(8,128)(2,1)}, bf16[32,768]{1,0:T(8,128)(2,1)S(1)}, u32[]{:S(2)}) copy-start(bf16[32,768]{1,0:T(8,128)(2,1)S(1)} %collective-permute-done) | copy-start | bytes 147460
  12.5 12.8 %collective-permute-start.5 = (bf16[192,768]{1,0:T(8,128)(2,1)}, bf16[192,768]{1,0:T(8,128)(2,1)}, u32[]{:S(2)}, u32[]{:S(2)}) collective-permute-start(bf16[192,768]{1,0:T(8,128)(2,1)} %refs_0_.3), channel_id=1, source_target_pairs={{0,4},{2,6},{4,0},{6,2},{8,12},{10,14},{12,8},{14,10},{16,20},{18,... | collective-permute-start | bytes 884744 | tf_op jit(solution)/shard_map/ppermute | solution.py:399
  15.2 13.9 %collective-permute-start.14 = (bf16[192,768]{1,0:T(8,128)(2,1)}, bf16[192,768]{1,0:T(8,128)(2,1)}, u32[]{:S(2)}, u32[]{:S(2)}) collective-permute-start(bf16[192,768]{1,0:T(8,128)(2,1)} %refs_8_.2), channel_id=1, source_target_pairs={{0,4},{2,6},{4,0},{6,2},{8,12},{10,14},{12,8},{14,10},{16,20},{18,... | collective-permute-start | bytes 884744 | tf_op jit(solution)/shard_map/ppermute | solution.py:399
  16.4 19.2 %copy-start.2 = (bf16[192,2048]{1,0:T(8,128)(2,1)S(1)}, bf16[192,2048]{1,0:T(8,128)(2,1)}, u32[]{:S(2)}) copy-start(bf16[192,2048]{1,0:T(8,128)(2,1)} %refs_0_.5) | copy-start | bytes 2359300
  18.0 6.7 %collective-permute-start.3 = (bf16[32,1536]{1,0:T(8,128)(2,1)S(1)}, bf16[32,1536]{1,0:T(8,128)(2,1)S(1)}, u32[]{:S(2)}, u32[]{:S(2)}) collective-permute-start(bf16[32,1536]{1,0:T(8,128)(2,1)S(1)} %get-tuple-element.69), channel_id=1, source_target_pairs={{0,16},{2,18},{4,20},{6,22},{8,24},{10,26},{12,28},{14,30},{16,0},... | collective-permute-start | bytes 294920 | tf_op jit(solution)/shard_map/ppermute | solution.py:399
  24.7 19.2 %collective-permute-start.6 = (bf16[192,2048]{1,0:T(8,128)(2,1)S(1)}, bf16[192,2048]{1,0:T(8,128)(2,1)}, u32[]{:S(2)}, u32[]{:S(2)}) collective-permute-start(bf16[192,2048]{1,0:T(8,128)(2,1)S(1)} %copy-done.1), channel_id=1, source_target_pairs={{0,8},{2,10},{4,12},{6,14},{8,0},{10,2},{12,4},{14,6},{16,24},{18,... | collective-permute-start | bytes 2359304 | tf_op jit(solution)/shard_map/ppermute | solution.py:399
  25.3 8.8 %collective-permute-start.22 = (bf16[384,384]{1,0:T(8,128)(2,1)}, bf16[384,384]{1,0:T(8,128)(2,1)}, u32[]{:S(2)}, u32[]{:S(2)}) collective-permute-start(bf16[384,384]{1,0:T(8,128)(2,1)} %pad_maximum_fusion.1.refs_0_), channel_id=1, source_target_pairs={{0,4},{2,6},{4,0},{6,2},{8,12},{10,14},{12,8},{14,10},{16,20},{18,... | collective-permute-start | bytes 884744 | tf_op jit(solution)/shard_map/ppermute | solution.py:399
  26.4 3.2 %copy-start.6 = (bf16[192,768]{1,0:T(8,128)(2,1)}, bf16[192,768]{1,0:T(8,128)(2,1)S(1)}, u32[]{:S(2)}) copy-start(bf16[192,768]{1,0:T(8,128)(2,1)S(1)} %collective-permute-done.11.refs_6_) | copy-start | bytes 884740
  26.4 9.2 %collective-permute-start.13 = (bf16[192,768]{1,0:T(8,128)(2,1)}, bf16[192,768]{1,0:T(8,128)(2,1)S(1)}, u32[]{:S(2)}, u32[]{:S(2)}) collective-permute-start(bf16[192,768]{1,0:T(8,128)(2,1)} %refs_8_.2), channel_id=1, source_target_pairs={{0,2},{2,0},{4,6},{6,4},{8,10},{10,8},{12,14},{14,12},{16,18},{18,... | collective-permute-start | bytes 884744 | tf_op jit(solution)/shard_map/ppermute | solution.py:399
  29.1 9.1 %collective-permute-start.8 = (bf16[192,768]{1,0:T(8,128)(2,1)}, bf16[192,768]{1,0:T(8,128)(2,1)S(1)}, u32[]{:S(2)}, u32[]{:S(2)}) collective-permute-start(bf16[192,768]{1,0:T(8,128)(2,1)} %refs_0_.3), channel_id=1, source_target_pairs={{0,2},{2,0},{4,6},{6,4},{8,10},{10,8},{12,14},{14,12},{16,18},{18,... | collective-permute-start | bytes 884744 | tf_op jit(solution)/shard_map/ppermute | solution.py:399
  29.1 11.2 %collective-permute-start.9 = (bf16[192,768]{1,0:T(8,128)(2,1)}, bf16[192,768]{1,0:T(8,128)(2,1)S(1)}, u32[]{:S(2)}, u32[]{:S(2)}) collective-permute-start(bf16[192,768]{1,0:T(8,128)(2,1)} %collective-permute-done.5.refs_2_), channel_id=1, source_target_pairs={{0,2},{2,0},{4,6},{6,4},{8,10},{10,8},{12,14},{14,12},{16,18},{18,... | collective-permute-start | bytes 884744 | tf_op jit(solution)/shard_map/ppermute | solution.py:399
  34.1 5.7 %collective-permute-start.4 = (bf16[2,32,1536]{2,1,0:T(8,128)(2,1)S(1)}, bf16[2,32,1536]{2,1,0:T(8,128)(2,1)S(1)}, u32[]{:S(2)}, u32[]{:S(2)}) collective-permute-start(bf16[2,32,1536]{2,1,0:T(8,128)(2,1)S(1)} %pad_maximum_fusion.3.mine_ref), channel_id=1, source_target_pairs={{0,1},{1,0},{2,3},{3,2},{4,5},{5,4},{6,7},{7,6},{8,9},{9,8},{10,11... | collective-permute-start | bytes 589832 | tf_op jit(solution)/shard_map/ppermute | solution.py:404
  35.6 14.6 %copy-start.7 = (bf16[192,768]{1,0:T(8,128)(2,1)}, bf16[192,768]{1,0:T(8,128)(2,1)S(1)}, u32[]{:S(2)}) copy-start(bf16[192,768]{1,0:T(8,128)(2,1)S(1)} %collective-permute-done.13.refs_9_) | copy-start | bytes 884740
  35.6 29.6 %collective-permute-start.17 = (bf16[192,2048]{1,0:T(8,128)(2,1)S(1)}, bf16[192,2048]{1,0:T(8,128)(2,1)}, u32[]{:S(2)}, u32[]{:S(2)}) collective-permute-start(bf16[192,2048]{1,0:T(8,128)(2,1)S(1)} %copy-done.2), channel_id=1, source_target_pairs={{0,8},{2,10},{4,12},{6,14},{8,0},{10,2},{12,4},{14,6},{16,24},{18,... | collective-permute-start | bytes 2359304 | tf_op jit(solution)/shard_map/ppermute | solution.py:399
  38.2 5.8 %copy-start.8 = (bf16[192,768]{1,0:T(8,128)(2,1)}, bf16[192,768]{1,0:T(8,128)(2,1)S(1)}, u32[]{:S(2)}) copy-start(bf16[192,768]{1,0:T(8,128)(2,1)S(1)} %collective-permute-done.8.refs_1_) | copy-start | bytes 884740
  38.2 31.1 %collective-permute-start.23 = (bf16[192,2048]{1,0:T(8,128)(2,1)S(1)}, bf16[192,2048]{1,0:T(8,128)(2,1)}, u32[]{:S(2)}, u32[]{:S(2)}) collective-permute-start(bf16[192,2048]{1,0:T(8,128)(2,1)S(1)} %copy-done.1), channel_id=1, source_target_pairs={{0,4},{2,6},{4,0},{6,2},{8,12},{10,14},{12,8},{14,10},{16,20},{18,... | collective-permute-start | bytes 2359304 | tf_op jit(solution)/shard_map/ppermute | solution.py:399
  39.7 35.9 %collective-permute-start.24 = (bf16[192,2048]{1,0:T(8,128)(2,1)S(1)}, bf16[192,2048]{1,0:T(8,128)(2,1)}, u32[]{:S(2)}, u32[]{:S(2)}) collective-permute-start(bf16[192,2048]{1,0:T(8,128)(2,1)S(1)} %copy-done.2), channel_id=1, source_target_pairs={{0,4},{2,6},{4,0},{6,2},{8,12},{10,14},{12,8},{14,10},{16,20},{18,... | collective-permute-start | bytes 2359304 | tf_op jit(solution)/shard_map/ppermute | solution.py:399
  40.3 3.6 %copy-start.9 = (bf16[192,768]{1,0:T(8,128)(2,1)}, bf16[192,768]{1,0:T(8,128)(2,1)S(1)}, u32[]{:S(2)}) copy-start(bf16[192,768]{1,0:T(8,128)(2,1)S(1)} %collective-permute-done.9.refs_3_) | copy-start | bytes 884740
  40.3 7.4 %collective-permute-start.12 = (bf16[192,768]{1,0:T(8,128)(2,1)}, bf16[192,768]{1,0:T(8,128)(2,1)S(1)}, u32[]{:S(2)}, u32[]{:S(2)}) collective-permute-start(bf16[192,768]{1,0:T(8,128)(2,1)} %copy-done.6), channel_id=1, source_target_pairs={{0,2},{2,0},{4,6},{6,4},{8,10},{10,8},{12,14},{14,12},{16,18},{18,... | collective-permute-start | bytes 884744 | tf_op jit(solution)/shard_map/ppermute | solution.py:399
  43.9 6.3 %collective-permute-start.15 = (bf16[192,768]{1,0:T(8,128)(2,1)}, bf16[192,768]{1,0:T(8,128)(2,1)}, u32[]{:S(2)}, u32[]{:S(2)}) collective-permute-start(bf16[192,768]{1,0:T(8,128)(2,1)} %collective-permute-done.14.refs_10_), channel_id=1, source_target_pairs={{0,2},{2,0},{4,6},{6,4},{8,10},{10,8},{12,14},{14,12},{16,18},{18,... | collective-permute-start | bytes 884744 | tf_op jit(solution)/shard_map/ppermute | solution.py:399
  47.7 2.5 %copy-start.10 = (bf16[192,768]{1,0:T(8,128)(2,1)}, bf16[192,768]{1,0:T(8,128)(2,1)S(1)}, u32[]{:S(2)}) copy-start(bf16[192,768]{1,0:T(8,128)(2,1)S(1)} %collective-permute-done.12.refs_7_) | copy-start | bytes 884740
  47.7 8.4 %collective-permute-start.7 = (bf16[4,32,768]{2,1,0:T(8,128)(2,1)}, bf16[4,32,768]{2,1,0:T(8,128)(2,1)}, u32[]{:S(2)}, u32[]{:S(2)}) collective-permute-start(bf16[4,32,768]{2,1,0:T(8,128)(2,1)} %pad_maximum_fusion.2.mine_ref), channel_id=1, source_target_pairs={{0,1},{1,0},{2,3},{3,2},{4,5},{5,4},{6,7},{7,6},{8,9},{9,8},{10,11... | collective-permute-start | bytes 589832 | tf_op jit(solution)/shard_map/ppermute | solution.py:404
  50.2 42.1 %collective-permute-start.25 = (bf16[1024,384]{1,0:T(8,128)(2,1)S(1)}, bf16[1024,384]{1,0:T(8,128)(2,1)S(1)}, u32[]{:S(2)}, u32[]{:S(2)}) collective-permute-start(bf16[1024,384]{1,0:T(8,128)(2,1)S(1)} %pad_maximum_fusion.refs_0_), channel_id=1, source_target_pairs={{0,4},{2,6},{4,0},{6,2},{8,12},{10,14},{12,8},{14,10},{16,20},{18,... | collective-permute-start | bytes 2359304 | tf_op jit(solution)/shard_map/ppermute | solution.py:399
  56.1 9.2 %collective-permute-start.16 = (bf16[384,384]{1,0:T(8,128)(2,1)}, bf16[384,384]{1,0:T(8,128)(2,1)}, u32[]{:S(2)}, u32[]{:S(2)}) collective-permute-start(bf16[384,384]{1,0:T(8,128)(2,1)} %pad_maximum_fusion.1.refs_0_), channel_id=1, source_target_pairs={{0,8},{2,10},{4,12},{6,14},{8,0},{10,2},{12,4},{14,6},{16,24},{18,... | collective-permute-start | bytes 884744 | tf_op jit(solution)/shard_map/ppermute | solution.py:399
  65.2 30.7 %collective-permute-start.18 = (bf16[64,2432]{1,0:T(8,128)(2,1)}, bf16[64,2432]{1,0:T(8,128)(2,1)}, u32[]{:S(2)}, u32[]{:S(2)}) collective-permute-start(bf16[64,2432]{1,0:T(8,128)(2,1)} %get-tuple-element.82), channel_id=1, source_target_pairs={{0,8},{2,10},{4,12},{6,14},{8,16},{10,18},{12,20},{14,22},{16,24},... | collective-permute-start | bytes 933896 | tf_op jit(solution)/shard_map/ppermute | solution.py:418
  65.7 30.3 %collective-permute-start.19 = (bf16[64,2432]{1,0:T(8,128)(2,1)}, bf16[64,2432]{1,0:T(8,128)(2,1)}, u32[]{:S(2)}, u32[]{:S(2)}) collective-permute-start(bf16[64,2432]{1,0:T(8,128)(2,1)} %get-tuple-element.83), channel_id=1, source_target_pairs={{0,16},{2,18},{4,20},{6,22},{8,24},{10,26},{12,28},{14,30},{16,0},... | collective-permute-start | bytes 933896 | tf_op jit(solution)/shard_map/ppermute | solution.py:418
  69.3 26.7 %collective-permute-start.20 = (bf16[64,2432]{1,0:T(8,128)(2,1)}, bf16[64,2432]{1,0:T(8,128)(2,1)}, u32[]{:S(2)}, u32[]{:S(2)}) collective-permute-start(bf16[64,2432]{1,0:T(8,128)(2,1)} %get-tuple-element.84), channel_id=1, source_target_pairs={{0,24},{2,26},{4,28},{6,30},{8,0},{10,2},{12,4},{14,6},{16,8},{18,... | collective-permute-start | bytes 933896 | tf_op jit(solution)/shard_map/ppermute | solution.py:418
  75.6 20.4 %collective-permute-start.21 = (bf16[384,384]{1,0:T(8,128)(2,1)}, bf16[384,384]{1,0:T(8,128)(2,1)}, u32[]{:S(2)}, u32[]{:S(2)}) collective-permute-start(bf16[384,384]{1,0:T(8,128)(2,1)} %collective-permute-done.16.refs_4_), channel_id=1, source_target_pairs={{0,4},{2,6},{4,0},{6,2},{8,12},{10,14},{12,8},{14,10},{16,20},{18,... | collective-permute-start | bytes 884744 | tf_op jit(solution)/shard_map/ppermute | solution.py:399
  92.3 14.6 %collective-permute-start.28 = (bf16[384,384]{1,0:T(8,128)(2,1)}, bf16[384,384]{1,0:T(8,128)(2,1)}, u32[]{:S(2)}, u32[]{:S(2)}) collective-permute-start(bf16[384,384]{1,0:T(8,128)(2,1)} %collective-permute-done.22.refs_2_), channel_id=1, source_target_pairs={{0,2},{2,0},{4,6},{6,4},{8,10},{10,8},{12,14},{14,12},{16,18},{18,... | collective-permute-start | bytes 884744 | tf_op jit(solution)/shard_map/ppermute | solution.py:399
  99.7 6.6 %collective-permute-start.26 = (bf16[64,768]{1,0:T(8,128)(2,1)}, bf16[64,768]{1,0:T(8,128)(2,1)S(1)}, u32[]{:S(2)}, u32[]{:S(2)}) collective-permute-start(bf16[64,768]{1,0:T(8,128)(2,1)} %get-tuple-element.94.own_ref), channel_id=1, source_target_pairs={{0,16},{2,18},{4,20},{6,22},{8,24},{10,26},{12,28},{14,30},{16,0},... | collective-permute-start | bytes 294920 | tf_op jit(solution)/shard_map/ppermute | solution.py:399
  100.9 22.4 %collective-permute-start.33 = (bf16[192,2048]{1,0:T(8,128)(2,1)}, bf16[192,2048]{1,0:T(8,128)(2,1)}, u32[]{:S(2)}, u32[]{:S(2)}) collective-permute-start(bf16[192,2048]{1,0:T(8,128)(2,1)} %collective-permute-done.6.refs_4_), channel_id=1, source_target_pairs={{0,4},{2,6},{4,0},{6,2},{8,12},{10,14},{12,8},{14,10},{16,20},{18,... | collective-permute-start | bytes 2359304 | tf_op jit(solution)/shard_map/ppermute | solution.py:399
  101.4 5.6 %collective-permute-start.29 = (bf16[384,384]{1,0:T(8,128)(2,1)}, bf16[384,384]{1,0:T(8,128)(2,1)}, u32[]{:S(2)}, u32[]{:S(2)}) collective-permute-start(bf16[384,384]{1,0:T(8,128)(2,1)} %collective-permute-done.16.refs_4_), channel_id=1, source_target_pairs={{0,2},{2,0},{4,6},{6,4},{8,10},{10,8},{12,14},{14,12},{16,18},{18,... | collective-permute-start | bytes 884744 | tf_op jit(solution)/shard_map/ppermute | solution.py:399
  101.4 5.5 %collective-permute-start.27 = (bf16[384,384]{1,0:T(8,128)(2,1)}, bf16[384,384]{1,0:T(8,128)(2,1)}, u32[]{:S(2)}, u32[]{:S(2)}) collective-permute-start(bf16[384,384]{1,0:T(8,128)(2,1)} %pad_maximum_fusion.1.refs_0_), channel_id=1, source_target_pairs={{0,2},{2,0},{4,6},{6,4},{8,10},{10,8},{12,14},{14,12},{16,18},{18,... | collective-permute-start | bytes 884744 | tf_op jit(solution)/shard_map/ppermute | solution.py:399
  106.3 1.9 collective-permute-start.30
  107.0 19.3 %collective-permute-start.32 = (bf16[1024,384]{1,0:T(8,128)(2,1)S(1)}, bf16[1024,384]{1,0:T(8,128)(2,1)S(1)}, u32[]{:S(2)}, u32[]{:S(2)}) collective-permute-start(bf16[1024,384]{1,0:T(8,128)(2,1)S(1)} %pad_maximum_fusion.refs_0_), channel_id=1, source_target_pairs={{0,8},{2,10},{4,12},{6,14},{8,0},{10,2},{12,4},{14,6},{16,24},{18,... | collective-permute-start | bytes 2359304 | tf_op jit(solution)/shard_map/ppermute | solution.py:399
  111.9 11.4 %collective-permute-start.31 = (bf16[128,1536]{1,0:T(8,128)(2,1)}, bf16[128,1536]{1,0:T(8,128)(2,1)S(1)}, u32[]{:S(2)}, u32[]{:S(2)}) collective-permute-start(bf16[128,1536]{1,0:T(8,128)(2,1)} %shard_map.142.a_ref), channel_id=1, source_target_pairs={{0,1},{1,0},{2,3},{3,2},{4,5},{5,4},{6,7},{7,6},{8,9},{9,8},{10,11... | collective-permute-start | bytes 1179656 | tf_op jit(solution)/shard_map/ppermute | solution.py:404
  113.3 15.6 %collective-permute-start.36 = (bf16[192,2048]{1,0:T(8,128)(2,1)}, bf16[192,2048]{1,0:T(8,128)(2,1)S(1)}, u32[]{:S(2)}, u32[]{:S(2)}) collective-permute-start(bf16[192,2048]{1,0:T(8,128)(2,1)} %collective-permute-done.6.refs_4_), channel_id=1, source_target_pairs={{0,2},{2,0},{4,6},{6,4},{8,10},{10,8},{12,14},{14,12},{16,18},{18,... | collective-permute-start | bytes 2359304 | tf_op jit(solution)/shard_map/ppermute | solution.py:399
  113.3 15.6 %collective-permute-start.35 = (bf16[192,2048]{1,0:T(8,128)(2,1)}, bf16[192,2048]{1,0:T(8,128)(2,1)S(1)}, u32[]{:S(2)}, u32[]{:S(2)}) collective-permute-start(bf16[192,2048]{1,0:T(8,128)(2,1)} %collective-permute-done.23.refs_2_), channel_id=1, source_target_pairs={{0,2},{2,0},{4,6},{6,4},{8,10},{10,8},{12,14},{14,12},{16,18},{18,... | collective-permute-start | bytes 2359304 | tf_op jit(solution)/shard_map/ppermute | solution.py:399
  123.2 5.8 %collective-permute-start.34 = (bf16[192,2048]{1,0:T(8,128)(2,1)S(1)}, bf16[192,2048]{1,0:T(8,128)(2,1)S(1)}, u32[]{:S(2)}, u32[]{:S(2)}) collective-permute-start(bf16[192,2048]{1,0:T(8,128)(2,1)S(1)} %copy-done.1), channel_id=1, source_target_pairs={{0,2},{2,0},{4,6},{6,4},{8,10},{10,8},{12,14},{14,12},{16,18},{18,... | collective-permute-start | bytes 2359304 | tf_op jit(solution)/shard_map/ppermute | solution.py:399
  123.2 5.8 %collective-permute-start.37 = (bf16[192,2048]{1,0:T(8,128)(2,1)}, bf16[192,2048]{1,0:T(8,128)(2,1)S(1)}, u32[]{:S(2)}, u32[]{:S(2)}) collective-permute-start(bf16[192,2048]{1,0:T(8,128)(2,1)} %collective-permute-done.33.refs_6_), channel_id=1, source_target_pairs={{0,2},{2,0},{4,6},{6,4},{8,10},{10,8},{12,14},{14,12},{16,18},{18,... | collective-permute-start | bytes 2359304 | tf_op jit(solution)/shard_map/ppermute | solution.py:399
  126.3 18.7 %collective-permute-start.42 = (bf16[192,2048]{1,0:T(8,128)(2,1)}, bf16[192,2048]{1,0:T(8,128)(2,1)S(1)}, u32[]{:S(2)}, u32[]{:S(2)}) collective-permute-start(bf16[192,2048]{1,0:T(8,128)(2,1)} %collective-permute-done.17.refs_4_), channel_id=1, source_target_pairs={{0,4},{2,6},{4,0},{6,2},{8,12},{10,14},{12,8},{14,10},{16,20},{18,... | collective-permute-start | bytes 2359304 | tf_op jit(solution)/shard_map/ppermute | solution.py:399
  129.0 4.0 %copy-start.3 = (bf16[192,2048]{1,0:T(8,128)(2,1)S(1)}, bf16[192,2048]{1,0:T(8,128)(2,1)}, u32[]{:S(2)}) copy-start(bf16[192,2048]{1,0:T(8,128)(2,1)} %refs_0_.5) | copy-start | bytes 2359300
  132.1 14.2 %collective-permute-start.38 = (bf16[64,2176]{1,0:T(8,128)(2,1)S(1)}, bf16[64,2176]{1,0:T(8,128)(2,1)S(1)}, u32[]{:S(2)}, u32[]{:S(2)}) collective-permute-start(bf16[64,2176]{1,0:T(8,128)(2,1)S(1)} %get-tuple-element.108), channel_id=1, source_target_pairs={{0,16},{2,18},{4,20},{6,22},{8,24},{10,26},{12,28},{14,30},{16,0},... | collective-permute-start | bytes 835592 | tf_op jit(solution)/shard_map/ppermute | solution.py:399
  132.5 15.2 %collective-permute-start.41 = (bf16[192,2048]{1,0:T(8,128)(2,1)}, bf16[192,2048]{1,0:T(8,128)(2,1)S(1)}, u32[]{:S(2)}, u32[]{:S(2)}) collective-permute-start(bf16[192,2048]{1,0:T(8,128)(2,1)} %collective-permute-done.17.refs_4_), channel_id=1, source_target_pairs={{0,2},{2,0},{4,6},{6,4},{8,10},{10,8},{12,14},{14,12},{16,18},{18,... | collective-permute-start | bytes 2359304 | tf_op jit(solution)/shard_map/ppermute | solution.py:399
  132.5 15.2 %collective-permute-start.40 = (bf16[192,2048]{1,0:T(8,128)(2,1)}, bf16[192,2048]{1,0:T(8,128)(2,1)S(1)}, u32[]{:S(2)}, u32[]{:S(2)}) collective-permute-start(bf16[192,2048]{1,0:T(8,128)(2,1)} %collective-permute-done.24.refs_2_), channel_id=1, source_target_pairs={{0,2},{2,0},{4,6},{6,4},{8,10},{10,8},{12,14},{14,12},{16,18},{18,... | collective-permute-start | bytes 2359304 | tf_op jit(solution)/shard_map/ppermute | solution.py:399
  133.0 14.7 %collective-permute-start.39 = (bf16[192,2048]{1,0:T(8,128)(2,1)S(1)}, bf16[192,2048]{1,0:T(8,128)(2,1)S(1)}, u32[]{:S(2)}, u32[]{:S(2)}) collective-permute-start(bf16[192,2048]{1,0:T(8,128)(2,1)S(1)} %copy-done.3), channel_id=1, source_target_pairs={{0,2},{2,0},{4,6},{6,4},{8,10},{10,8},{12,14},{14,12},{16,18},{18,... | collective-permute-start | bytes 2359304 | tf_op jit(solution)/shard_map/ppermute | solution.py:399
  146.3 2.3 %collective-permute-start.43 = (bf16[192,2048]{1,0:T(8,128)(2,1)S(1)}, bf16[192,2048]{1,0:T(8,128)(2,1)S(1)}, u32[]{:S(2)}, u32[]{:S(2)}) collective-permute-start(bf16[192,2048]{1,0:T(8,128)(2,1)S(1)} %collective-permute-done.42.refs_6_), channel_id=1, source_target_pairs={{0,2},{2,0},{4,6},{6,4},{8,10},{10,8},{12,14},{14,12},{16,18},{18,... | collective-permute-start | bytes 2359304 | tf_op jit(solution)/shard_map/ppermute | solution.py:399
  146.3 20.1 %collective-permute-start.49 = (bf16[1024,384]{1,0:T(8,128)(2,1)S(1)}, bf16[1024,384]{1,0:T(8,128)(2,1)}, u32[]{:S(2)}, u32[]{:S(2)}) collective-permute-start(bf16[1024,384]{1,0:T(8,128)(2,1)S(1)} %collective-permute-done.32.refs_4_), channel_id=1, source_target_pairs={{0,4},{2,6},{4,0},{6,2},{8,12},{10,14},{12,8},{14,10},{16,20},{18,... | collective-permute-start | bytes 2359304 | tf_op jit(solution)/shard_map/ppermute | solution.py:399
  151.5 14.9 %collective-permute-start.44 = (bf16[64,2048]{1,0:T(8,128)(2,1)S(1)}, bf16[64,2048]{1,0:T(8,128)(2,1)S(1)}, u32[]{:S(2)}, u32[]{:S(2)}) collective-permute-start(bf16[64,2048]{1,0:T(8,128)(2,1)S(1)} %get-tuple-element.117), channel_id=1, source_target_pairs={{0,16},{2,18},{4,20},{6,22},{8,24},{10,26},{12,28},{14,30},{16,0},... | collective-permute-start | bytes 786440 | tf_op jit(solution)/shard_map/ppermute | solution.py:399
  151.6 29.2 %collective-permute-start.48 = (bf16[1024,384]{1,0:T(8,128)(2,1)S(1)}, bf16[1024,384]{1,0:T(8,128)(2,1)}, u32[]{:S(2)}, u32[]{:S(2)}) collective-permute-start(bf16[1024,384]{1,0:T(8,128)(2,1)S(1)} %collective-permute-done.32.refs_4_), channel_id=1, source_target_pairs={{0,2},{2,0},{4,6},{6,4},{8,10},{10,8},{12,14},{14,12},{16,18},{18,... | collective-permute-start | bytes 2359304 | tf_op jit(solution)/shard_map/ppermute | solution.py:399
  151.8 29.0 %collective-permute-start.47 = (bf16[1024,384]{1,0:T(8,128)(2,1)S(1)}, bf16[1024,384]{1,0:T(8,128)(2,1)}, u32[]{:S(2)}, u32[]{:S(2)}) collective-permute-start(bf16[1024,384]{1,0:T(8,128)(2,1)S(1)} %collective-permute-done.25.refs_2_), channel_id=1, source_target_pairs={{0,2},{2,0},{4,6},{6,4},{8,10},{10,8},{12,14},{14,12},{16,18},{18,... | collective-permute-start | bytes 2359304 | tf_op jit(solution)/shard_map/ppermute | solution.py:399
  152.2 28.6 %collective-permute-start.46 = (bf16[1024,384]{1,0:T(8,128)(2,1)S(1)}, bf16[1024,384]{1,0:T(8,128)(2,1)}, u32[]{:S(2)}, u32[]{:S(2)}) collective-permute-start(bf16[1024,384]{1,0:T(8,128)(2,1)S(1)} %pad_maximum_fusion.refs_0_), channel_id=1, source_target_pairs={{0,2},{2,0},{4,6},{6,4},{8,10},{10,8},{12,14},{14,12},{16,18},{18,... | collective-permute-start | bytes 2359304 | tf_op jit(solution)/shard_map/ppermute | solution.py:399
  166.4 14.5 %collective-permute-start.50 = (bf16[1024,384]{1,0:T(8,128)(2,1)}, bf16[1024,384]{1,0:T(8,128)(2,1)}, u32[]{:S(2)}, u32[]{:S(2)}) collective-permute-start(bf16[1024,384]{1,0:T(8,128)(2,1)} %collective-permute-done.49.refs_6_), channel_id=1, source_target_pairs={{0,2},{2,0},{4,6},{6,4},{8,10},{10,8},{12,14},{14,12},{16,18},{18,... | collective-permute-start | bytes 2359304 | tf_op jit(solution)/shard_map/ppermute | solution.py:399
  166.8 14.0 %collective-permute-start.45 = (bf16[64,2048]{1,0:T(8,128)(2,1)S(1)}, bf16[64,2048]{1,0:T(8,128)(2,1)S(1)}, u32[]{:S(2)}, u32[]{:S(2)}) collective-permute-start(bf16[64,2048]{1,0:T(8,128)(2,1)S(1)} %multiply_convert_fusion.own_ref), channel_id=1, source_target_pairs={{0,16},{2,18},{4,20},{6,22},{8,24},{10,26},{12,28},{14,30},{16,0},... | collective-permute-start | bytes 786440 | tf_op jit(solution)/shard_map/ppermute | solution.py:399
  185.4 7.0 %collective-permute-start.51 = (bf16[2,32,1536]{2,1,0:T(8,128)(2,1)S(1)}, bf16[2,32,1536]{2,1,0:T(8,128)(2,1)S(1)}, u32[]{:S(2)}, u32[]{:S(2)}) collective-permute-start(bf16[2,32,1536]{2,1,0:T(8,128)(2,1)S(1)} %dynamic-slice_bitcast_fusion), channel_id=1, source_target_pairs={{0,1},{1,0},{2,3},{3,2},{4,5},{5,4},{6,7},{7,6},{8,9},{9,8},{10,11... | collective-permute-start | bytes 589832 | tf_op jit(solution)/shard_map/ppermute | solution.py:404
  193.4 6.9 %collective-permute-start.52 = (bf16[32,1536]{1,0:T(8,128)(2,1)S(1)}, bf16[32,1536]{1,0:T(8,128)(2,1)S(1)}, u32[]{:S(2)}, u32[]{:S(2)}) collective-permute-start(bf16[32,1536]{1,0:T(8,128)(2,1)S(1)} %get-tuple-element.130), channel_id=1, source_target_pairs={{0,16},{2,18},{4,20},{6,22},{8,24},{10,26},{12,28},{14,30},{16,0},... | collective-permute-start | bytes 294920 | tf_op jit(solution)/shard_map/ppermute | solution.py:399
  (7 other events, 5.4 us)

commit v6 on v5

--- a/solution.py
+++ b/solution.py
@@ -253,11 +253,12 @@
         c.start()
     a_ref[:keep] = own_ref[...]
     a_ref[keep:] = got_ref[...]
+    below, above = wide // 128 * 128, -(-wide // 128) * 128
     for k in range(OCT):
         copies[k].wait()
-        lower = dot(a_ref[:, : depth // 2], held[k])
-        upper = dot(a_ref[:, depth // 2 :], held[k])
-        parts[place[0] ^ k] = (lower[:, :wide] + upper[:, wide:]).astype(BF)
+        lower = dot(a_ref[:, : depth // 2], held[k, :, :above])
+        upper = dot(a_ref[:, depth // 2 :], held[k, :, below:])
+        parts[place[0] ^ k] = (lower[:, :wide] + upper[:, wide - below :]).astype(BF)
     for i in range(OCT):
         out_ref[:, i * wide : (i + 1) * wide] = parts[i]
 
@@ -293,10 +294,11 @@
     a_ref[:keep] = own_ref[...]
     a_ref[keep:] = got_ref[...]
     wide = weights[0].shape[-1] // 2
+    below, above = wide // 128 * 128, -(-wide // 128) * 128
     for k in range(OCT):
-        lower = dot(a_ref[:, : depth // 2], weights[k][...])
-        upper = dot(a_ref[:, depth // 2 :], weights[k][...])
-        parts[place[0] ^ k] = (lower[:, :wide] + upper[:, wide:]).astype(BF)
+        lower = dot(a_ref[:, : depth // 2], weights[k][:, :above])
+        upper = dot(a_ref[:, depth // 2 :], weights[k][:, below:])
+        parts[place[0] ^ k] = (lower[:, :wide] + upper[:, wide - below :]).astype(BF)
     for i in range(OCT):
         out_ref[:, i * wide : (i + 1) * wide] = parts[i]
 

time: 202 us -> 201 us (level)
  no operation moved by 1% of the time
where the time goes in v6:
time: 201 us
  waiting for transfers between devices  120 us (60%)
  starting transfers between devices  37.9 us (19%)
  Pallas kernels  24.6 us (12%)
  local copies, waits for them, and re-layouts  9.77 us (5%)
  other arithmetic  6.83 us (3%)
    ppermute x43, waiting for transfers between devices, swap(): return lambda x: lax.ppermute(x, 'group', pairs)  98.5 us
    ppermute x43, starting transfers between devices, swap(): return lambda x: lax.ppermute(x, 'group', pairs)  20.7 us
    ppermute x4, waiting for transfers between devices, other_head(): return lax.ppermute(x, 'head', [(0, 1), (1, 0)])  19.8 us
    ppermute x6, starting transfers between devices, turn(): return lambda x: lax.ppermute(x, 'group', pairs)  9.87 us
    ppermute x4, starting transfers between devices, other_head(): return lax.ppermute(x, 'head', [(0, 1), (1, 0)])  7.28 us
    pallas_call x2, Pallas kernels, rows_product(): pl.pallas_call(rows_kernel, grid_spec=pltpu.PrefetchScalarGridSpec(num_sc...  5.99 us
    pallas_call x1, Pallas kernels, first_rows_product(): pl.pallas_call(first_rows_kernel, grid_spec=pltpu.PrefetchScalarGridSpec(...  5.05 us
    unnamed x40, local copies, waits for them, and re-layouts  4.28 us
  transfers between devices with their start and end apart: 53, of which 22 were waited for; matrix products, arithmetic and copies ran while one was open for 6% of the time, Pallas kernels for 10%

profile of v6, /device:TPU:0, one launch (start us, length us, event | category | flops | bytes accessed | tf_op | source)
XLA Modules:
  0.0 200.5 jit_solution(11596814445098625836)
XLA Ops:
  0.6 3.0 %collective-permute-start.11 = (bf16[192,768]{1,0:T(8,128)(2,1)}, bf16[192,768]{1,0:T(8,128)(2,1)S(1)}, u32[]{:S(2)}, u32[]{:S(2)}) collective-permute-start(bf16[192,768]{1,0:T(8,128)(2,1)} %refs_4_.1), channel_id=1, source_target_pairs={{0,4},{2,6},{4,0},{6,2},{8,12},{10,14},{12,8},{14,10},{16,20},{18,... | collective-permute-start | bytes 884744 | tf_op jit(solution)/shard_map/ppermute | solution.py:401
  3.6 1.0 dynamic-slice_bitcast_fusion.1
  4.6 0.9 constant_dynamic-slice_fusion.1
  5.5 3.7 %collective-permute-start = (bf16[32,768]{1,0:T(8,128)(2,1)S(1)}, bf16[32,768]{1,0:T(8,128)(2,1)S(1)}, u32[]{:S(2)}, u32[]{:S(2)}) collective-permute-start(bf16[32,768]{1,0:T(8,128)(2,1)S(1)} %get-tuple-element.66), channel_id=1, source_target_pairs={{0,24},{2,26},{4,28},{6,30},{8,0},{10,2},{12,4},{14,6},{16,8},{18,... | collective-permute-start | bytes 147464 | tf_op jit(solution)/shard_map/ppermute | solution.py:420
  9.2 1.0 collective-permute-start.2
  11.2 0.6 slice_bitcast_fusion.2
  12.5 0.6 collective-permute-start.5
  13.1 2.1 %collective-permute-done.1 = bf16[32,768]{1,0:T(8,128)(2,1)S(1)} collective-permute-done((bf16[32,768]{1,0:T(8,128)(2,1)S(1)}, bf16[32,768]{1,0:T(8,128)(2,1)S(1)}, u32[]{:S(2)}, u32[]{:S(2)}) %collective-permute-start.1) | collective-permute-done | bytes 49184 | tf_op jit(solution)/shard_map/ppermute | solution.py:420
  15.8 0.5 copy-done.15
  16.4 1.6 pad_maximum_fusion.2.mine_ref
  18.0 1.1 collective-permute-start.3
  19.1 0.8 pad_maximum_fusion.1.refs_0_
  19.9 4.7 %collective-permute-done.3 = bf16[32,1536]{1,0:T(8,128)(2,1)S(1)} collective-permute-done((bf16[32,1536]{1,0:T(8,128)(2,1)S(1)}, bf16[32,1536]{1,0:T(8,128)(2,1)S(1)}, u32[]{:S(2)}, u32[]{:S(2)}) %collective-permute-start.3) | collective-permute-done | bytes 98336 | tf_op jit(solution)/shard_map/ppermute | solution.py:401
  25.3 1.1 collective-permute-start.22
  26.5 2.6 %collective-permute-done.14.refs_10_ = bf16[192,768]{1,0:T(8,128)(2,1)} collective-permute-done((bf16[192,768]{1,0:T(8,128)(2,1)}, bf16[192,768]{1,0:T(8,128)(2,1)}, u32[]{:S(2)}, u32[]{:S(2)}) %collective-permute-start.14) | collective-permute-done | bytes 294944 | tf_op jit(solution)/shard_map/ppermute | solution.py:401
  29.6 4.4 %collective-permute-done.22.refs_2_ = bf16[384,384]{1,0:T(8,128)(2,1)} collective-permute-done((bf16[384,384]{1,0:T(8,128)(2,1)}, bf16[384,384]{1,0:T(8,128)(2,1)}, u32[]{:S(2)}, u32[]{:S(2)}) %collective-permute-start.22) | collective-permute-done | bytes 294944 | tf_op jit(solution)/shard_map/ppermute | solution.py:401
  34.1 1.5 collective-permute-start.4
  35.6 2.5 %collective-permute-start.17 = (bf16[192,2048]{1,0:T(8,128)(2,1)S(1)}, bf16[192,2048]{1,0:T(8,128)(2,1)}, u32[]{:S(2)}, u32[]{:S(2)}) collective-permute-start(bf16[192,2048]{1,0:T(8,128)(2,1)S(1)} %copy-done.2), channel_id=1, source_target_pairs={{0,8},{2,10},{4,12},{6,14},{8,0},{10,2},{12,4},{14,6},{16,24},{18,... | collective-permute-start | bytes 2359304 | tf_op jit(solution)/shard_map/ppermute | solution.py:401
  38.7 1.0 collective-permute-done.4.others_ref
  40.3 3.6 %collective-permute-done.6.refs_4_ = bf16[192,2048]{1,0:T(8,128)(2,1)} collective-permute-done((bf16[192,2048]{1,0:T(8,128)(2,1)S(1)}, bf16[192,2048]{1,0:T(8,128)(2,1)}, u32[]{:S(2)}, u32[]{:S(2)}) %collective-permute-start.6) | collective-permute-done | bytes 786464 | tf_op jit(solution)/shard_map/ppermute | solution.py:401
  43.9 0.8 dynamic_slice.41
  44.7 0.8 dynamic_slice.40
  45.5 0.6 reshape.121.gain_ref
  46.1 1.6 fusion.2
  47.7 2.5 %collective-permute-start.7 = (bf16[4,32,768]{2,1,0:T(8,128)(2,1)}, bf16[4,32,768]{2,1,0:T(8,128)(2,1)}, u32[]{:S(2)}, u32[]{:S(2)}) collective-permute-start(bf16[4,32,768]{2,1,0:T(8,128)(2,1)} %pad_maximum_fusion.2.mine_ref), channel_id=1, source_target_pairs={{0,1},{1,0},{2,3},{3,2},{4,5},{5,4},{6,7},{7,6},{8,9},{9,8},{10,11... | collective-permute-start | bytes 589832 | tf_op jit(solution)/shard_map/ppermute | solution.py:406
  50.2 1.7 collective-permute-start.25
  51.9 4.2 %collective-permute-done.7.others_ref = bf16[4,32,768]{2,1,0:T(8,128)(2,1)} collective-permute-done((bf16[4,32,768]{2,1,0:T(8,128)(2,1)}, bf16[4,32,768]{2,1,0:T(8,128)(2,1)}, u32[]{:S(2)}, u32[]{:S(2)}) %collective-permute-start.7) | collective-permute-done | bytes 196640 | tf_op jit(solution)/shard_map/ppermute | solution.py:406
  56.1 0.6 collective-permute-start.16
  56.7 2.1 %shard_map.139 = (bf16[256,768]{1,0:T(8,128)(2,1)}, bf16[4,256,192]{2,1,0:T(8,128)(2,1)}, bf16[192,128]{1,0:T(8,128)(2,1)}, f32[64,128]{1,0:T(8,128)}) custom-call(s32[1]{0:T(128)} %bitcast.row, bf16[4,32,768]{2,1,0:T(8,128)(2,1)} %pad_maximum_fusion.2.mine_ref, bf16[4,32,768]{2,1,0:T(8,128)(2,1)} %collective-permute-done.7.others_ref, ...), custom_call_target="tpu_custom_call" | custom-call | tf_op jit(solution)/shard_map/pallas_call | solution.py:139
  58.7 5.0 %shard_map.140 = (bf16[64,2432]{1,0:T(8,128)(2,1)}, bf16[64,2432]{1,0:T(8,128)(2,1)}, bf16[64,2432]{1,0:T(8,128)(2,1)}, f32[64,2304]{1,0:T(8,128)}) custom-call(s32[1]{0:T(128)} %bitcast.8.place, bf16[4,256,192]{2,1,0:T(8,128)(2,1)} %get-tuple-element.74.lhs, bf16[192,128]{1,0:T(8,128)(2,1)} %get-tuple-element.75.coded_ref, bf16[192,768]{1,0:T(8,128)(2,1)} %refs_0_.3, ...), custom_call_target="tpu_custom_call" | custom-call | tf_op jit(solution)/shard_map/pallas_call | solution.py:233
  63.8 1.5 collective-permute-done.16.refs_4_
  65.7 3.6 %collective-permute-start.19 = (bf16[64,2432]{1,0:T(8,128)(2,1)}, bf16[64,2432]{1,0:T(8,128)(2,1)}, u32[]{:S(2)}, u32[]{:S(2)}) collective-permute-start(bf16[64,2432]{1,0:T(8,128)(2,1)} %get-tuple-element.83), channel_id=1, source_target_pairs={{0,16},{2,18},{4,20},{6,22},{8,24},{10,26},{12,28},{14,30},{16,0},... | collective-permute-start | bytes 933896 | tf_op jit(solution)/shard_map/ppermute | solution.py:420
  69.3 1.2 collective-permute-start.20
  70.4 5.2 %collective-permute-done.24.refs_2_ = bf16[192,2048]{1,0:T(8,128)(2,1)} collective-permute-done((bf16[192,2048]{1,0:T(8,128)(2,1)S(1)}, bf16[192,2048]{1,0:T(8,128)(2,1)}, u32[]{:S(2)}, u32[]{:S(2)}) %collective-permute-start.24) | collective-permute-done | bytes 786464 | tf_op jit(solution)/shard_map/ppermute | solution.py:401
  76.1 16.2 %collective-permute-done.25.refs_2_ = bf16[1024,384]{1,0:T(8,128)(2,1)S(1)} collective-permute-done((bf16[1024,384]{1,0:T(8,128)(2,1)S(1)}, bf16[1024,384]{1,0:T(8,128)(2,1)S(1)}, u32[]{:S(2)}, u32[]{:S(2)}) %collective-permute-start.25) | collective-permute-done | bytes 786464 | tf_op jit(solution)/shard_map/ppermute | solution.py:401
  92.3 0.7 copy.28.refs_9_
  93.0 2.9 %collective-permute-done.21.refs_6_ = bf16[384,384]{1,0:T(8,128)(2,1)} collective-permute-done((bf16[384,384]{1,0:T(8,128)(2,1)}, bf16[384,384]{1,0:T(8,128)(2,1)}, u32[]{:S(2)}, u32[]{:S(2)}) %collective-permute-start.21) | collective-permute-done | bytes 294944 | tf_op jit(solution)/shard_map/ppermute | solution.py:401
  96.0 3.7 %shard_map.141 = (bf16[64,768]{1,0:T(8,128)(2,1)}, bf16[64,768]{1,0:T(8,128)(2,1)}, bf16[64,768]{1,0:T(8,128)(2,1)}) custom-call(f32[64,2304]{1,0:T(8,128)} %get-tuple-element.76.refs_0_, bf16[64,2432]{1,0:T(8,128)(2,1)} %collective-permute-done.18.refs_1_, bf16[64,2432]{1,0:T(8,128)(2,1)} %collective-permute-done.19.refs_2_, ...), custom_call_target="tpu_custom_call" | custom-call | tf_op jit(solution)/shard_map/pallas_call | solution.py:377
  99.7 1.2 collective-permute-start.26
  100.9 0.5 collective-permute-start.33
  101.9 4.4 %collective-permute-done.26.got_ref = bf16[64,768]{1,0:T(8,128)(2,1)S(1)} collective-permute-done((bf16[64,768]{1,0:T(8,128)(2,1)}, bf16[64,768]{1,0:T(8,128)(2,1)S(1)}, u32[]{:S(2)}, u32[]{:S(2)}) %collective-permute-start.26) | collective-permute-done | bytes 98336 | tf_op jit(solution)/shard_map/ppermute | solution.py:401
  106.3 0.6 copy-done.12
  107.0 1.3 collective-permute-done.30.refs_7_
  108.2 3.3 %shard_map.142.a_ref = bf16[128,1536]{1,0:T(8,128)(2,1)} custom-call(s32[1]{0:T(128)} %bitcast.7.place, bf16[64,768]{1,0:T(8,128)(2,1)} %get-tuple-element.94.own_ref, bf16[64,768]{1,0:T(8,128)(2,1)} %copy-done.12, bf16[384,384]{1,0:T(8,128)(2,1)} %pad_maximum_fusion.1.refs_0_, bf16[384,384]{1,0:T(8,128)(2,1)} %collective-permute-done.27.refs_1_, ...), custom_call_target="tpu_custom_call" | custom-call | tf_op jit(solution)/shard_map/pallas_call | solution.py:312
  111.6 1.5 collective-permute-start.31
  113.6 9.4 %collective-permute-done.31.b_ref = bf16[128,1536]{1,0:T(8,128)(2,1)S(1)} collective-permute-done((bf16[128,1536]{1,0:T(8,128)(2,1)}, bf16[128,1536]{1,0:T(8,128)(2,1)S(1)}, u32[]{:S(2)}, u32[]{:S(2)}) %collective-permute-start.31) | collective-permute-done | bytes 393248 | tf_op jit(solution)/shard_map/ppermute | solution.py:406
  123.5 2.8 %collective-permute-done.32.refs_4_ = bf16[1024,384]{1,0:T(8,128)(2,1)S(1)} collective-permute-done((bf16[1024,384]{1,0:T(8,128)(2,1)S(1)}, bf16[1024,384]{1,0:T(8,128)(2,1)S(1)}, u32[]{:S(2)}, u32[]{:S(2)}) %collective-permute-start.32) | collective-permute-done | bytes 786464 | tf_op jit(solution)/shard_map/ppermute | solution.py:401
  126.3 0.6 collective-permute-start.42
  126.9 1.0 copy-done
  128.2 0.7 copy-done.4
  129.0 3.1 %shard_map.144 = (bf16[64,2176]{1,0:T(8,128)(2,1)S(1)}, f32[64,2048]{1,0:T(8,128)S(1)}) custom-call(s32[1]{0:T(128)} %bitcast.7.place, bf16[128,1536]{1,0:T(8,128)(2,1)S(1)} %get-tuple-element.110.lhs, bf16[64,128]{1,0:T(8,128)(2,1)S(1)} %get-tuple-element.103.coded_ref, bf16[192,2048]{1,0:T(8,128)(2,1)S(1)} %copy-done.1, ...), custom_call_target="tpu_custom_call" | custom-call | tf_op jit(solution)/shard_map/pallas_call | solution.py:190
  133.0 11.9 %collective-permute-done.42.refs_6_ = bf16[192,2048]{1,0:T(8,128)(2,1)S(1)} collective-permute-done((bf16[192,2048]{1,0:T(8,128)(2,1)}, bf16[192,2048]{1,0:T(8,128)(2,1)S(1)}, u32[]{:S(2)}, u32[]{:S(2)}) %collective-permute-start.42) | collective-permute-done | bytes 786464 | tf_op jit(solution)/shard_map/ppermute | solution.py:401
  144.9 1.4 collective-permute-done.38
  146.3 1.4 collective-permute-start.49
  147.7 0.9 collective-permute-done.43.refs_7_
  148.6 2.9 %shard_map.145 = (bf16[64,2048]{1,0:T(8,128)(2,1)S(1)}, f32[64,2048]{1,0:T(8,128)S(1)}) custom-call(s32[1]{0:T(128)} %bitcast.7.place, bf16[128,1536]{1,0:T(8,128)(2,1)S(1)} %get-tuple-element.110.lhs, bf16[64,128]{1,0:T(8,128)(2,1)S(1)} %get-tuple-element.103.coded_ref, bf16[192,2048]{1,0:T(8,128)(2,1)S(1)} %copy-done.3, ...), custom_call_target="tpu_custom_call" | custom-call | tf_op jit(solution)/shard_map/pallas_call | solution.py:190
  152.3 14.0 %collective-permute-done.49.refs_6_ = bf16[1024,384]{1,0:T(8,128)(2,1)} collective-permute-done((bf16[1024,384]{1,0:T(8,128)(2,1)S(1)}, bf16[1024,384]{1,0:T(8,128)(2,1)}, u32[]{:S(2)}, u32[]{:S(2)}) %collective-permute-start.49) | collective-permute-done | bytes 786464 | tf_op jit(solution)/shard_map/ppermute | solution.py:401
  166.9 13.9 %collective-permute-done.45.got_ref = bf16[64,2048]{1,0:T(8,128)(2,1)S(1)} collective-permute-done((bf16[64,2048]{1,0:T(8,128)(2,1)S(1)}, bf16[64,2048]{1,0:T(8,128)(2,1)S(1)}, u32[]{:S(2)}, u32[]{:S(2)}) %collective-permute-start.45) | collective-permute-done | bytes 262176 | tf_op jit(solution)/shard_map/ppermute | solution.py:401
  180.8 4.1 %shard_map.146 = bf16[128,1536]{1,0:T(8,128)(2,1)S(1)} custom-call(s32[1]{0:T(128)} %bitcast.7.place, bf16[64,2048]{1,0:T(8,128)(2,1)S(1)} %multiply_convert_fusion.own_ref, bf16[64,2048]{1,0:T(8,128)(2,1)S(1)} %collective-permute-done.45.got_ref, bf16[1024,384]{1,0:T(8,128)(2,1)S(1)} %pad_maximum_fusion.refs_0_, ...), custom_call_target="tpu_custom_call" | custom-call | tf_op jit(solution)/shard_map/pallas_call | solution.py:272
  184.9 1.7 collective-permute-start.51
  186.7 5.2 %collective-permute-done.51 = bf16[2,32,1536]{2,1,0:T(8,128)(2,1)S(1)} collective-permute-done((bf16[2,32,1536]{2,1,0:T(8,128)(2,1)S(1)}, bf16[2,32,1536]{2,1,0:T(8,128)(2,1)S(1)}, u32[]{:S(2)}, u32[]{:S(2)}) %collective-permute-start.51) | collective-permute-done | bytes 196640 | tf_op jit(solution)/shard_map/ppermute | solution.py:406
  191.9 1.0 fusion.1
  193.0 6.8 %collective-permute-done.52 = bf16[32,1536]{1,0:T(8,128)(2,1)S(1)} collective-permute-done((bf16[32,1536]{1,0:T(8,128)(2,1)S(1)}, bf16[32,1536]{1,0:T(8,128)(2,1)S(1)}, u32[]{:S(2)}, u32[]{:S(2)}) %collective-permute-start.52) | collective-permute-done | bytes 98336 | tf_op jit(solution)/shard_map/ppermute | solution.py:401
  199.8 0.7 maximum_select_fusion
  (119 shorter events, 9.9 us)
Async XLA Ops:
  0.6 9.5 %copy-start.5 = (bf16[2048,192]{0,1:T(8,128)(2,1)S(1)}, bf16[2048,192]{0,1:T(8,128)(2,1)}, u32[]{:S(2)}) copy-start(bf16[2048,192]{0,1:T(8,128)(2,1)} %param.21) | copy-start | bytes 2359300
  0.6 25.8 %collective-permute-start.11 = (bf16[192,768]{1,0:T(8,128)(2,1)}, bf16[192,768]{1,0:T(8,128)(2,1)S(1)}, u32[]{:S(2)}, u32[]{:S(2)}) collective-permute-start(bf16[192,768]{1,0:T(8,128)(2,1)} %refs_4_.1), channel_id=1, source_target_pairs={{0,4},{2,6},{4,0},{6,2},{8,12},{10,14},{12,8},{14,10},{16,20},{18,... | collective-permute-start | bytes 884744 | tf_op jit(solution)/shard_map/ppermute | solution.py:401
  3.6 25.4 %collective-permute-start.10 = (bf16[192,768]{1,0:T(8,128)(2,1)}, bf16[192,768]{1,0:T(8,128)(2,1)}, u32[]{:S(2)}, u32[]{:S(2)}) collective-permute-start(bf16[192,768]{1,0:T(8,128)(2,1)} %refs_4_.1), channel_id=1, source_target_pairs={{0,2},{2,0},{4,6},{6,4},{8,10},{10,8},{12,14},{14,12},{16,18},{18,... | collective-permute-start | bytes 884744 | tf_op jit(solution)/shard_map/ppermute | solution.py:401
  5.5 6.9 %collective-permute-start = (bf16[32,768]{1,0:T(8,128)(2,1)S(1)}, bf16[32,768]{1,0:T(8,128)(2,1)S(1)}, u32[]{:S(2)}, u32[]{:S(2)}) collective-permute-start(bf16[32,768]{1,0:T(8,128)(2,1)S(1)} %get-tuple-element.66), channel_id=1, source_target_pairs={{0,24},{2,26},{4,28},{6,30},{8,0},{10,2},{12,4},{14,6},{16,8},{18,... | collective-permute-start | bytes 147464 | tf_op jit(solution)/shard_map/ppermute | solution.py:420
  9.2 6.0 %collective-permute-start.1 = (bf16[32,768]{1,0:T(8,128)(2,1)S(1)}, bf16[32,768]{1,0:T(8,128)(2,1)S(1)}, u32[]{:S(2)}, u32[]{:S(2)}) collective-permute-start(bf16[32,768]{1,0:T(8,128)(2,1)S(1)} %get-tuple-element.67), channel_id=1, source_target_pairs={{0,16},{2,18},{4,20},{6,22},{8,24},{10,26},{12,28},{14,30},{16,0},... | collective-permute-start | bytes 147464 | tf_op jit(solution)/shard_map/ppermute | solution.py:420
  9.2 6.6 %collective-permute-start.2 = (bf16[32,768]{1,0:T(8,128)(2,1)S(1)}, bf16[32,768]{1,0:T(8,128)(2,1)S(1)}, u32[]{:S(2)}, u32[]{:S(2)}) collective-permute-start(bf16[32,768]{1,0:T(8,128)(2,1)S(1)} %get-tuple-element.68), channel_id=1, source_target_pairs={{0,8},{2,10},{4,12},{6,14},{8,16},{10,18},{12,20},{14,22},{16,24},... | collective-permute-start | bytes 147464 | tf_op jit(solution)/shard_map/ppermute | solution.py:420
  12.3 12.4 %copy-start.1 = (bf16[192,2048]{1,0:T(8,128)(2,1)S(1)}, bf16[192,2048]{1,0:T(8,128)(2,1)}, u32[]{:S(2)}) copy-start(bf16[192,2048]{1,0:T(8,128)(2,1)} %refs_0_.4) | copy-start | bytes 2359300
  12.3 12.6 %copy-start.17 = (s32[63,1]{0,1:T(1,128)S(1)}, s32[63,1]{0,1:T(1,128)}, u32[]{:S(2)}) copy-start(s32[63,1]{0,1:T(1,128)} %slice_bitcast_fusion.2) | copy-start | bytes 760
  12.5 3.3 %copy-start.13 = (bf16[32,768]{1,0:T(8,128)(2,1)}, bf16[32,768]{1,0:T(8,128)(2,1)S(1)}, u32[]{:S(2)}) copy-start(bf16[32,768]{1,0:T(8,128)(2,1)S(1)} %collective-permute-done) | copy-start | bytes 147460
  12.5 12.8 %collective-permute-start.5 = (bf16[192,768]{1,0:T(8,128)(2,1)}, bf16[192,768]{1,0:T(8,128)(2,1)}, u32[]{:S(2)}, u32[]{:S(2)}) collective-permute-start(bf16[192,768]{1,0:T(8,128)(2,1)} %refs_0_.3), channel_id=1, source_target_pairs={{0,4},{2,6},{4,0},{6,2},{8,12},{10,14},{12,8},{14,10},{16,20},{18,... | collective-permute-start | bytes 884744 | tf_op jit(solution)/shard_map/ppermute | solution.py:401
  15.2 13.9 %collective-permute-start.14 = (bf16[192,768]{1,0:T(8,128)(2,1)}, bf16[192,768]{1,0:T(8,128)(2,1)}, u32[]{:S(2)}, u32[]{:S(2)}) collective-permute-start(bf16[192,768]{1,0:T(8,128)(2,1)} %refs_8_.2), channel_id=1, source_target_pairs={{0,4},{2,6},{4,0},{6,2},{8,12},{10,14},{12,8},{14,10},{16,20},{18,... | collective-permute-start | bytes 884744 | tf_op jit(solution)/shard_map/ppermute | solution.py:401
  16.4 19.2 %copy-start.2 = (bf16[192,2048]{1,0:T(8,128)(2,1)S(1)}, bf16[192,2048]{1,0:T(8,128)(2,1)}, u32[]{:S(2)}) copy-start(bf16[192,2048]{1,0:T(8,128)(2,1)} %refs_0_.5) | copy-start | bytes 2359300
  18.0 6.7 %collective-permute-start.3 = (bf16[32,1536]{1,0:T(8,128)(2,1)S(1)}, bf16[32,1536]{1,0:T(8,128)(2,1)S(1)}, u32[]{:S(2)}, u32[]{:S(2)}) collective-permute-start(bf16[32,1536]{1,0:T(8,128)(2,1)S(1)} %get-tuple-element.69), channel_id=1, source_target_pairs={{0,16},{2,18},{4,20},{6,22},{8,24},{10,26},{12,28},{14,30},{16,0},... | collective-permute-start | bytes 294920 | tf_op jit(solution)/shard_map/ppermute | solution.py:401
  24.7 19.2 %collective-permute-start.6 = (bf16[192,2048]{1,0:T(8,128)(2,1)S(1)}, bf16[192,2048]{1,0:T(8,128)(2,1)}, u32[]{:S(2)}, u32[]{:S(2)}) collective-permute-start(bf16[192,2048]{1,0:T(8,128)(2,1)S(1)} %copy-done.1), channel_id=1, source_target_pairs={{0,8},{2,10},{4,12},{6,14},{8,0},{10,2},{12,4},{14,6},{16,24},{18,... | collective-permute-start | bytes 2359304 | tf_op jit(solution)/shard_map/ppermute | solution.py:401
  25.3 8.8 %collective-permute-start.22 = (bf16[384,384]{1,0:T(8,128)(2,1)}, bf16[384,384]{1,0:T(8,128)(2,1)}, u32[]{:S(2)}, u32[]{:S(2)}) collective-permute-start(bf16[384,384]{1,0:T(8,128)(2,1)} %pad_maximum_fusion.1.refs_0_), channel_id=1, source_target_pairs={{0,4},{2,6},{4,0},{6,2},{8,12},{10,14},{12,8},{14,10},{16,20},{18,... | collective-permute-start | bytes 884744 | tf_op jit(solution)/shard_map/ppermute | solution.py:401
  26.4 3.2 %copy-start.6 = (bf16[192,768]{1,0:T(8,128)(2,1)}, bf16[192,768]{1,0:T(8,128)(2,1)S(1)}, u32[]{:S(2)}) copy-start(bf16[192,768]{1,0:T(8,128)(2,1)S(1)} %collective-permute-done.11.refs_6_) | copy-start | bytes 884740
  26.4 9.2 %collective-permute-start.13 = (bf16[192,768]{1,0:T(8,128)(2,1)}, bf16[192,768]{1,0:T(8,128)(2,1)S(1)}, u32[]{:S(2)}, u32[]{:S(2)}) collective-permute-start(bf16[192,768]{1,0:T(8,128)(2,1)} %refs_8_.2), channel_id=1, source_target_pairs={{0,2},{2,0},{4,6},{6,4},{8,10},{10,8},{12,14},{14,12},{16,18},{18,... | collective-permute-start | bytes 884744 | tf_op jit(solution)/shard_map/ppermute | solution.py:401
  29.1 9.1 %collective-permute-start.8 = (bf16[192,768]{1,0:T(8,128)(2,1)}, bf16[192,768]{1,0:T(8,128)(2,1)S(1)}, u32[]{:S(2)}, u32[]{:S(2)}) collective-permute-start(bf16[192,768]{1,0:T(8,128)(2,1)} %refs_0_.3), channel_id=1, source_target_pairs={{0,2},{2,0},{4,6},{6,4},{8,10},{10,8},{12,14},{14,12},{16,18},{18,... | collective-permute-start | bytes 884744 | tf_op jit(solution)/shard_map/ppermute | solution.py:401
  29.1 11.2 %collective-permute-start.9 = (bf16[192,768]{1,0:T(8,128)(2,1)}, bf16[192,768]{1,0:T(8,128)(2,1)S(1)}, u32[]{:S(2)}, u32[]{:S(2)}) collective-permute-start(bf16[192,768]{1,0:T(8,128)(2,1)} %collective-permute-done.5.refs_2_), channel_id=1, source_target_pairs={{0,2},{2,0},{4,6},{6,4},{8,10},{10,8},{12,14},{14,12},{16,18},{18,... | collective-permute-start | bytes 884744 | tf_op jit(solution)/shard_map/ppermute | solution.py:401
  34.1 5.7 %collective-permute-start.4 = (bf16[2,32,1536]{2,1,0:T(8,128)(2,1)S(1)}, bf16[2,32,1536]{2,1,0:T(8,128)(2,1)S(1)}, u32[]{:S(2)}, u32[]{:S(2)}) collective-permute-start(bf16[2,32,1536]{2,1,0:T(8,128)(2,1)S(1)} %pad_maximum_fusion.3.mine_ref), channel_id=1, source_target_pairs={{0,1},{1,0},{2,3},{3,2},{4,5},{5,4},{6,7},{7,6},{8,9},{9,8},{10,11... | collective-permute-start | bytes 589832 | tf_op jit(solution)/shard_map/ppermute | solution.py:406
  35.6 14.6 %copy-start.7 = (bf16[192,768]{1,0:T(8,128)(2,1)}, bf16[192,768]{1,0:T(8,128)(2,1)S(1)}, u32[]{:S(2)}) copy-start(bf16[192,768]{1,0:T(8,128)(2,1)S(1)} %collective-permute-done.13.refs_9_) | copy-start | bytes 884740
  35.6 29.6 %collective-permute-start.17 = (bf16[192,2048]{1,0:T(8,128)(2,1)S(1)}, bf16[192,2048]{1,0:T(8,128)(2,1)}, u32[]{:S(2)}, u32[]{:S(2)}) collective-permute-start(bf16[192,2048]{1,0:T(8,128)(2,1)S(1)} %copy-done.2), channel_id=1, source_target_pairs={{0,8},{2,10},{4,12},{6,14},{8,0},{10,2},{12,4},{14,6},{16,24},{18,... | collective-permute-start | bytes 2359304 | tf_op jit(solution)/shard_map/ppermute | solution.py:401
  38.2 5.8 %copy-start.8 = (bf16[192,768]{1,0:T(8,128)(2,1)}, bf16[192,768]{1,0:T(8,128)(2,1)S(1)}, u32[]{:S(2)}) copy-start(bf16[192,768]{1,0:T(8,128)(2,1)S(1)} %collective-permute-done.8.refs_1_) | copy-start | bytes 884740
  38.2 31.1 %collective-permute-start.23 = (bf16[192,2048]{1,0:T(8,128)(2,1)S(1)}, bf16[192,2048]{1,0:T(8,128)(2,1)}, u32[]{:S(2)}, u32[]{:S(2)}) collective-permute-start(bf16[192,2048]{1,0:T(8,128)(2,1)S(1)} %copy-done.1), channel_id=1, source_target_pairs={{0,4},{2,6},{4,0},{6,2},{8,12},{10,14},{12,8},{14,10},{16,20},{18,... | collective-permute-start | bytes 2359304 | tf_op jit(solution)/shard_map/ppermute | solution.py:401
  39.7 35.9 %collective-permute-start.24 = (bf16[192,2048]{1,0:T(8,128)(2,1)S(1)}, bf16[192,2048]{1,0:T(8,128)(2,1)}, u32[]{:S(2)}, u32[]{:S(2)}) collective-permute-start(bf16[192,2048]{1,0:T(8,128)(2,1)S(1)} %copy-done.2), channel_id=1, source_target_pairs={{0,4},{2,6},{4,0},{6,2},{8,12},{10,14},{12,8},{14,10},{16,20},{18,... | collective-permute-start | bytes 2359304 | tf_op jit(solution)/shard_map/ppermute | solution.py:401
  40.3 3.6 %copy-start.9 = (bf16[192,768]{1,0:T(8,128)(2,1)}, bf16[192,768]{1,0:T(8,128)(2,1)S(1)}, u32[]{:S(2)}) copy-start(bf16[192,768]{1,0:T(8,128)(2,1)S(1)} %collective-permute-done.9.refs_3_) | copy-start | bytes 884740
  40.3 7.4 %collective-permute-start.12 = (bf16[192,768]{1,0:T(8,128)(2,1)}, bf16[192,768]{1,0:T(8,128)(2,1)S(1)}, u32[]{:S(2)}, u32[]{:S(2)}) collective-permute-start(bf16[192,768]{1,0:T(8,128)(2,1)} %copy-done.6), channel_id=1, source_target_pairs={{0,2},{2,0},{4,6},{6,4},{8,10},{10,8},{12,14},{14,12},{16,18},{18,... | collective-permute-start | bytes 884744 | tf_op jit(solution)/shard_map/ppermute | solution.py:401
  43.9 6.3 %collective-permute-start.15 = (bf16[192,768]{1,0:T(8,128)(2,1)}, bf16[192,768]{1,0:T(8,128)(2,1)}, u32[]{:S(2)}, u32[]{:S(2)}) collective-permute-start(bf16[192,768]{1,0:T(8,128)(2,1)} %collective-permute-done.14.refs_10_), channel_id=1, source_target_pairs={{0,2},{2,0},{4,6},{6,4},{8,10},{10,8},{12,14},{14,12},{16,18},{18,... | collective-permute-start | bytes 884744 | tf_op jit(solution)/shard_map/ppermute | solution.py:401
  47.7 2.5 %copy-start.10 = (bf16[192,768]{1,0:T(8,128)(2,1)}, bf16[192,768]{1,0:T(8,128)(2,1)S(1)}, u32[]{:S(2)}) copy-start(bf16[192,768]{1,0:T(8,128)(2,1)S(1)} %collective-permute-done.12.refs_7_) | copy-start | bytes 884740
  47.7 8.4 %collective-permute-start.7 = (bf16[4,32,768]{2,1,0:T(8,128)(2,1)}, bf16[4,32,768]{2,1,0:T(8,128)(2,1)}, u32[]{:S(2)}, u32[]{:S(2)}) collective-permute-start(bf16[4,32,768]{2,1,0:T(8,128)(2,1)} %pad_maximum_fusion.2.mine_ref), channel_id=1, source_target_pairs={{0,1},{1,0},{2,3},{3,2},{4,5},{5,4},{6,7},{7,6},{8,9},{9,8},{10,11... | collective-permute-start | bytes 589832 | tf_op jit(solution)/shard_map/ppermute | solution.py:406
  50.2 42.1 %collective-permute-start.25 = (bf16[1024,384]{1,0:T(8,128)(2,1)S(1)}, bf16[1024,384]{1,0:T(8,128)(2,1)S(1)}, u32[]{:S(2)}, u32[]{:S(2)}) collective-permute-start(bf16[1024,384]{1,0:T(8,128)(2,1)S(1)} %pad_maximum_fusion.refs_0_), channel_id=1, source_target_pairs={{0,4},{2,6},{4,0},{6,2},{8,12},{10,14},{12,8},{14,10},{16,20},{18,... | collective-permute-start | bytes 2359304 | tf_op jit(solution)/shard_map/ppermute | solution.py:401
  56.1 9.2 %collective-permute-start.16 = (bf16[384,384]{1,0:T(8,128)(2,1)}, bf16[384,384]{1,0:T(8,128)(2,1)}, u32[]{:S(2)}, u32[]{:S(2)}) collective-permute-start(bf16[384,384]{1,0:T(8,128)(2,1)} %pad_maximum_fusion.1.refs_0_), channel_id=1, source_target_pairs={{0,8},{2,10},{4,12},{6,14},{8,0},{10,2},{12,4},{14,6},{16,24},{18,... | collective-permute-start | bytes 884744 | tf_op jit(solution)/shard_map/ppermute | solution.py:401
  65.2 30.7 %collective-permute-start.18 = (bf16[64,2432]{1,0:T(8,128)(2,1)}, bf16[64,2432]{1,0:T(8,128)(2,1)}, u32[]{:S(2)}, u32[]{:S(2)}) collective-permute-start(bf16[64,2432]{1,0:T(8,128)(2,1)} %get-tuple-element.82), channel_id=1, source_target_pairs={{0,8},{2,10},{4,12},{6,14},{8,16},{10,18},{12,20},{14,22},{16,24},... | collective-permute-start | bytes 933896 | tf_op jit(solution)/shard_map/ppermute | solution.py:420
  65.7 30.3 %collective-permute-start.19 = (bf16[64,2432]{1,0:T(8,128)(2,1)}, bf16[64,2432]{1,0:T(8,128)(2,1)}, u32[]{:S(2)}, u32[]{:S(2)}) collective-permute-start(bf16[64,2432]{1,0:T(8,128)(2,1)} %get-tuple-element.83), channel_id=1, source_target_pairs={{0,16},{2,18},{4,20},{6,22},{8,24},{10,26},{12,28},{14,30},{16,0},... | collective-permute-start | bytes 933896 | tf_op jit(solution)/shard_map/ppermute | solution.py:420
  69.3 26.7 %collective-permute-start.20 = (bf16[64,2432]{1,0:T(8,128)(2,1)}, bf16[64,2432]{1,0:T(8,128)(2,1)}, u32[]{:S(2)}, u32[]{:S(2)}) collective-permute-start(bf16[64,2432]{1,0:T(8,128)(2,1)} %get-tuple-element.84), channel_id=1, source_target_pairs={{0,24},{2,26},{4,28},{6,30},{8,0},{10,2},{12,4},{14,6},{16,8},{18,... | collective-permute-start | bytes 933896 | tf_op jit(solution)/shard_map/ppermute | solution.py:420
  75.6 20.4 %collective-permute-start.21 = (bf16[384,384]{1,0:T(8,128)(2,1)}, bf16[384,384]{1,0:T(8,128)(2,1)}, u32[]{:S(2)}, u32[]{:S(2)}) collective-permute-start(bf16[384,384]{1,0:T(8,128)(2,1)} %collective-permute-done.16.refs_4_), channel_id=1, source_target_pairs={{0,4},{2,6},{4,0},{6,2},{8,12},{10,14},{12,8},{14,10},{16,20},{18,... | collective-permute-start | bytes 884744 | tf_op jit(solution)/shard_map/ppermute | solution.py:401
  92.3 14.6 %collective-permute-start.28 = (bf16[384,384]{1,0:T(8,128)(2,1)}, bf16[384,384]{1,0:T(8,128)(2,1)}, u32[]{:S(2)}, u32[]{:S(2)}) collective-permute-start(bf16[384,384]{1,0:T(8,128)(2,1)} %collective-permute-done.22.refs_2_), channel_id=1, source_target_pairs={{0,2},{2,0},{4,6},{6,4},{8,10},{10,8},{12,14},{14,12},{16,18},{18,... | collective-permute-start | bytes 884744 | tf_op jit(solution)/shard_map/ppermute | solution.py:401
  99.7 6.6 %collective-permute-start.26 = (bf16[64,768]{1,0:T(8,128)(2,1)}, bf16[64,768]{1,0:T(8,128)(2,1)S(1)}, u32[]{:S(2)}, u32[]{:S(2)}) collective-permute-start(bf16[64,768]{1,0:T(8,128)(2,1)} %get-tuple-element.94.own_ref), channel_id=1, source_target_pairs={{0,16},{2,18},{4,20},{6,22},{8,24},{10,26},{12,28},{14,30},{16,0},... | collective-permute-start | bytes 294920 | tf_op jit(solution)/shard_map/ppermute | solution.py:401
  100.9 22.1 %collective-permute-start.33 = (bf16[192,2048]{1,0:T(8,128)(2,1)}, bf16[192,2048]{1,0:T(8,128)(2,1)}, u32[]{:S(2)}, u32[]{:S(2)}) collective-permute-start(bf16[192,2048]{1,0:T(8,128)(2,1)} %collective-permute-done.6.refs_4_), channel_id=1, source_target_pairs={{0,4},{2,6},{4,0},{6,2},{8,12},{10,14},{12,8},{14,10},{16,20},{18,... | collective-permute-start | bytes 2359304 | tf_op jit(solution)/shard_map/ppermute | solution.py:401
  101.4 5.6 %collective-permute-start.29 = (bf16[384,384]{1,0:T(8,128)(2,1)}, bf16[384,384]{1,0:T(8,128)(2,1)}, u32[]{:S(2)}, u32[]{:S(2)}) collective-permute-start(bf16[384,384]{1,0:T(8,128)(2,1)} %collective-permute-done.16.refs_4_), channel_id=1, source_target_pairs={{0,2},{2,0},{4,6},{6,4},{8,10},{10,8},{12,14},{14,12},{16,18},{18,... | collective-permute-start | bytes 884744 | tf_op jit(solution)/shard_map/ppermute | solution.py:401
  101.4 5.5 %collective-permute-start.27 = (bf16[384,384]{1,0:T(8,128)(2,1)}, bf16[384,384]{1,0:T(8,128)(2,1)}, u32[]{:S(2)}, u32[]{:S(2)}) collective-permute-start(bf16[384,384]{1,0:T(8,128)(2,1)} %pad_maximum_fusion.1.refs_0_), channel_id=1, source_target_pairs={{0,2},{2,0},{4,6},{6,4},{8,10},{10,8},{12,14},{14,12},{16,18},{18,... | collective-permute-start | bytes 884744 | tf_op jit(solution)/shard_map/ppermute | solution.py:401
  106.3 1.9 collective-permute-start.30
  107.0 19.3 %collective-permute-start.32 = (bf16[1024,384]{1,0:T(8,128)(2,1)S(1)}, bf16[1024,384]{1,0:T(8,128)(2,1)S(1)}, u32[]{:S(2)}, u32[]{:S(2)}) collective-permute-start(bf16[1024,384]{1,0:T(8,128)(2,1)S(1)} %pad_maximum_fusion.refs_0_), channel_id=1, source_target_pairs={{0,8},{2,10},{4,12},{6,14},{8,0},{10,2},{12,4},{14,6},{16,24},{18,... | collective-permute-start | bytes 2359304 | tf_op jit(solution)/shard_map/ppermute | solution.py:401
  111.6 11.4 %collective-permute-start.31 = (bf16[128,1536]{1,0:T(8,128)(2,1)}, bf16[128,1536]{1,0:T(8,128)(2,1)S(1)}, u32[]{:S(2)}, u32[]{:S(2)}) collective-permute-start(bf16[128,1536]{1,0:T(8,128)(2,1)} %shard_map.142.a_ref), channel_id=1, source_target_pairs={{0,1},{1,0},{2,3},{3,2},{4,5},{5,4},{6,7},{7,6},{8,9},{9,8},{10,11... | collective-permute-start | bytes 1179656 | tf_op jit(solution)/shard_map/ppermute | solution.py:406
  113.1 15.9 %collective-permute-start.36 = (bf16[192,2048]{1,0:T(8,128)(2,1)}, bf16[192,2048]{1,0:T(8,128)(2,1)S(1)}, u32[]{:S(2)}, u32[]{:S(2)}) collective-permute-start(bf16[192,2048]{1,0:T(8,128)(2,1)} %collective-permute-done.6.refs_4_), channel_id=1, source_target_pairs={{0,2},{2,0},{4,6},{6,4},{8,10},{10,8},{12,14},{14,12},{16,18},{18,... | collective-permute-start | bytes 2359304 | tf_op jit(solution)/shard_map/ppermute | solution.py:401
  113.1 15.9 %collective-permute-start.35 = (bf16[192,2048]{1,0:T(8,128)(2,1)}, bf16[192,2048]{1,0:T(8,128)(2,1)S(1)}, u32[]{:S(2)}, u32[]{:S(2)}) collective-permute-start(bf16[192,2048]{1,0:T(8,128)(2,1)} %collective-permute-done.23.refs_2_), channel_id=1, source_target_pairs={{0,2},{2,0},{4,6},{6,4},{8,10},{10,8},{12,14},{14,12},{16,18},{18,... | collective-permute-start | bytes 2359304 | tf_op jit(solution)/shard_map/ppermute | solution.py:401
  122.9 6.0 %collective-permute-start.34 = (bf16[192,2048]{1,0:T(8,128)(2,1)S(1)}, bf16[192,2048]{1,0:T(8,128)(2,1)S(1)}, u32[]{:S(2)}, u32[]{:S(2)}) collective-permute-start(bf16[192,2048]{1,0:T(8,128)(2,1)S(1)} %copy-done.1), channel_id=1, source_target_pairs={{0,2},{2,0},{4,6},{6,4},{8,10},{10,8},{12,14},{14,12},{16,18},{18,... | collective-permute-start | bytes 2359304 | tf_op jit(solution)/shard_map/ppermute | solution.py:401
  123.0 6.0 %collective-permute-start.37 = (bf16[192,2048]{1,0:T(8,128)(2,1)}, bf16[192,2048]{1,0:T(8,128)(2,1)S(1)}, u32[]{:S(2)}, u32[]{:S(2)}) collective-permute-start(bf16[192,2048]{1,0:T(8,128)(2,1)} %collective-permute-done.33.refs_6_), channel_id=1, source_target_pairs={{0,2},{2,0},{4,6},{6,4},{8,10},{10,8},{12,14},{14,12},{16,18},{18,... | collective-permute-start | bytes 2359304 | tf_op jit(solution)/shard_map/ppermute | solution.py:401
  126.3 18.7 %collective-permute-start.42 = (bf16[192,2048]{1,0:T(8,128)(2,1)}, bf16[192,2048]{1,0:T(8,128)(2,1)S(1)}, u32[]{:S(2)}, u32[]{:S(2)}) collective-permute-start(bf16[192,2048]{1,0:T(8,128)(2,1)} %collective-permute-done.17.refs_4_), channel_id=1, source_target_pairs={{0,4},{2,6},{4,0},{6,2},{8,12},{10,14},{12,8},{14,10},{16,20},{18,... | collective-permute-start | bytes 2359304 | tf_op jit(solution)/shard_map/ppermute | solution.py:401
  129.0 4.0 %copy-start.3 = (bf16[192,2048]{1,0:T(8,128)(2,1)S(1)}, bf16[192,2048]{1,0:T(8,128)(2,1)}, u32[]{:S(2)}) copy-start(bf16[192,2048]{1,0:T(8,128)(2,1)} %refs_0_.5) | copy-start | bytes 2359300
  132.1 14.2 %collective-permute-start.38 = (bf16[64,2176]{1,0:T(8,128)(2,1)S(1)}, bf16[64,2176]{1,0:T(8,128)(2,1)S(1)}, u32[]{:S(2)}, u32[]{:S(2)}) collective-permute-start(bf16[64,2176]{1,0:T(8,128)(2,1)S(1)} %get-tuple-element.108), channel_id=1, source_target_pairs={{0,16},{2,18},{4,20},{6,22},{8,24},{10,26},{12,28},{14,30},{16,0},... | collective-permute-start | bytes 835592 | tf_op jit(solution)/shard_map/ppermute | solution.py:401
  132.5 15.2 %collective-permute-start.41 = (bf16[192,2048]{1,0:T(8,128)(2,1)}, bf16[192,2048]{1,0:T(8,128)(2,1)S(1)}, u32[]{:S(2)}, u32[]{:S(2)}) collective-permute-start(bf16[192,2048]{1,0:T(8,128)(2,1)} %collective-permute-done.17.refs_4_), channel_id=1, source_target_pairs={{0,2},{2,0},{4,6},{6,4},{8,10},{10,8},{12,14},{14,12},{16,18},{18,... | collective-permute-start | bytes 2359304 | tf_op jit(solution)/shard_map/ppermute | solution.py:401
  132.5 15.2 %collective-permute-start.40 = (bf16[192,2048]{1,0:T(8,128)(2,1)}, bf16[192,2048]{1,0:T(8,128)(2,1)S(1)}, u32[]{:S(2)}, u32[]{:S(2)}) collective-permute-start(bf16[192,2048]{1,0:T(8,128)(2,1)} %collective-permute-done.24.refs_2_), channel_id=1, source_target_pairs={{0,2},{2,0},{4,6},{6,4},{8,10},{10,8},{12,14},{14,12},{16,18},{18,... | collective-permute-start | bytes 2359304 | tf_op jit(solution)/shard_map/ppermute | solution.py:401
  133.0 14.7 %collective-permute-start.39 = (bf16[192,2048]{1,0:T(8,128)(2,1)S(1)}, bf16[192,2048]{1,0:T(8,128)(2,1)S(1)}, u32[]{:S(2)}, u32[]{:S(2)}) collective-permute-start(bf16[192,2048]{1,0:T(8,128)(2,1)S(1)} %copy-done.3), channel_id=1, source_target_pairs={{0,2},{2,0},{4,6},{6,4},{8,10},{10,8},{12,14},{14,12},{16,18},{18,... | collective-permute-start | bytes 2359304 | tf_op jit(solution)/shard_map/ppermute | solution.py:401
  146.3 2.3 %collective-permute-start.43 = (bf16[192,2048]{1,0:T(8,128)(2,1)S(1)}, bf16[192,2048]{1,0:T(8,128)(2,1)S(1)}, u32[]{:S(2)}, u32[]{:S(2)}) collective-permute-start(bf16[192,2048]{1,0:T(8,128)(2,1)S(1)} %collective-permute-done.42.refs_6_), channel_id=1, source_target_pairs={{0,2},{2,0},{4,6},{6,4},{8,10},{10,8},{12,14},{14,12},{16,18},{18,... | collective-permute-start | bytes 2359304 | tf_op jit(solution)/shard_map/ppermute | solution.py:401
  146.3 20.1 %collective-permute-start.49 = (bf16[1024,384]{1,0:T(8,128)(2,1)S(1)}, bf16[1024,384]{1,0:T(8,128)(2,1)}, u32[]{:S(2)}, u32[]{:S(2)}) collective-permute-start(bf16[1024,384]{1,0:T(8,128)(2,1)S(1)} %collective-permute-done.32.refs_4_), channel_id=1, source_target_pairs={{0,4},{2,6},{4,0},{6,2},{8,12},{10,14},{12,8},{14,10},{16,20},{18,... | collective-permute-start | bytes 2359304 | tf_op jit(solution)/shard_map/ppermute | solution.py:401
  151.5 14.9 %collective-permute-start.44 = (bf16[64,2048]{1,0:T(8,128)(2,1)S(1)}, bf16[64,2048]{1,0:T(8,128)(2,1)S(1)}, u32[]{:S(2)}, u32[]{:S(2)}) collective-permute-start(bf16[64,2048]{1,0:T(8,128)(2,1)S(1)} %get-tuple-element.117), channel_id=1, source_target_pairs={{0,16},{2,18},{4,20},{6,22},{8,24},{10,26},{12,28},{14,30},{16,0},... | collective-permute-start | bytes 786440 | tf_op jit(solution)/shard_map/ppermute | solution.py:401
  151.6 29.2 %collective-permute-start.48 = (bf16[1024,384]{1,0:T(8,128)(2,1)S(1)}, bf16[1024,384]{1,0:T(8,128)(2,1)}, u32[]{:S(2)}, u32[]{:S(2)}) collective-permute-start(bf16[1024,384]{1,0:T(8,128)(2,1)S(1)} %collective-permute-done.32.refs_4_), channel_id=1, source_target_pairs={{0,2},{2,0},{4,6},{6,4},{8,10},{10,8},{12,14},{14,12},{16,18},{18,... | collective-permute-start | bytes 2359304 | tf_op jit(solution)/shard_map/ppermute | solution.py:401
  151.8 29.0 %collective-permute-start.47 = (bf16[1024,384]{1,0:T(8,128)(2,1)S(1)}, bf16[1024,384]{1,0:T(8,128)(2,1)}, u32[]{:S(2)}, u32[]{:S(2)}) collective-permute-start(bf16[1024,384]{1,0:T(8,128)(2,1)S(1)} %collective-permute-done.25.refs_2_), channel_id=1, source_target_pairs={{0,2},{2,0},{4,6},{6,4},{8,10},{10,8},{12,14},{14,12},{16,18},{18,... | collective-permute-start | bytes 2359304 | tf_op jit(solution)/shard_map/ppermute | solution.py:401
  152.2 28.6 %collective-permute-start.46 = (bf16[1024,384]{1,0:T(8,128)(2,1)S(1)}, bf16[1024,384]{1,0:T(8,128)(2,1)}, u32[]{:S(2)}, u32[]{:S(2)}) collective-permute-start(bf16[1024,384]{1,0:T(8,128)(2,1)S(1)} %pad_maximum_fusion.refs_0_), channel_id=1, source_target_pairs={{0,2},{2,0},{4,6},{6,4},{8,10},{10,8},{12,14},{14,12},{16,18},{18,... | collective-permute-start | bytes 2359304 | tf_op jit(solution)/shard_map/ppermute | solution.py:401
  166.4 14.5 %collective-permute-start.50 = (bf16[1024,384]{1,0:T(8,128)(2,1)}, bf16[1024,384]{1,0:T(8,128)(2,1)}, u32[]{:S(2)}, u32[]{:S(2)}) collective-permute-start(bf16[1024,384]{1,0:T(8,128)(2,1)} %collective-permute-done.49.refs_6_), channel_id=1, source_target_pairs={{0,2},{2,0},{4,6},{6,4},{8,10},{10,8},{12,14},{14,12},{16,18},{18,... | collective-permute-start | bytes 2359304 | tf_op jit(solution)/shard_map/ppermute | solution.py:401
  166.8 14.0 %collective-permute-start.45 = (bf16[64,2048]{1,0:T(8,128)(2,1)S(1)}, bf16[64,2048]{1,0:T(8,128)(2,1)S(1)}, u32[]{:S(2)}, u32[]{:S(2)}) collective-permute-start(bf16[64,2048]{1,0:T(8,128)(2,1)S(1)} %multiply_convert_fusion.own_ref), channel_id=1, source_target_pairs={{0,16},{2,18},{4,20},{6,22},{8,24},{10,26},{12,28},{14,30},{16,0},... | collective-permute-start | bytes 786440 | tf_op jit(solution)/shard_map/ppermute | solution.py:401
  184.9 6.9 %collective-permute-start.51 = (bf16[2,32,1536]{2,1,0:T(8,128)(2,1)S(1)}, bf16[2,32,1536]{2,1,0:T(8,128)(2,1)S(1)}, u32[]{:S(2)}, u32[]{:S(2)}) collective-permute-start(bf16[2,32,1536]{2,1,0:T(8,128)(2,1)S(1)} %dynamic-slice_bitcast_fusion), channel_id=1, source_target_pairs={{0,1},{1,0},{2,3},{3,2},{4,5},{5,4},{6,7},{7,6},{8,9},{9,8},{10,11... | collective-permute-start | bytes 589832 | tf_op jit(solution)/shard_map/ppermute | solution.py:406
  192.9 6.9 %collective-permute-start.52 = (bf16[32,1536]{1,0:T(8,128)(2,1)S(1)}, bf16[32,1536]{1,0:T(8,128)(2,1)S(1)}, u32[]{:S(2)}, u32[]{:S(2)}) collective-permute-start(bf16[32,1536]{1,0:T(8,128)(2,1)S(1)} %get-tuple-element.130), channel_id=1, source_target_pairs={{0,16},{2,18},{4,20},{6,22},{8,24},{10,26},{12,28},{14,30},{16,0},... | collective-permute-start | bytes 294920 | tf_op jit(solution)/shard_map/ppermute | solution.py:401
  (7 other events, 5.4 us)
